TPU v7x, 512 devices: a whole 4x8x8 slice. The times are simulated.
512 devices in a mesh: img: 128 (over y, z, core), view: 4 (over x).
Axes of the slice: x: 4, y: 8, z: 8, core: 2. Of those that a mesh axis runs over, the one named last changes fastest.
Arguments:
- gauss_params: float32 [59, 1048576], P(None, 'img'), may hold values from -6 to 6, as said below
- camera: float32 [4, 6], P('view'), may hold values from -0.3 to 6, as said below
- background: float32 [3], replicated, may hold values from 0 to 1
- tile_lists: int32 [4, 512, 256], P('view', 'img'), may hold values from 0 to 1048575, as said below
- tile_lengths: int32 [4, 512], P('view', 'img'), may hold values from 1 to 256, 78643 in all within a row
- pixel_cotangent: float32 [4, 3, 512, 256], P('view', None, 'img'), may hold values from -24 to 24
Outputs:
- gauss_grads: float32 [59, 1048576], P(None, 'img')
Inputs may be any that keep to these rules, and one draw needn't show every extreme that they name: `tile_lists`: entry g names Gaussian g, owned by index g // 8192 of img at column g % 8192; slots are composited in list order. Within the 4 tiles of one view on one index of img, at most 16 slots name Gaussians of one owner, and exactly 16 for some owner; a Gaussian may stand in several slots. `tile_lengths`: slots at or beyond a tile's length are empty. `gauss_params`: rows 0 to 2 lie in [-6, 6]; rows 3 to 5 in [-3, -0.5]; row 6 in [0.5, 1.5], rows 7 to 9 in [-1.5, 1.5]; row 10 in [-5, -2]; rows 11 to 58 in [-1, 1]. `camera`: columns 0 to 2 lie in [-0.15, 0.15], columns 3 and 4 in [-0.3, 0.3], column 5 in [4, 6].
All inputs are finite; a program needn't handle non-finite values. No bound on the sum of `tile_lengths` on one device may be relied on, other than what follows from the above.
Results may differ from a plain program's by a relative error of at most 0.0003.
Values sent between devices are 32-bit elements; how exact they have to be, the bound alone decides.
No kernel may reach another device: no remote copies, remote signals or barrier semaphores. Data moves between devices by JAX's collectives and lax.ppermute only.
A program may use at most 128 MiB of HBM per device.

v0:
```python
import jax
import jax.numpy as jnp
from jax import lax
from jax.sharding import PartitionSpec as P

SIDE = 16
TX = 16


FOCAL = 2.0
DILATION = 0.0001
SH_ZERO = 0.28209479177387814
SH_ONE = 0.4886025119029199
SH_TWO = (
    1.0925484305920792,
    -1.0925484305920792,
    0.31539156525252005,
    -1.0925484305920792,
    0.5462742152960396,
)
SH_THREE = (
    -0.5900435899266435,
    2.890611442640554,
    -0.4570457994644658,
    0.3731763325901154,
    -0.4570457994644658,
    1.445305721320277,
    -0.5900435899266435,
)


def rotation(angles):
    cos_x, sin_x = (jnp.cos(angles[0]), jnp.sin(angles[0]))
    cos_y, sin_y = (jnp.cos(angles[1]), jnp.sin(angles[1]))
    cos_z, sin_z = (jnp.cos(angles[2]), jnp.sin(angles[2]))
    unity = jnp.ones_like(cos_x)
    zeros = jnp.zeros_like(cos_x)
    about_x = jnp.stack(
        [
            jnp.stack([unity, zeros, zeros]),
            jnp.stack([zeros, cos_x, -sin_x]),
            jnp.stack([zeros, sin_x, cos_x]),
        ]
    )
    about_y = jnp.stack(
        [
            jnp.stack([cos_y, zeros, sin_y]),
            jnp.stack([zeros, unity, zeros]),
            jnp.stack([-sin_y, zeros, cos_y]),
        ]
    )
    about_z = jnp.stack(
        [
            jnp.stack([cos_z, -sin_z, zeros]),
            jnp.stack([sin_z, cos_z, zeros]),
            jnp.stack([zeros, zeros, unity]),
        ]
    )
    inner_pair = jnp.dot(about_y, about_x, precision=lax.Precision.HIGHEST)
    return jnp.dot(about_z, inner_pair, precision=lax.Precision.HIGHEST)


def harmonics(direction):
    along_x, along_y, along_z = (direction[0], direction[1], direction[2])
    square_x, square_y, square_z = (along_x * along_x, along_y * along_y, along_z * along_z)
    return [
        SH_ZERO * jnp.ones_like(along_x),
        -SH_ONE * along_y,
        SH_ONE * along_z,
        -SH_ONE * along_x,
        SH_TWO[0] * along_x * along_y,
        SH_TWO[1] * along_y * along_z,
        SH_TWO[2] * (2.0 * square_z - square_x - square_y),
        SH_TWO[3] * along_x * along_z,
        SH_TWO[4] * (square_x - square_y),
        SH_THREE[0] * along_y * (3.0 * square_x - square_y),
        SH_THREE[1] * along_x * along_y * along_z,
        SH_THREE[2] * along_y * (4.0 * square_z - square_x - square_y),
        SH_THREE[3] * along_z * (2.0 * square_z - 3.0 * square_x - 3.0 * square_y),
        SH_THREE[4] * along_x * (4.0 * square_z - square_x - square_y),
        SH_THREE[5] * along_z * (square_x - square_y),
        SH_THREE[6] * along_x * (square_x - 3.0 * square_y),
    ]


def project(params, camera):
    rotate = rotation(camera[0:3])
    offset = camera[3:6]
    centers = params[0:3]
    viewed = jnp.dot(rotate, centers, precision=lax.Precision.HIGHEST) + offset[:, None]
    depth_inv = 1.0 / viewed[2]
    screen_x = FOCAL * viewed[0] * depth_inv
    screen_y = FOCAL * viewed[1] * depth_inv
    scales = jnp.exp(params[3:6])
    quaternion = params[6:10]
    quaternion = quaternion * lax.rsqrt(jnp.sum(quaternion * quaternion, axis=0, keepdims=True))
    real_part, imag_i, imag_j, imag_k = (quaternion[0], quaternion[1], quaternion[2], quaternion[3])
    local_rot = [
        [
            1.0 - 2.0 * (imag_j * imag_j + imag_k * imag_k),
            2.0 * (imag_i * imag_j - real_part * imag_k),
            2.0 * (imag_i * imag_k + real_part * imag_j),
        ],
        [
            2.0 * (imag_i * imag_j + real_part * imag_k),
            1.0 - 2.0 * (imag_i * imag_i + imag_k * imag_k),
            2.0 * (imag_j * imag_k - real_part * imag_i),
        ],
        [
            2.0 * (imag_i * imag_k - real_part * imag_j),
            2.0 * (imag_j * imag_k + real_part * imag_i),
            1.0 - 2.0 * (imag_i * imag_i + imag_j * imag_j),
        ],
    ]
    scaled = [
        [local_rot[row_index][col_index] * scales[col_index] for col_index in range(3)]
        for row_index in range(3)
    ]
    jacobian = [
        [FOCAL * depth_inv, 0.0, -FOCAL * viewed[0] * depth_inv * depth_inv],
        [0.0, FOCAL * depth_inv, -FOCAL * viewed[1] * depth_inv * depth_inv],
    ]
    to_camera = [
        [
            sum(
                (
                    jacobian[row_index][mid_index] * rotate[mid_index, col_index]
                    for mid_index in range(3)
                )
            )
            for col_index in range(3)
        ]
        for row_index in range(2)
    ]
    screen_map = [
        [
            sum(
                (
                    to_camera[row_index][mid_index] * scaled[mid_index][col_index]
                    for mid_index in range(3)
                )
            )
            for col_index in range(3)
        ]
        for row_index in range(2)
    ]
    cov_a = (
        sum((screen_map[0][col_index] * screen_map[0][col_index] for col_index in range(3)))
        + DILATION
    )
    cov_b = sum((screen_map[0][col_index] * screen_map[1][col_index] for col_index in range(3)))
    cov_c = (
        sum((screen_map[1][col_index] * screen_map[1][col_index] for col_index in range(3)))
        + DILATION
    )
    determinant = cov_a * cov_c - cov_b * cov_b
    opacity = jax.nn.sigmoid(params[10])
    center = -jnp.dot(rotate.T, offset, precision=lax.Precision.HIGHEST)
    toward = centers - center[:, None]
    toward = toward * lax.rsqrt(jnp.sum(toward * toward, axis=0, keepdims=True))
    sh_basis = jnp.stack(harmonics(toward))
    coeffs = params[11:59].reshape(16, 3, -1)
    colors = 0.5 + jnp.sum(sh_basis[:, None, :] * coeffs, axis=0)
    screen = jnp.stack(
        [
            screen_x,
            screen_y,
            cov_c / determinant,
            -cov_b / determinant,
            cov_a / determinant,
            opacity,
        ]
    )
    return jnp.concatenate([screen, colors], axis=0)


def render_tile(feature, live_mask, pixel_x, pixel_y, background):
    delta_x = pixel_x[:, None] - feature[0][None, :]
    delta_y = pixel_y[:, None] - feature[1][None, :]
    quadric = (
        feature[2] * delta_x * delta_x
        + 2.0 * feature[3] * delta_x * delta_y
        + feature[4] * delta_y * delta_y
    )
    coverage = (feature[5] * live_mask)[None, :] * jnp.exp(-0.5 * quadric)
    log_pass = jnp.log1p(-coverage)
    positions = jnp.arange(live_mask.shape[0])
    earlier = (positions[:, None] < positions[None, :]).astype(jnp.float32)
    prefix = jnp.dot(log_pass, earlier, precision=lax.Precision.HIGHEST)
    weights = coverage * jnp.exp(prefix)
    shaded = lax.dot_general(
        feature[6:9], weights, (((1,), (1,)), ((), ())), precision=lax.Precision.HIGHEST
    )
    remain = jnp.exp(jnp.sum(log_pass, axis=1))
    return shaded + background[:, None] * remain[None, :]


def tile_grads(feature, live_mask, pixel_x, pixel_y, background, cotangent):
    unused, pullback = jax.vjp(
        lambda values: render_tile(values, live_mask, pixel_x, pixel_y, background), feature
    )
    return pullback(cotangent)[0]


def grads_for_tiles(features, live_mask, pixel_x, pixel_y, background, cotangent):
    pair_count = features.shape[0] // 2

    def one_group(blocks):
        return jax.vmap(tile_grads, in_axes=(0, 0, 0, 0, None, 0))(
            blocks[0], blocks[1], blocks[2], blocks[3], background, blocks[4]
        )

    grouped = tuple(
        (
            member.reshape((pair_count, 2) + member.shape[1:])
            for member in (features, live_mask, pixel_x, pixel_y, cotangent)
        )
    )
    stacked = lax.map(one_group, grouped)
    return stacked.reshape(features.shape)


def pixel_grid(first_tile, tile_count, tiles_total):
    tile_ids = first_tile + jnp.arange(tile_count)
    tile_row = tile_ids // TX
    tile_col = tile_ids % TX
    height = tiles_total // TX
    within = jnp.arange(SIDE * SIDE)
    local_row = within // SIDE
    local_col = within % SIDE
    pixel_x = ((tile_col[:, None] * SIDE + local_col[None, :]).astype(jnp.float32) + 0.5) / (
        TX * SIDE
    ) * 2.0 - 1.0
    pixel_y = ((tile_row[:, None] * SIDE + local_row[None, :]).astype(jnp.float32) + 0.5) / (
        height * SIDE
    ) * 2.0 - 1.0
    return (pixel_x, pixel_y)


def per_device(gauss_params, camera, background, tile_lists, tile_lengths, pixel_cotangent):
    owners_total = lax.axis_size("img")
    tiles_here = tile_lists.shape[1]
    slot_count = tile_lists.shape[2]
    gauss_here = gauss_params.shape[1]
    rows_here = tiles_here * slot_count
    capacity = max(2, 2 * rows_here // owners_total)
    wanted_ids = tile_lists.reshape(-1)
    owner_of = wanted_ids // gauss_here
    column_of = wanted_ids % gauss_here
    ranking = jnp.argsort(owner_of, stable=True)
    sorted_owner = owner_of[ranking]
    counts = jnp.sum(
        (owner_of[:, None] == jnp.arange(owners_total, dtype=jnp.int32)[None, :]).astype(jnp.int32),
        axis=0,
    )
    starts = jnp.cumsum(counts) - counts
    rank_sorted = jnp.arange(rows_here, dtype=jnp.int32) - starts[sorted_owner]
    position = (
        jnp.zeros((rows_here,), jnp.int32).at[ranking].set(sorted_owner * capacity + rank_sorted)
    )
    requests = jnp.zeros((owners_total * capacity,), jnp.int32).at[position].set(column_of)
    requested = lax.all_to_all(requests, "img", split_axis=0, concat_axis=0, tiled=True)
    view_camera = camera[0]
    live_mask = (jnp.arange(slot_count)[None, :] < tile_lengths[0][:, None]).astype(jnp.float32)
    pixel_x, pixel_y = pixel_grid(
        lax.axis_index("img") * tiles_here, tiles_here, tiles_here * owners_total
    )
    cotangent = jnp.transpose(pixel_cotangent[0], (1, 0, 2))
    arrived = lax.all_to_all(
        gauss_params[:, requested], "img", split_axis=1, concat_axis=1, tiled=True
    )
    slot_feats, slot_back = jax.vjp(
        lambda values: project(values, view_camera), arrived[:, position]
    )
    per_tile = jnp.transpose(slot_feats.reshape(9, tiles_here, slot_count), (1, 0, 2))
    result = grads_for_tiles(per_tile, live_mask, pixel_x, pixel_y, background, cotangent)
    param_grads = slot_back(jnp.transpose(result, (1, 0, 2)).reshape(9, rows_here))[0]
    outgoing = (
        jnp.zeros((gauss_params.shape[0], owners_total * capacity), jnp.float32)
        .at[:, position]
        .set(param_grads)
    )
    returned = lax.all_to_all(outgoing, "img", split_axis=1, concat_axis=1, tiled=True)
    local_grads = jnp.zeros(gauss_params.shape, jnp.float32).at[:, requested].add(returned)
    return lax.psum(local_grads, "view")


def solution(mesh):
    placed = (
        P(None, "img"),
        P("view", None),
        P(),
        P("view", "img", None),
        P("view", "img"),
        P("view", None, "img", None),
    )
    return jax.shard_map(
        per_device, mesh=mesh, in_specs=placed, out_specs=P(None, "img"), check_vma=False
    )
```

profile of v0, /device:TPU:1, one launch (start us, length us, event | category | flops | bytes accessed | tf_op | source)
XLA Modules:
  0.0 297.4 jit_solution(15419429696890813769)
XLA Ops:
  7.5 4.4 %sort.17 = (s32[1024]{0:T(1024)}, s32[1024]{0:T(1024)S(1)}) sort(s32[1024]{0:T(1024)S(1)} %get-tuple-element.205, s32[1024]{0:T(1024)S(1)} %iota.55), dimensions={0}, to_apply=%region_0.1 | sort | flops 10240 | bytes 16384 | tf_op jit(solution)/shard_map/jit(argsort)/sort | solution.py:250
  11.9 4.5 %gather_fusion = s32[1024]{0:T(1024)S(1)} fusion(s32[1024]{0:T(1024)S(1)} %get-tuple-element.205, s32[1024]{0:T(1024)S(1)} %get-tuple-element.206), kind=kCustom, calls=%fused_computation | custom fusion | bytes 12288 | tf_op jit(solution)/shard_map/gather | solution.py:251
  16.9 6.6 %gather_fusion.1 = s32[1024]{0:T(1024)S(1)} fusion(s32[128]{0:T(128)S(1)} %sub.280, s32[1024]{0:T(1024)S(1)} %broadcast_clamp_fusion.2), kind=kCustom, calls=%fused_computation.1 | custom fusion | bytes 12288 | tf_op jit(solution)/shard_map/gather | solution.py:257
  23.5 4.3 %scatter_custom_fusion = s32[1024]{0:T(1024)S(1)} fusion(s32[1024]{0:T(1024)S(1)} %get-tuple-element.207, s32[1024]{0:T(1024)S(1)} %subtract_add_fusion, s32[]{:T(128)} %copy.102), kind=kCustom, calls=%fused_computation.308 | custom fusion | bytes 4100 | tf_op jit(solution)/shard_map/scatter | solution.py:259
  27.8 4.3 %scatter_custom_fusion.1 = s32[2048]{0:T(1024)S(1)} fusion(s32[1024]{0:T(1024)S(1)} %get-tuple-element.203, s32[1024]{0:T(1024)S(1)} %get-tuple-element.204, s32[]{:T(128)} %copy.102), kind=kCustom, calls=%fused_computation.252 | custom fusion | bytes 8196 | tf_op jit(solution)/shard_map/scatter | solution.py:261
  32.1 0.7 all_to_all.24
  32.8 18.4 %all-to-all-start = ((s32[128,16,1]{1,2,0:T(1,128)}), s32[128,16,1]{1,2,0:T(1,128)S(1)}, u32[]{:S(2)}, u32[]{:S(2)}) async-start(s32[128,16,1]{1,2,0:T(1,128)} %bitcast.10), calls=%async_computation | async-start | bytes 131072 | tf_op jit(solution)/shard_map/all_to_all | solution.py:262
  66.0 2.8 copy.52
  68.8 0.7 reduce.7
  69.7 7.6 %gather_fusion.2 = f32[2048,59]{1,0:T(8,128)S(1)} fusion(f32[59,8192]{0,1:T(8,128)} %copy.52, s32[2048]{0:T(1024)S(1)} %broadcast_clamp_fusion), kind=kCustom, calls=%fused_computation.2 | custom fusion | bytes 974848 | tf_op jit(solution)/shard_map/gather | solution.py:270
  77.3 2.8 reshape.524
  80.1 13.7 %all-to-all-start.1 = ((f32[128,1,944]{2,1,0:T(1,128)}), f32[128,1,944]{2,1,0:T(1,128)S(1)}, u32[]{:S(2)}, u32[]{:S(2)}) async-start(f32[128,1,944]{2,1,0:T(1,128)} %reshape.524), calls=%async_computation.1 | async-start | bytes 1048576 | tf_op jit(solution)/shard_map/all_to_all | solution.py:269
  94.5 18.8 %all-to-all-done.1 = f32[128,1,944]{2,1,0:T(1,128)S(1)} async-done(((f32[128,1,944]{2,1,0:T(1,128)}), f32[128,1,944]{2,1,0:T(1,128)S(1)}, u32[]{:S(2)}, u32[]{:S(2)}) %all-to-all-start.1) | async-done | bytes 483360 | tf_op jit(solution)/shard_map/all_to_all | solution.py:269
  113.8 1.9 reduce.9
  115.7 0.8 reshape.525
  116.5 2.8 gather_fusion.3
  120.1 2.0 fusion.131
  122.7 9.1 %while.10 = (s32[]{:T(128)}, f32[2,2,9,256]{3,2,1,0:T(8,128)S(1)}, f32[2,2,3,256]{3,2,1,0:T(4,128)S(1)}, f32[2,2,9,256]{3,2,1,0:T(8,128)S(1)}, f32[2,2,256]{2,0,...) while((s32[]{:T(128)}, f32[2,2,9,256]{3,2,1,0:T(8,128)S(1)}, ...), condition=%wide.region_17.18_spmd, body=%wide.region_8.17_spmd.sunk | while | flops 827749888 | bytes 2936977 | solution.py:219
  124.1 0.8 convolution_exponential_fusion.2
  124.9 1.5 fusion.155
  128.6 0.8 convolution_exponential_fusion.2
  129.5 1.5 fusion.155
  133.2 1.9 multiply_multiply_fusion.4
  135.2 5.6 %fusion.82 = f32[1,1024]{1,0:T(1,128)S(1)} fusion(f32[1,1024]{1,0:T(1,128)S(1)} %bitcast.197, f32[1,1024]{1,0:T(1,128)S(1)} %bitcast.199, f32[1,1024]{1,0:T(1,128)S(1)} %get-tuple-element.164, f32[1,1024]{1,0:T(1,128)S(1)} %get-tuple-element.165, f32[1,1024]{1,0:T(1,128)S(1)} %get-tuple-element.166, f32[1,1024]{1,0:T(1,128)S(1)} %get-tuple-element.98, ...), kind=kLoop, calls=%fused_computation.255 | loop fusion | flops 48128 | bytes 53284 | tf_op jit(solution)/shard_map/transpose(jvp())/neg | solution.py:91
  141.3 3.3 %scatter_custom_fusion.2 = f32[59,2048]{0,1:T(8,128)S(1)} fusion(s32[1024]{0:T(1024)S(1)} %get-tuple-element.203, f32[1024,59]{1,0:T(8,128)S(1)} %copy.63, f32[]{:T(128)} %constant.146.clone.1), kind=kCustom, calls=%fused_computation.92 | custom fusion | bytes 483332 | tf_op jit(solution)/shard_map/scatter | solution.py:281
  144.6 2.0 reshape.526
  146.6 26.4 %all_to_all.36 = f32[128,1,944]{2,1,0:T(1,128)S(1)} all-to-all(f32[128,1,944]{2,1,0:T(1,128)S(1)} %reshape.526), channel_id=1, replica_groups=mesh['img'=128,'view'=4] {'img'}, dimensions={0} | all-to-all | bytes 966656 | tf_op jit(solution)/shard_map/all_to_all | solution.py:283
  173.0 1.9 reduce.10
  174.9 0.8 reshape.527
  175.7 13.7 %scatter_custom_fusion.3 = f32[59,8192]{0,1:T(8,128)} fusion(s32[2048]{0:T(1024)S(1)} %bitcast.206, f32[2048,59]{1,0:T(8,128)S(1)} %bitcast.188, f32[]{:T(128)} %constant.146.clone.1), kind=kCustom, calls=%fused_computation.86 | custom fusion | flops 120832 | bytes 1933316 | tf_op jit(solution)/shard_map/scatter-add | solution.py:284
  189.5 97.3 %all-reduce.35.cloned.1.call-done = f32[59,8192]{0,1:T(8,128)} async-done(((f32[59,8192]{0,1:T(8,128)}), f32[59,8192]{0,1:T(8,128)}) %all-reduce.35.cloned.1.call-update) | async-done | bytes 1933328 | tf_op jit(solution)/shard_map/psum | solution.py:285
  286.7 3.8 %copy.64 = f32[59,8192]{1,0:T(8,128)} copy(f32[59,8192]{0,1:T(8,128)} %all-reduce.35.cloned.1.call-done) | data formatting | bytes 3866624 | tf_op jit(solution)/shard_map/psum | solution.py:285
  (155 shorter events, 12.9 us)
Async XLA Ops:
  11.8 39.4 %copy-start.3 = (f32[1,6]{1,0:T(1,128)S(1)}, f32[1,6]{1,0:T(1,128)}, u32[]{:S(2)}) copy-start(f32[1,6]{1,0:T(1,128)} %param.9) | copy-start | bytes 76
  11.8 44.6 %copy-start.6 = (f32[1,3]{1,0:T(1,128)S(1)}, f32[1,3]{1,0:T(1,128)}, u32[]{:S(2)}) copy-start(f32[1,3]{1,0:T(1,128)} %constant.161.clone.1) | copy-start | bytes 40
  11.8 44.6 %copy-start.7 = (f32[1,3]{1,0:T(1,128)S(1)}, f32[1,3]{1,0:T(1,128)}, u32[]{:S(2)}) copy-start(f32[1,3]{1,0:T(1,128)} %constant.160.clone.1) | copy-start | bytes 40
  11.9 44.7 %copy-start.4 = (f32[1,3]{1,0:T(1,128)S(1)}, f32[1,3]{1,0:T(1,128)}, u32[]{:S(2)}) copy-start(f32[1,3]{1,0:T(1,128)} %constant.159.clone.1) | copy-start | bytes 40
  11.9 53.4 %copy-start.5 = (s32[1,4]{1,0:T(1,128)S(1)}, s32[1,4]{1,0:T(1,128)}, u32[]{:S(2)}) copy-start(s32[1,4]{1,0:T(1,128)} %param.12) | copy-start | bytes 52
  11.9 54.1 %copy-start.2 = (f32[1,3,4,256]{3,2,1,0:T(4,128)S(1)}, f32[1,3,4,256]{3,2,1,0:T(4,128)}, u32[]{:S(2)}) copy-start(f32[1,3,4,256]{3,2,1,0:T(4,128)} %param.13) | copy-start | bytes 36868
  11.9 54.1 %copy-start = (f32[59,8192]{1,0:T(8,128)S(1)}, f32[59,8192]{1,0:T(8,128)}, u32[]{:S(2)}) copy-start(f32[59,8192]{1,0:T(8,128)} %param.8) | copy-start | bytes 5799940
  32.8 36.0 %all-to-all-start = ((s32[128,16,1]{1,2,0:T(1,128)}), s32[128,16,1]{1,2,0:T(1,128)S(1)}, u32[]{:S(2)}, u32[]{:S(2)}) async-start(s32[128,16,1]{1,2,0:T(1,128)} %bitcast.10), calls=%async_computation | async-start | bytes 131072 | tf_op jit(solution)/shard_map/all_to_all | solution.py:262
  80.1 33.2 %all-to-all-start.1 = ((f32[128,1,944]{2,1,0:T(1,128)}), f32[128,1,944]{2,1,0:T(1,128)S(1)}, u32[]{:S(2)}, u32[]{:S(2)}) async-start(f32[128,1,944]{2,1,0:T(1,128)} %reshape.524), calls=%async_computation.1 | async-start | bytes 1048576 | tf_op jit(solution)/shard_map/all_to_all | solution.py:269
  93.8 28.9 %copy-start.1 = (f32[3]{0:T(128)S(1)}, f32[3]{0:T(128)}, u32[]{:S(2)}) copy-start(f32[3]{0:T(128)} %param.10) | copy-start | bytes 40
  93.8 192.9 %all-reduce.35.cloned.1.call-start = ((), (), s32[]{:S(2)}) async-start(), calls=%async_computation.3 | async-start | bytes 8388608 | tf_op jit(solution)/shard_map/psum | solution.py:285
Sparse Core Ops, SparseCore 0:
  189.6 97.1 all-reduce.34
where the time goes:
time: 298 us; the launch traced here: 297 us
  waiting for transfers between devices  116 us (39%)
  local copies, waits for them, and re-layouts  51.8 us (17%)
  other arithmetic  36.7 us (12%)
  starting transfers between devices  32.4 us (11%)
  blocking collectives  26.4 us (9%)
  between operations  25.6 us (9%)
  matrix products  8.1 us (3%)
    psum x1, waiting for transfers between devices, per_device(): return lax.psum(local_grads, 'view')  97.3 us
    all_to_all x1, blocking collectives, per_device(): lax.all_to_all(outgoing, 'img', split_axis=1, concat_axis=1, tiled=True)  26.4 us
    all_to_all x1, waiting for transfers between devices, per_device(): lax.all_to_all(gauss_params[:, requested], 'img', split_axis=1, concat_ax...  18.8 us
    all_to_all x1, starting transfers between devices, per_device(): lax.all_to_all(requests, 'img', split_axis=0, concat_axis=0, tiled=True)  18.4 us
    all_to_all x1, starting transfers between devices, per_device(): lax.all_to_all(gauss_params[:, requested], 'img', split_axis=1, concat_ax...  13.7 us
    scatter-add x1, other arithmetic, per_device(): jnp.zeros(gauss_params.shape, jnp.float32).at[:, requested].add(returned)  13.7 us
    unnamed x31, local copies, waits for them, and re-layouts  9.93 us
    gather x1, local copies, waits for them, and re-layouts, per_device(): gauss_params[:, requested]  7.65 us
  transfers between devices with their start and end apart: 3, of which 2 were waited for; matrix products, arithmetic and copies ran while one was open for 2% of the time, Pallas kernels for 0%

commit v1 on v0

v1 whole, which is shorter than its diff:
```python
import functools

import jax
import jax.numpy as jnp
from jax import lax
from jax.experimental import pallas as pl
from jax.experimental.pallas import tpu as pltpu
from jax.sharding import PartitionSpec as P

SIDE = 16
TX = 16
PIX = 256
SLOTS = 256
TILES_DEV = 4
OWNERS = 128
CAP = 16
LANES = 128
G_DEV = 8192
GROUPS = G_DEV // LANES
PARAMS = 59
PITCH = 64
CHUNKS = 8
CHUNK = G_DEV // CHUNKS
FEATS = 9
PACK = 256

FOCAL = 2.0
DILATION = 0.0001
SH_ZERO = 0.28209479177387814
SH_ONE = 0.4886025119029199
SH_TWO = (
    1.0925484305920792,
    -1.0925484305920792,
    0.31539156525252005,
    -1.0925484305920792,
    0.5462742152960396,
)
SH_THREE = (
    -0.5900435899266435,
    2.890611442640554,
    -0.4570457994644658,
    0.3731763325901154,
    -0.4570457994644658,
    1.445305721320277,
    -0.5900435899266435,
)

F32 = jnp.float32
BF16 = jnp.bfloat16
VMEM_LIMIT = 32 * 1024 * 1024


def iota(shape, axis, dtype=jnp.int32):
    return lax.broadcasted_iota(dtype, shape, axis)


def spread(row, shape):
    return jnp.broadcast_to(row, shape)


def halves(values):
    high = values.astype(BF16)
    low = (values - high.astype(F32)).astype(BF16)
    return high, low


def dot(left, right):
    return jnp.dot(left, right, preferred_element_type=F32)


def dot_lanes(left, right):
    return lax.dot_general(left, right, (((1,), (1,)), ((), ())), preferred_element_type=F32)


def camera_rows(camera_ref):
    row = iota((8, LANES), 0)
    block = jnp.zeros((8, LANES), F32)
    for index in range(6):
        block = jnp.where(row == index, camera_ref[0, index], block)
    return block


def rotation(block):
    cosines, sines = jnp.cos(block), jnp.sin(block)

    def take(values, index):
        return spread(values[index : index + 1, :], (8, LANES))

    cx, cy, cz = (take(cosines, index) for index in range(3))
    sx, sy, sz = (take(sines, index) for index in range(3))
    inner = [
        [cy, sy * sx, sy * cx],
        [None, cx, -sx],
        [-sy, cy * sx, cy * cx],
    ]
    rotate = [
        [cz * inner[0][0], cz * inner[0][1] - sz * inner[1][1], cz * inner[0][2] - sz * inner[1][2]],
        [sz * inner[0][0], sz * inner[0][1] + cz * inner[1][1], sz * inner[0][2] + cz * inner[1][2]],
        inner[2],
    ]
    offset = [take(block, 3 + index) for index in range(3)]
    return rotate, offset


def camera_center(rotate, offset):
    return [
        -(rotate[0][col] * offset[0] + rotate[1][col] * offset[1] + rotate[2][col] * offset[2])
        for col in range(3)
    ]


def shape_matrix(log_scales, quaternion):
    scales = [jnp.exp(value) for value in log_scales]
    norm = lax.rsqrt(
        quaternion[0] * quaternion[0]
        + quaternion[1] * quaternion[1]
        + quaternion[2] * quaternion[2]
        + quaternion[3] * quaternion[3]
    )
    real, im_i, im_j, im_k = (part * norm for part in quaternion)
    local = [
        [1.0 - 2.0 * (im_j * im_j + im_k * im_k), 2.0 * (im_i * im_j - real * im_k), 2.0 * (im_i * im_k + real * im_j)],
        [2.0 * (im_i * im_j + real * im_k), 1.0 - 2.0 * (im_i * im_i + im_k * im_k), 2.0 * (im_j * im_k - real * im_i)],
        [2.0 * (im_i * im_k - real * im_j), 2.0 * (im_j * im_k + real * im_i), 1.0 - 2.0 * (im_i * im_i + im_j * im_j)],
    ]
    return [[local[row][col] * scales[col] for col in range(3)] for row in range(3)]


def harmonics(along_x, along_y, along_z):
    square_x, square_y, square_z = along_x * along_x, along_y * along_y, along_z * along_z
    return [
        jnp.full_like(along_x, SH_ZERO),
        -SH_ONE * along_y,
        SH_ONE * along_z,
        -SH_ONE * along_x,
        SH_TWO[0] * along_x * along_y,
        SH_TWO[1] * along_y * along_z,
        SH_TWO[2] * (2.0 * square_z - square_x - square_y),
        SH_TWO[3] * along_x * along_z,
        SH_TWO[4] * (square_x - square_y),
        SH_THREE[0] * along_y * (3.0 * square_x - square_y),
        SH_THREE[1] * along_x * along_y * along_z,
        SH_THREE[2] * along_y * (4.0 * square_z - square_x - square_y),
        SH_THREE[3] * along_z * (2.0 * square_z - 3.0 * square_x - 3.0 * square_y),
        SH_THREE[4] * along_x * (4.0 * square_z - square_x - square_y),
        SH_THREE[5] * along_z * (square_x - square_y),
        SH_THREE[6] * along_x * (square_x - 3.0 * square_y),
    ]


def screen_features(center, shape, rotate, offset):
    viewed = [
        rotate[row][0] * center[0] + rotate[row][1] * center[1] + rotate[row][2] * center[2] + offset[row]
        for row in range(3)
    ]
    depth_inv = 1.0 / viewed[2]
    near = FOCAL * depth_inv
    screen_x = viewed[0] * near
    screen_y = viewed[1] * near
    slope_x = -screen_x * depth_inv
    slope_y = -screen_y * depth_inv
    to_camera = [
        [near * rotate[0][col] + slope_x * rotate[2][col] for col in range(3)],
        [near * rotate[1][col] + slope_y * rotate[2][col] for col in range(3)],
    ]
    mapped = [
        [
            to_camera[row][0] * shape[0][col] + to_camera[row][1] * shape[1][col] + to_camera[row][2] * shape[2][col]
            for col in range(3)
        ]
        for row in range(2)
    ]
    first, second = mapped
    cov_a = first[0] * first[0] + first[1] * first[1] + first[2] * first[2] + DILATION
    cov_b = first[0] * second[0] + first[1] * second[1] + first[2] * second[2]
    cov_c = second[0] * second[0] + second[1] * second[1] + second[2] * second[2] + DILATION
    inverse = 1.0 / (cov_a * cov_c - cov_b * cov_b)
    return [screen_x, screen_y, cov_c * inverse, -cov_b * inverse, cov_a * inverse]


def direction_basis(center, eye):
    toward = [center[index] - eye[index] for index in range(3)]
    norm = lax.rsqrt(toward[0] * toward[0] + toward[1] * toward[1] + toward[2] * toward[2])
    return harmonics(toward[0] * norm, toward[1] * norm, toward[2] * norm)


def spread_columns(params_ref, held_ref):
    for group in range(CHUNK // LANES):
        columns = slice(group * LANES, (group + 1) * LANES)
        held_ref[group * PITCH : group * PITCH + 56, :] = params_ref[0:56, columns]
        held_ref[group * PITCH + 56 : group * PITCH + PARAMS, :] = params_ref[56:PARAMS, columns]


def project_kernel(camera_ref, params_ref, feats_ref, held_ref):
    spread_columns(params_ref, held_ref)

    def param(index):
        return held_ref[pl.ds(index, 8, stride=PITCH), :]

    rotate, offset = rotation(camera_rows(camera_ref))
    center = [param(index) for index in range(3)]
    shape = shape_matrix([param(3 + index) for index in range(3)], [param(6 + index) for index in range(4)])
    screen = screen_features(center, shape, rotate, offset)
    basis = direction_basis(center, camera_center(rotate, offset))
    opacity = 1.0 / (1.0 + jnp.exp(-param(10)))
    colors = []
    for channel in range(3):
        total = basis[0] * param(11 + channel)
        for term in range(1, 16):
            total = total + basis[term] * param(11 + 3 * term + channel)
        colors.append(total + 0.5)
    for index, value in enumerate(screen + [opacity] + colors):
        feats_ref[index] = value


def route_kernel(lists_ref, request_ref, aux_ref):
    owner_iota = iota((OWNERS, LANES), 0)
    before = (iota((LANES, 2 * LANES), 0) < iota((LANES, 2 * LANES), 1)).astype(F32)
    before = before.astype(BF16)
    rank_iota = iota((CAP, LANES), 0)
    lane = iota((1, LANES), 1)
    carried = jnp.zeros((OWNERS, LANES), F32)
    table = jnp.zeros((4 * CAP, OWNERS), F32)
    for row in range(8):
        ids = lists_ref[0, row // 2 : row // 2 + 1, (row % 2) * LANES : (row % 2 + 1) * LANES]
        owner = ids // G_DEV
        column = ids % G_DEV
        hot = owner_iota == spread(owner, (OWNERS, LANES))
        hot_f32 = hot.astype(F32)
        hot_bf16 = hot_f32.astype(BF16)
        counts = dot(hot_bf16, before)
        rank = jnp.sum(jnp.where(hot, counts[:, :LANES] + carried, 0.0), axis=0, keepdims=True)
        carried = carried + counts[:, LANES:]
        rank = rank.astype(jnp.int32)
        at_rank = rank_iota == spread(rank, (CAP, LANES))
        pieces = [column // LANES, column % LANES, lane * 0 + row, lane + 1]
        stacked = jnp.concatenate(
            [jnp.where(at_rank, spread(piece.astype(F32), (CAP, LANES)), 0.0) for piece in pieces], axis=0
        )
        table = table + dot_lanes(stacked.astype(BF16), hot_bf16)
        aux_ref[row : row + 1, :] = owner
        aux_ref[8 + row : 9 + row, :] = rank
    high, low, slot_row, slot_lane = (table[CAP * part : CAP * (part + 1)] for part in range(4))
    used = slot_lane > 0.5
    slot = jnp.where(used, slot_row * LANES + slot_lane - 1.0, -1.0)
    wanted = jnp.where(used, high * LANES + low, -1.0)
    aux_ref[16 : 16 + CAP, :] = slot.astype(jnp.int32)
    aux_ref[16 + CAP : 16 + 2 * CAP, :] = wanted.astype(jnp.int32)
    padded = jnp.concatenate([wanted, jnp.zeros((LANES - CAP, OWNERS), F32)], axis=0)
    request_ref[...] = padded.T.astype(jnp.int32)


def pick(row, lanes_at):
    return jnp.take_along_axis(spread(row, (8, LANES)), lanes_at, axis=1, mode="promise_in_bounds")


def store_rows(out_ref, table):
    out_ref[pl.ds(0, LANES, stride=2), :] = table[:LANES].T
    out_ref[pl.ds(1, LANES, stride=2), :] = table[LANES:].T


def gather_kernel(request_ref, feats_ref, out_ref):
    wanted = request_ref[...].astype(F32).T[:CAP].astype(jnp.int32)
    high, low = wanted >> 7, wanted & (LANES - 1)
    parts = [(high[:8], low[:8]), (high[8:], low[8:])]

    def step(group, found):
        found = list(found)
        for index in range(FEATS):
            row = feats_ref[index, pl.ds(group, 1), :]
            for part, (at_group, at_lane) in enumerate(parts):
                place = 2 * index + part
                found[place] = jnp.where(at_group == group, pick(row, at_lane), found[place])
        return tuple(found)

    start = tuple(jnp.zeros((8, LANES), F32) for _ in range(2 * FEATS))
    found = lax.fori_loop(0, GROUPS, step, start, unroll=8)
    table = jnp.concatenate(list(found) + [jnp.zeros((PACK - FEATS * CAP, LANES), F32)], axis=0)
    store_rows(out_ref, table)


PIX_CHUNK = 64


def render_kernel(
    height, lengths_ref, background_ref, camera_ref, first_ref, arrived_ref, aux_ref, cotangent_ref, out_ref,
    slot_ref, table_ref, grad_ref, pixel_ref, weight_ref,
):
    table_ref[:LANES, :] = arrived_ref[pl.ds(0, LANES, stride=2), :].T
    table_ref[LANES:, :] = arrived_ref[pl.ds(1, LANES, stride=2), :].T
    owner = aux_ref[0:8, :]
    rank = aux_ref[8:16, :]
    at_rank = [rank == place for place in range(CAP)]
    for index in range(FEATS):
        value = jnp.zeros((8, LANES), F32)
        for place in range(CAP):
            row = table_ref[index * CAP + place : index * CAP + place + 1, :]
            value = jnp.where(at_rank[place], pick(row, owner), value)
        slot_ref[index * 8 : index * 8 + 8, :] = value

    within = iota((PIX, SLOTS), 0)
    pixel_ref[0] = (within % SIDE).astype(F32) * (2.0 / (TX * SIDE))
    pixel_ref[1] = (within // SIDE).astype(F32) * (2.0 / (height * SIDE))
    slot_row, slot_col = iota((SLOTS, SLOTS), 0), iota((SLOTS, SLOTS), 1)
    weight_ref[0] = (slot_row < slot_col).astype(F32).astype(BF16)
    weight_ref[1] = (slot_row > slot_col).astype(F32).astype(BF16)
    slot_place = iota((1, SLOTS), 1)

    def tile(index, carry):
        def slots(feature):
            return jnp.concatenate(
                [slot_ref[pl.ds(feature * 8 + 2 * index + half, 1), :] for half in range(2)], axis=1
            )

        tile_id = first_ref[0] + index
        tile_x = ((tile_id % TX * SIDE).astype(F32) + 0.5) * (2.0 / (TX * SIDE)) - 1.0
        tile_y = ((tile_id // TX * SIDE).astype(F32) + 0.5) * (2.0 / (height * SIDE)) - 1.0
        at_x = slots(0) - tile_x
        at_y = slots(1) - tile_y
        conic_a, conic_b, conic_c = slots(2), slots(3), slots(4)
        opacity = slots(5)
        live_opacity = jnp.where(slot_place < lengths_ref[0, index], opacity, 0.0)
        colors = [slots(6 + channel) for channel in range(3)]
        half_a, full_b, half_c = -0.5 * conic_a, -conic_b, -0.5 * conic_c
        shades = [cotangent_ref[0, channel, pl.ds(index, 1), :] for channel in range(3)]
        behind = (
            shades[0] * background_ref[0] + shades[1] * background_ref[1] + shades[2] * background_ref[2]
        )
        columns = jnp.concatenate(shades + [behind, jnp.zeros((4, PIX), F32)], axis=0).T

        sums = [jnp.zeros((8, SLOTS), F32) for _ in range(9)]

        def fold(values):
            return jnp.sum(values.reshape(PIX_CHUNK // 8, 8, SLOTS), axis=0)

        for chunk in range(PIX // PIX_CHUNK):
            rows = slice(chunk * PIX_CHUNK, (chunk + 1) * PIX_CHUNK)
            shape = (PIX_CHUNK, SLOTS)
            delta_x = pixel_ref[0, rows, :] - at_x
            delta_y = pixel_ref[1, rows, :] - at_y
            exponent = (half_a * delta_x + full_b * delta_y) * delta_x + half_c * delta_y * delta_y
            coverage = live_opacity * jnp.exp(exponent)
            log_pass = jnp.log(1.0 - coverage)
            high, low = halves(log_pass)
            prefix = dot(high, weight_ref[0]) + dot(low, weight_ref[0])
            passed = jnp.exp(prefix)
            weight = coverage * passed
            shade = [spread(columns[rows, channel : channel + 1], shape) for channel in range(3)]
            gain = shade[0] * colors[0] + shade[1] * colors[1] + shade[2] * colors[2]
            product = weight * gain
            high, low = halves(product)
            later = dot(high, weight_ref[1]) + dot(low, weight_ref[1])
            remain = jnp.exp(prefix[:, SLOTS - 1 :] + log_pass[:, SLOTS - 1 :])
            later = later + spread(columns[rows, 3:4] * remain, shape)
            slope = -0.5 * (product - coverage / (1.0 - coverage) * later)
            slope_x = slope * delta_x
            slope_y = slope * delta_y
            parts = [slope, slope_x, slope_y, slope_x * delta_x, slope_x * delta_y, slope_y * delta_y]
            parts += [shade[channel] * weight for channel in range(3)]
            sums = [total + fold(part) for total, part in zip(sums, parts)]

        sums = [jnp.sum(total, axis=0, keepdims=True) for total in sums]
        total, sum_x, sum_y, sum_xx, sum_xy, sum_yy = sums[:6]
        grads = [
            -2.0 * (conic_a * sum_x + conic_b * sum_y),
            -2.0 * (conic_b * sum_x + conic_c * sum_y),
            sum_xx,
            2.0 * sum_xy,
            sum_yy,
            -2.0 * total / opacity,
        ] + sums[6:]
        for feature, value in enumerate(grads):
            for half in range(2):
                grad_ref[pl.ds(feature * 8 + 2 * index + half, 1), :] = value[:, half * LANES : (half + 1) * LANES]
        return carry

    lax.fori_loop(0, TILES_DEV, tile, 0)

    slot = aux_ref[16 : 16 + CAP, :]
    wanted = aux_ref[16 + CAP : 16 + 2 * CAP, :].astype(F32)
    parts = [(slot[8 * part : 8 * part + 8] >> 7, slot[8 * part : 8 * part + 8] & (LANES - 1)) for part in range(2)]
    blocks = []
    for feature in range(FEATS):
        for at_row, at_lane in parts:
            value = jnp.zeros((8, LANES), F32)
            for row in range(8):
                grads = grad_ref[feature * 8 + row : feature * 8 + row + 1, :]
                value = jnp.where(at_row == row, pick(grads, at_lane), value)
            blocks.append(value)
    blocks += [wanted, camera_rows(camera_ref), jnp.zeros((PACK - FEATS * CAP - CAP - 8, LANES), F32)]
    store_rows(out_ref, jnp.concatenate(blocks, axis=0))


WIDE = 256
TALL = G_DEV // WIDE


def scatter_view(view, arrived_ref, grads_ref, camera_ref):
    tall_iota = iota((TALL, LANES), 0)
    wide_iota = iota((WIDE, LANES), 0)
    first = arrived_ref[view, pl.ds(0, LANES, stride=2), :].T
    second = arrived_ref[view, pl.ds(1, LANES, stride=2), :].T
    rest = FEATS * CAP - LANES
    values = jnp.concatenate([first, second[:rest]], axis=0)
    wanted = second[rest : rest + CAP].astype(jnp.int32)
    camera_ref[view] = second[rest + CAP : rest + CAP + 8]
    high_place, low_place = wanted >> 8, wanted & (WIDE - 1)
    high, low = halves(values)
    high, low = high.astype(F32), low.astype(F32)
    lefts, rights = [], []
    for place in range(CAP):
        at_high = tall_iota == spread(high_place[place : place + 1], (TALL, LANES))
        at_low = wide_iota == spread(low_place[place : place + 1], (WIDE, LANES))
        at_low = at_low.astype(F32).astype(BF16)
        for source in (high, low):
            rows = [source[index * CAP + place : index * CAP + place + 1] for index in range(FEATS)]
            left = [jnp.where(at_high, spread(row, (TALL, LANES)), 0.0) for row in rows]
            lefts.append(jnp.concatenate(left, axis=0).astype(BF16))
            rights.append(at_low)
    total = dot_lanes(jnp.concatenate(lefts, axis=1), jnp.concatenate(rights, axis=1))
    for half in range(2):
        grads_ref[view, pl.ds(half, FEATS * TALL, stride=2), :] = total[:, half * LANES : (half + 1) * LANES]


def pullback_kernel(arrived_ref, params_ref, out_ref, held_ref, sums_ref, grads_ref, camera_ref):
    views = arrived_ref.shape[0]
    chunk = pl.program_id(0)

    @pl.when(chunk == 0)
    def scatter():
        def one_view(view, carry):
            scatter_view(view, arrived_ref, grads_ref, camera_ref)
            return carry

        lax.fori_loop(0, views, one_view, 0)

    spread_columns(params_ref, held_ref)

    def param(index):
        return held_ref[pl.ds(index, 8, stride=PITCH), :]

    def keep(index, value):
        sums_ref[pl.ds(index, 8, stride=PITCH), :] = value

    def kept(index):
        return sums_ref[pl.ds(index, 8, stride=PITCH), :]

    center = [param(index) for index in range(3)]
    shape, shape_back = jax.vjp(
        shape_matrix, [param(3 + index) for index in range(3)], [param(6 + index) for index in range(4)]
    )
    center_grad, shape_grad, opacity_grad = None, None, None
    for view in range(views):
        def cotangent(feature):
            return grads_ref[view, pl.ds(pl.multiple_of(feature * GROUPS + chunk * 8, 8), 8), :]

        rotate, offset = rotation(camera_ref[view])
        eye = camera_center(rotate, offset)
        basis, basis_back = jax.vjp(lambda place: direction_basis(place, eye), center)
        colors = [cotangent(6 + channel) for channel in range(3)]
        basis_grad = []
        for term in range(16):
            total = None
            for channel in range(3):
                index = 11 + 3 * term + channel
                piece = basis[term] * colors[channel]
                keep(index, piece if view == 0 else kept(index) + piece)
                piece = param(index) * colors[channel]
                total = piece if total is None else total + piece
            basis_grad.append(total)
        (along,) = basis_back(basis_grad)
        unused, screen_back = jax.vjp(
            lambda place, matrix: screen_features(place, matrix, rotate, offset), center, shape
        )
        moved, bent = screen_back([cotangent(index) for index in range(5)])
        pieces = [along[axis] + moved[axis] for axis in range(3)]
        faded = cotangent(5)
        if view == 0:
            center_grad, shape_grad, opacity_grad = pieces, bent, faded
        else:
            center_grad = [one + other for one, other in zip(center_grad, pieces)]
            shape_grad = [[one + other for one, other in zip(*rows)] for rows in zip(shape_grad, bent)]
            opacity_grad = opacity_grad + faded
    scale_grad, quaternion_grad = shape_back(shape_grad)
    opacity = 1.0 / (1.0 + jnp.exp(-param(10)))
    firsts = center_grad + list(scale_grad) + list(quaternion_grad) + [opacity * (1.0 - opacity) * opacity_grad]
    for index, value in enumerate(firsts):
        keep(index, value)
    for group in range(CHUNK // LANES):
        columns = slice(group * LANES, (group + 1) * LANES)
        out_ref[0:56, columns] = sums_ref[group * PITCH : group * PITCH + 56, :]
        out_ref[56:PARAMS, columns] = sums_ref[group * PITCH + 56 : group * PITCH + PARAMS, :]


def call(kernel, out_shape, operands, smalls=(), scratch=(), **kwargs):
    spaces = [pltpu.SMEM if index < smalls else pltpu.VMEM for index in range(len(operands))]
    single = not isinstance(out_shape, (list, tuple))
    outs = pl.BlockSpec(memory_space=pltpu.VMEM)
    return pl.pallas_call(
        kernel,
        out_shape=out_shape,
        in_specs=[pl.BlockSpec(memory_space=space) for space in spaces],
        out_specs=outs if single else [outs] * len(out_shape),
        scratch_shapes=list(scratch),
        compiler_params=pltpu.CompilerParams(vmem_limit_bytes=VMEM_LIMIT),
        **kwargs,
    )(*operands)


def route(tile_lists):
    return call(
        route_kernel,
        [jax.ShapeDtypeStruct((OWNERS, LANES), jnp.int32), jax.ShapeDtypeStruct((16 + 2 * CAP, LANES), jnp.int32)],
        [tile_lists],
        smalls=0,
    )


def project(camera, gauss_params):
    return pl.pallas_call(
        project_kernel,
        grid=(CHUNKS,),
        out_shape=jax.ShapeDtypeStruct((FEATS, GROUPS, LANES), F32),
        in_specs=[
            pl.BlockSpec(memory_space=pltpu.SMEM),
            pl.BlockSpec((PARAMS, CHUNK), lambda chunk: (0, chunk)),
        ],
        out_specs=pl.BlockSpec((FEATS, 8, LANES), lambda chunk: (0, chunk, 0)),
        scratch_shapes=[pltpu.VMEM((8 * PITCH, LANES), F32)],
        compiler_params=pltpu.CompilerParams(vmem_limit_bytes=VMEM_LIMIT),
    )(camera, gauss_params)


def gather(requested, features):
    return call(
        gather_kernel, jax.ShapeDtypeStruct((2 * OWNERS, LANES), F32), [requested, features], smalls=0
    )


def render(height, tile_lengths, background, camera, first_tile, arrived, aux, cotangent):
    return call(
        functools.partial(render_kernel, height),
        jax.ShapeDtypeStruct((2 * OWNERS, LANES), F32),
        [tile_lengths, background, camera, first_tile, arrived, aux, cotangent],
        smalls=4,
        scratch=[
            pltpu.VMEM((FEATS * 8, LANES), F32),
            pltpu.VMEM((2 * OWNERS, LANES), F32),
            pltpu.VMEM((FEATS * 8, LANES), F32),
            pltpu.VMEM((2, PIX, SLOTS), F32),
            pltpu.VMEM((2, SLOTS, SLOTS), BF16),
        ],
    )


def pullback(arrived, gauss_params):
    views = arrived.shape[0]
    return pl.pallas_call(
        pullback_kernel,
        grid=(CHUNKS,),
        out_shape=jax.ShapeDtypeStruct((PARAMS, G_DEV), F32),
        in_specs=[
            pl.BlockSpec((views, 2 * OWNERS, LANES), lambda chunk: (0, 0, 0)),
            pl.BlockSpec((PARAMS, CHUNK), lambda chunk: (0, chunk)),
        ],
        out_specs=pl.BlockSpec((PARAMS, CHUNK), lambda chunk: (0, chunk)),
        scratch_shapes=[
            pltpu.VMEM((8 * PITCH, LANES), F32),
            pltpu.VMEM((8 * PITCH, LANES), F32),
            pltpu.VMEM((views, FEATS * GROUPS, LANES), F32),
            pltpu.VMEM((views, 8, LANES), F32),
        ],
        compiler_params=pltpu.CompilerParams(vmem_limit_bytes=VMEM_LIMIT),
    )(arrived, gauss_params)


def per_device(gauss_params, camera, background, tile_lists, tile_lengths, pixel_cotangent):
    owners_total = lax.axis_size("img")
    views = lax.axis_size("view")
    tiles_here = tile_lists.shape[1]
    height = tiles_here * owners_total // TX
    first_tile = (lax.axis_index("img") * tiles_here).astype(jnp.int32).reshape(1)
    requests, aux = route(tile_lists)
    features = project(camera, gauss_params)
    requested = lax.all_to_all(requests, "img", split_axis=0, concat_axis=0, tiled=True)
    outgoing = gather(requested, features)
    arrived = lax.all_to_all(outgoing, "img", split_axis=0, concat_axis=0, tiled=True)
    slot_grads = render(
        height, tile_lengths, background, camera, first_tile, arrived, aux, pixel_cotangent
    )
    returned = lax.all_to_all(slot_grads, "img", split_axis=0, concat_axis=0, tiled=True)
    copies = jnp.broadcast_to(returned[None], (views,) + returned.shape)
    everyone = lax.all_to_all(copies, "view", split_axis=0, concat_axis=0, tiled=True)
    return pullback(everyone, gauss_params)


def solution(mesh):
    placed = (
        P(None, "img"),
        P("view", None),
        P(),
        P("view", "img", None),
        P("view", "img"),
        P("view", None, "img", None),
    )
    return jax.shard_map(
        per_device, mesh=mesh, in_specs=placed, out_specs=P(None, "img"), check_vma=False
    )
```

time: 298 us -> 106 us (0.36)
  waiting for transfers between devices: 116 us -> 19 us
  local copies, waits for them, and re-layouts: 51.8 us -> 3 us
  other arithmetic: 36.7 us -> 0 us
  Pallas kernels: 0 us -> 27.5 us
  between operations: 25.6 us -> 0.07 us
  matrix products: 8.1 us -> 0 us
  starting transfers between devices: 32.4 us -> 25.3 us
  blocking collectives: 26.4 us -> 30.4 us
    psum x1 -> x0, waiting for transfers between devices: 97.3 us -> none  [per_device(): return lax.psum(local_grads, 'view')]
    pallas_call x0 -> x5, Pallas kernels: none -> 27.5 us  [the longest x1 16.9 us: pullback(): pl.pallas_call(pullback_kernel, grid=(CHUNKS,), out_shape=jax.ShapeDtypeS...]
    gather x5 -> x0, local copies, waits for them, and re-layouts: 21.8 us -> none  [the longest x1 7.65 us: per_device(): gauss_params[:, requested]]
    scatter-add x1 -> x0, other arithmetic: 13.7 us -> none  [per_device(): jnp.zeros(gauss_params.shape, jnp.float32).at[:, requested].add(returned)]
    scatter x3 -> x0, local copies, waits for them, and re-layouts: 12 us -> none  [the longest x1 4.32 us: per_device(): jnp.zeros((owners_total * capacity,), jnp.int32).at[position].set(column_of)]
    dot_general x13 -> x0, matrix products: 8.1 us -> none  [the longest x4 4.58 us: render_tile(): prefix = jnp.dot(log_pass, earlier, precision=lax.Precision.HIGHEST)]
    unnamed x31 -> x16, local copies, waits for them, and re-layouts: 9.93 us -> 2.96 us
    all_to_all x1, waiting for transfers between devices: 0.01 us -> 6.84 us  [per_device(): lax.all_to_all(requests, 'img', split_axis=0, concat_axis=0, tiled=True)]
  transfers between devices with their start and end apart: 3 -> 2, of which waited for: 2 -> 2; matrix products, arithmetic and copies ran while one was open for 2% -> 0% of each run, Pallas kernels for 0% -> 2%
where the time goes in v1:
time: 106 us; the launch traced here: 105 us
  blocking collectives  30.4 us (29%)
  Pallas kernels  27.5 us (26%)
  starting transfers between devices  25.3 us (24%)
  waiting for transfers between devices  19 us (18%)
  local copies, waits for them, and re-layouts  3 us (3%)
    all_to_all x1, starting transfers between devices, per_device(): lax.all_to_all(requests, 'img', split_axis=0, concat_axis=0, tiled=True)  18.4 us
    all_to_all x1, blocking collectives, per_device(): lax.all_to_all(slot_grads, 'img', split_axis=0, concat_axis=0, tiled=True)  18.1 us
    pallas_call x1, Pallas kernels, pullback(): pl.pallas_call(pullback_kernel, grid=(CHUNKS,), out_shape=jax.ShapeDtypeS...  16.9 us
    all_to_all x1, blocking collectives, per_device(): lax.all_to_all(copies, 'view', split_axis=0, concat_axis=0, tiled=True)  12.3 us
    all_to_all x1, waiting for transfers between devices, per_device(): lax.all_to_all(outgoing, 'img', split_axis=0, concat_axis=0, tiled=True)  12.2 us
    pallas_call x3, Pallas kernels, call(): pl.pallas_call(kernel, out_shape=out_shape, in_specs=[pl.BlockSpec(memory...  8.25 us
    all_to_all x1, starting transfers between devices, per_device(): lax.all_to_all(outgoing, 'img', split_axis=0, concat_axis=0, tiled=True)  6.9 us
    all_to_all x1, waiting for transfers between devices, per_device(): lax.all_to_all(requests, 'img', split_axis=0, concat_axis=0, tiled=True)  6.84 us
  transfers between devices with their start and end apart: 2, of which 2 were waited for; matrix products, arithmetic and copies ran while one was open for 0% of the time, Pallas kernels for 2%

profile of v1, /device:TPU:1, one launch (start us, length us, event | category | flops | bytes accessed | tf_op | source)
XLA Modules:
  0.0 105.4 jit_solution(10185790610291248646)
XLA Ops:
  0.0 0.0 copy-start.2
  0.0 0.0 copy-start.3
  0.0 0.7 copy-done.3
  0.7 0.0 copy-start.5
  0.7 0.0 copy-start.6
  0.7 0.0 copy-start.7
  0.7 1.3 %shard_map.64 = (s32[128,128]{1,0:T(8,128)}, s32[48,128]{1,0:T(8,128)S(1)}) custom-call(s32[1,4,256]{2,1,0:T(4,128)S(1)} %copy-done.3), custom_call_target="tpu_custom_call" | custom-call | tf_op jit(solution)/shard_map/pallas_call | solution.py:499
  2.0 18.4 %all-to-all-start = ((s32[128,1,128]{2,1,0:T(1,128)}), s32[128,1,128]{2,1,0:T(1,128)S(1)}, u32[]{:S(2)}, u32[]{:S(2)}) async-start(s32[128,1,128]{2,1,0:T(1,128)} %bitcast.2), calls=%async_computation | async-start | bytes 131072 | tf_op jit(solution)/shard_map/all_to_all | solution.py:585
  20.4 0.0 copy-start
  20.4 1.6 %copy-done = f32[59,8192]{1,0:T(8,128)S(1)} copy-done((f32[59,8192]{1,0:T(8,128)S(1)}, f32[59,8192]{1,0:T(8,128)}, u32[]{:S(2)}) %copy-start) | copy-done | bytes 1933336
  22.0 0.0 copy-start.4
  22.0 0.7 copy-done.4
  22.6 2.3 %shard_map.65.feats_ref = f32[9,64,128]{2,1,0:T(8,128)S(1)} custom-call(f32[1,6]{1,0:T(1,128)S(1)} %copy-done.4, f32[59,8192]{1,0:T(8,128)S(1)} %copy-done), custom_call_target="tpu_custom_call" | custom-call | tf_op jit(solution)/shard_map/pallas_call | solution.py:520
  25.0 0.0 copy-start.1
  25.0 6.8 %all-to-all-done = s32[128,1,128]{2,1,0:T(1,128)S(1)} async-done(((s32[128,1,128]{2,1,0:T(1,128)}), s32[128,1,128]{2,1,0:T(1,128)S(1)}, u32[]{:S(2)}, u32[]{:S(2)}) %all-to-all-start) | async-done | bytes 65568 | tf_op jit(solution)/shard_map/all_to_all | solution.py:585
  31.8 2.7 %shard_map.66 = f32[256,128]{1,0:T(8,128)} custom-call(s32[128,128]{1,0:T(8,128)S(1)} %bitcast.11, f32[9,64,128]{2,1,0:T(8,128)S(1)} %shard_map.65.feats_ref), custom_call_target="tpu_custom_call" | custom-call | tf_op jit(solution)/shard_map/pallas_call | solution.py:499
  34.5 6.9 %all-to-all-start.1 = ((f32[128,2,128]{2,1,0:T(2,128)}), f32[128,2,128]{2,1,0:T(2,128)S(1)}, u32[]{:S(2)}, u32[]{:S(2)}) async-start(f32[128,2,128]{2,1,0:T(2,128)} %bitcast.4), calls=%async_computation.1 | async-start | bytes 262144 | tf_op jit(solution)/shard_map/all_to_all | solution.py:587
  41.4 12.2 %all-to-all-done.1 = f32[128,2,128]{2,1,0:T(2,128)S(1)} async-done(((f32[128,2,128]{2,1,0:T(2,128)}), f32[128,2,128]{2,1,0:T(2,128)S(1)}, u32[]{:S(2)}, u32[]{:S(2)}) %all-to-all-start.1) | async-done | bytes 131104 | tf_op jit(solution)/shard_map/all_to_all | solution.py:587
  53.6 0.0 copy-done.2
  53.6 0.0 copy-done.5
  53.6 0.0 copy-done.6
  53.6 0.0 copy-done.7
  53.6 4.3 %shard_map.67 = f32[256,128]{1,0:T(8,128)S(1)} custom-call(s32[1,4]{1,0:T(1,128)S(1)} %copy-done.6, f32[3]{0:T(128)S(1)} %copy-done.7, f32[1,6]{1,0:T(1,128)S(1)} %copy-done.5, s32[1]{0:T(128)} %bitcast.first_ref, f32[256,128]{1,0:T(8,128)S(1)} %bitcast.9, s32[48,128]{1,0:T(8,128)S(1)} %get-tuple-element.8.aux_ref, f32[1,3,4,256]{3,2,1,0:T(4,128)S(1)} %copy-done.2), custom_call_target="tpu_custom_call" | custom-call | tf_op jit(solution)/shard_map/pallas_call | solution.py:499
  58.0 18.1 %all_to_all.36 = f32[128,2,128]{2,1,0:T(2,128)S(1)} all-to-all(f32[128,2,128]{2,1,0:T(2,128)S(1)} %bitcast.10), channel_id=1, replica_groups=mesh['img'=128,'view'=4] {'img'}, dimensions={0} | all-to-all | bytes 262144 | tf_op jit(solution)/shard_map/all_to_all | solution.py:591
  76.2 12.3 %all_to_all.37.arrived_ref = f32[4,256,128]{2,1,0:T(8,128)S(1)} all-to-all(f32[4,256,128]{2,1,0:T(8,128)S(1)} %broadcast_in_dim.9), channel_id=1, replica_groups=mesh['img'=128,'view'=4] {'view'}, dimensions={0} | all-to-all | bytes 1048576 | tf_op jit(solution)/shard_map/all_to_all | solution.py:593
  88.5 0.0 copy-done.1
  88.5 16.9 %shard_map.68 = f32[59,8192]{1,0:T(8,128)} custom-call(f32[4,256,128]{2,1,0:T(8,128)S(1)} %all_to_all.37.arrived_ref, f32[59,8192]{1,0:T(8,128)S(1)} %copy-done.1), custom_call_target="tpu_custom_call" | custom-call | tf_op jit(solution)/shard_map/pallas_call | solution.py:558
  (1 shorter events, 0.0 us)
Async XLA Ops:
  0.0 53.6 %copy-start.2 = (f32[1,3,4,256]{3,2,1,0:T(4,128)S(1)}, f32[1,3,4,256]{3,2,1,0:T(4,128)}, u32[]{:S(2)}) copy-start(f32[1,3,4,256]{3,2,1,0:T(4,128)} %cotangent_ref.1) | copy-start | bytes 36868
  0.0 0.7 copy-start.3
  0.7 52.9 %copy-start.5 = (f32[1,6]{1,0:T(1,128)S(1)}, f32[1,6]{1,0:T(1,128)}, u32[]{:S(2)}) copy-start(f32[1,6]{1,0:T(1,128)} %camera_ref.3) | copy-start | bytes 76
  0.7 52.9 %copy-start.6 = (s32[1,4]{1,0:T(1,128)S(1)}, s32[1,4]{1,0:T(1,128)}, u32[]{:S(2)}) copy-start(s32[1,4]{1,0:T(1,128)} %lengths_ref.1) | copy-start | bytes 52
  0.7 52.9 %copy-start.7 = (f32[3]{0:T(128)S(1)}, f32[3]{0:T(128)}, u32[]{:S(2)}) copy-start(f32[3]{0:T(128)} %background_ref.1) | copy-start | bytes 40
  2.0 29.9 %all-to-all-start = ((s32[128,1,128]{2,1,0:T(1,128)}), s32[128,1,128]{2,1,0:T(1,128)S(1)}, u32[]{:S(2)}, u32[]{:S(2)}) async-start(s32[128,1,128]{2,1,0:T(1,128)} %bitcast.2), calls=%async_computation | async-start | bytes 131072 | tf_op jit(solution)/shard_map/all_to_all | solution.py:585
  20.4 1.6 %copy-start = (f32[59,8192]{1,0:T(8,128)S(1)}, f32[59,8192]{1,0:T(8,128)}, u32[]{:S(2)}) copy-start(f32[59,8192]{1,0:T(8,128)} %params_ref.3) | copy-start | bytes 5799940
  22.0 0.7 copy-start.4
  25.0 63.5 %copy-start.1 = (f32[59,8192]{1,0:T(8,128)S(1)}, f32[59,8192]{1,0:T(8,128)}, u32[]{:S(2)}) copy-start(f32[59,8192]{1,0:T(8,128)} %params_ref.3) | copy-start | bytes 5799940
  34.5 19.1 %all-to-all-start.1 = ((f32[128,2,128]{2,1,0:T(2,128)}), f32[128,2,128]{2,1,0:T(2,128)S(1)}, u32[]{:S(2)}, u32[]{:S(2)}) async-start(f32[128,2,128]{2,1,0:T(2,128)} %bitcast.4), calls=%async_computation.1 | async-start | bytes 262144 | tf_op jit(solution)/shard_map/all_to_all | solution.py:587

commit v2 on v1

--- a/solution.py
+++ b/solution.py
@@ -18,7 +18,7 @@
 G_DEV = 8192
 GROUPS = G_DEV // LANES
 PARAMS = 59
-PITCH = 64
+PITCH = 65
 CHUNKS = 8
 CHUNK = G_DEV // CHUNKS
 FEATS = 9
@@ -72,34 +72,42 @@
     return lax.dot_general(left, right, (((1,), (1,)), ((), ())), preferred_element_type=F32)
 
 
-def camera_rows(camera_ref):
+GEO = 24
+
+
+def write_geometry(geo_ref, camera_ref, first_ref, height):
     row = iota((8, LANES), 0)
     block = jnp.zeros((8, LANES), F32)
     for index in range(6):
         block = jnp.where(row == index, camera_ref[0, index], block)
-    return block
-
-
-def rotation(block):
     cosines, sines = jnp.cos(block), jnp.sin(block)
-
-    def take(values, index):
-        return spread(values[index : index + 1, :], (8, LANES))
-
-    cx, cy, cz = (take(cosines, index) for index in range(3))
-    sx, sy, sz = (take(sines, index) for index in range(3))
+    cx, cy, cz = (cosines[index : index + 1, :] for index in range(3))
+    sx, sy, sz = (sines[index : index + 1, :] for index in range(3))
     inner = [
         [cy, sy * sx, sy * cx],
         [None, cx, -sx],
         [-sy, cy * sx, cy * cx],
     ]
-    rotate = [
+    entries = [
         [cz * inner[0][0], cz * inner[0][1] - sz * inner[1][1], cz * inner[0][2] - sz * inner[1][2]],
         [sz * inner[0][0], sz * inner[0][1] + cz * inner[1][1], sz * inner[0][2] + cz * inner[1][2]],
         inner[2],
     ]
-    offset = [take(block, 3 + index) for index in range(3)]
-    return rotate, offset
+    for index, value in enumerate(entries[0] + entries[1] + entries[2]):
+        geo_ref[index : index + 1, :] = value
+    geo_ref[9:12, :] = block[3:6, :]
+    for index in range(TILES_DEV):
+        tile_id = first_ref[0] + index
+        tile_x = ((tile_id % TX * SIDE).astype(F32) + 0.5) * (2.0 / (TX * SIDE)) - 1.0
+        tile_y = ((tile_id // TX * SIDE).astype(F32) + 0.5) * (2.0 / (height * SIDE)) - 1.0
+        geo_ref[12 + index : 13 + index, :] = jnp.full((1, LANES), tile_x, F32)
+        geo_ref[16 + index : 17 + index, :] = jnp.full((1, LANES), tile_y, F32)
+    geo_ref[20:GEO, :] = jnp.zeros((GEO - 20, LANES), F32)
+
+
+def camera_of(geo):
+    entries = [spread(geo[index : index + 1, :], (8, LANES)) for index in range(12)]
+    return [entries[0:3], entries[3:6], entries[6:9]], entries[9:12]
 
 
 def camera_center(rotate, offset):
@@ -184,36 +192,57 @@
     return harmonics(toward[0] * norm, toward[1] * norm, toward[2] * norm)
 
 
-def spread_columns(params_ref, held_ref):
+def chunk_columns(chunk):
+    return pl.ds(pl.multiple_of(chunk * CHUNK, CHUNK), CHUNK)
+
+
+def spread_columns(params_ref, held_ref, chunk):
     for group in range(CHUNK // LANES):
-        columns = slice(group * LANES, (group + 1) * LANES)
-        held_ref[group * PITCH : group * PITCH + 56, :] = params_ref[0:56, columns]
-        held_ref[group * PITCH + 56 : group * PITCH + PARAMS, :] = params_ref[56:PARAMS, columns]
-
-
-def project_kernel(camera_ref, params_ref, feats_ref, held_ref):
-    spread_columns(params_ref, held_ref)
-
-    def param(index):
-        return held_ref[pl.ds(index, 8, stride=PITCH), :]
-
-    rotate, offset = rotation(camera_rows(camera_ref))
-    center = [param(index) for index in range(3)]
-    shape = shape_matrix([param(3 + index) for index in range(3)], [param(6 + index) for index in range(4)])
-    screen = screen_features(center, shape, rotate, offset)
-    basis = direction_basis(center, camera_center(rotate, offset))
-    opacity = 1.0 / (1.0 + jnp.exp(-param(10)))
-    colors = []
-    for channel in range(3):
-        total = basis[0] * param(11 + channel)
-        for term in range(1, 16):
-            total = total + basis[term] * param(11 + 3 * term + channel)
-        colors.append(total + 0.5)
-    for index, value in enumerate(screen + [opacity] + colors):
-        feats_ref[index] = value
-
-
-def route_kernel(lists_ref, request_ref, aux_ref):
+        columns = pl.ds(pl.multiple_of(chunk * CHUNK + group * LANES, LANES), LANES)
+        held_ref[group * PITCH : group * PITCH + PARAMS, :] = params_ref[:, columns]
+
+
+def project_kernel(params_ref, geo_ref, feats_ref, staged_ref, held_ref, semaphores):
+    def fetch(chunk):
+        columns = chunk_columns(chunk)
+        return pltpu.make_async_copy(params_ref.at[:, columns], staged_ref.at[:, columns], semaphores.at[chunk])
+
+    def start(chunk, carry):
+        fetch(chunk).start()
+        return carry
+
+    lax.fori_loop(0, CHUNKS, start, 0)
+    rotate, offset = camera_of(geo_ref[...])
+    eye = camera_center(rotate, offset)
+
+    def step(chunk, carry):
+        fetch(chunk).wait()
+        spread_columns(staged_ref, held_ref, chunk)
+
+        def param(index):
+            return held_ref[pl.ds(index, 8, stride=PITCH), :]
+
+        center = [param(index) for index in range(3)]
+        shape = shape_matrix([param(3 + index) for index in range(3)], [param(6 + index) for index in range(4)])
+        screen = screen_features(center, shape, rotate, offset)
+        basis = direction_basis(center, eye)
+        opacity = 1.0 / (1.0 + jnp.exp(-param(10)))
+        colors = []
+        for channel in range(3):
+            total = basis[0] * param(11 + channel)
+            for term in range(1, 16):
+                total = total + basis[term] * param(11 + 3 * term + channel)
+            colors.append(total + 0.5)
+        rows = pl.ds(pl.multiple_of(chunk * 8, 8), 8)
+        for index, value in enumerate(screen + [opacity] + colors):
+            feats_ref[index, rows, :] = value
+        return carry
+
+    lax.fori_loop(0, CHUNKS, step, 0)
+
+
+def route_kernel(height, camera_ref, first_ref, lists_ref, request_ref, aux_ref, geo_ref):
+    write_geometry(geo_ref, camera_ref, first_ref, height)
     owner_iota = iota((OWNERS, LANES), 0)
     before = (iota((LANES, 2 * LANES), 0) < iota((LANES, 2 * LANES), 1)).astype(F32)
     before = before.astype(BF16)
@@ -250,8 +279,23 @@
     request_ref[...] = padded.T.astype(jnp.int32)
 
 
+LANE_GATHER = lax.GatherDimensionNumbers(
+    offset_dims=(),
+    collapsed_slice_dims=(1,),
+    start_index_map=(1,),
+    operand_batching_dims=(0,),
+    start_indices_batching_dims=(0,),
+)
+
+
 def pick(row, lanes_at):
-    return jnp.take_along_axis(spread(row, (8, LANES)), lanes_at, axis=1, mode="promise_in_bounds")
+    return lax.gather(
+        spread(row, (8, LANES)),
+        lanes_at[:, :, None],
+        LANE_GATHER,
+        slice_sizes=(1, 1),
+        mode=lax.GatherScatterMode.PROMISE_IN_BOUNDS,
+    )
 
 
 def store_rows(out_ref, table):
@@ -283,7 +327,7 @@
 
 
 def render_kernel(
-    height, lengths_ref, background_ref, camera_ref, first_ref, arrived_ref, aux_ref, cotangent_ref, out_ref,
+    height, lengths_ref, background_ref, geo_ref, arrived_ref, aux_ref, cotangent_ref, out_ref,
     slot_ref, table_ref, grad_ref, pixel_ref, weight_ref,
 ):
     table_ref[:LANES, :] = arrived_ref[pl.ds(0, LANES, stride=2), :].T
@@ -312,11 +356,9 @@
                 [slot_ref[pl.ds(feature * 8 + 2 * index + half, 1), :] for half in range(2)], axis=1
             )
 
-        tile_id = first_ref[0] + index
-        tile_x = ((tile_id % TX * SIDE).astype(F32) + 0.5) * (2.0 / (TX * SIDE)) - 1.0
-        tile_y = ((tile_id // TX * SIDE).astype(F32) + 0.5) * (2.0 / (height * SIDE)) - 1.0
-        at_x = slots(0) - tile_x
-        at_y = slots(1) - tile_y
+        tile_x, tile_y = geo_ref[pl.ds(12 + index, 1), :], geo_ref[pl.ds(16 + index, 1), :]
+        at_x = slots(0) - jnp.concatenate([tile_x] * 2, axis=1)
+        at_y = slots(1) - jnp.concatenate([tile_y] * 2, axis=1)
         conic_a, conic_b, conic_c = slots(2), slots(3), slots(4)
         opacity = slots(5)
         live_opacity = jnp.where(slot_place < lengths_ref[0, index], opacity, 0.0)
@@ -387,7 +429,7 @@
                 grads = grad_ref[feature * 8 + row : feature * 8 + row + 1, :]
                 value = jnp.where(at_row == row, pick(grads, at_lane), value)
             blocks.append(value)
-    blocks += [wanted, camera_rows(camera_ref), jnp.zeros((PACK - FEATS * CAP - CAP - 8, LANES), F32)]
+    blocks += [wanted, geo_ref[0:16, :], jnp.zeros((PACK - FEATS * CAP - CAP - 16, LANES), F32)]
     store_rows(out_ref, jnp.concatenate(blocks, axis=0))
 
 
@@ -403,7 +445,7 @@
     rest = FEATS * CAP - LANES
     values = jnp.concatenate([first, second[:rest]], axis=0)
     wanted = second[rest : rest + CAP].astype(jnp.int32)
-    camera_ref[view] = second[rest + CAP : rest + CAP + 8]
+    camera_ref[view] = second[rest + CAP : rest + CAP + 16]
     high_place, low_place = wanted >> 8, wanted & (WIDE - 1)
     high, low = halves(values)
     high, low = high.astype(F32), low.astype(F32)
@@ -422,19 +464,20 @@
         grads_ref[view, pl.ds(half, FEATS * TALL, stride=2), :] = total[:, half * LANES : (half + 1) * LANES]
 
 
-def pullback_kernel(arrived_ref, params_ref, out_ref, held_ref, sums_ref, grads_ref, camera_ref):
+def pullback_kernel(
+    arrived_ref, params_ref, out_ref, held_ref, sums_ref, grads_ref, camera_ref, staged_ref, semaphores
+):
     views = arrived_ref.shape[0]
-    chunk = pl.program_id(0)
-
-    @pl.when(chunk == 0)
-    def scatter():
-        def one_view(view, carry):
-            scatter_view(view, arrived_ref, grads_ref, camera_ref)
-            return carry
-
-        lax.fori_loop(0, views, one_view, 0)
-
-    spread_columns(params_ref, held_ref)
+
+    def one_view(view, carry):
+        scatter_view(view, arrived_ref, grads_ref, camera_ref)
+        return carry
+
+    lax.fori_loop(0, views, one_view, 0)
+
+    def send(chunk):
+        columns = chunk_columns(chunk)
+        return pltpu.make_async_copy(staged_ref.at[:, columns], out_ref.at[:, columns], semaphores.at[chunk])
 
     def param(index):
         return held_ref[pl.ds(index, 8, stride=PITCH), :]
@@ -445,51 +488,62 @@
     def kept(index):
         return sums_ref[pl.ds(index, 8, stride=PITCH), :]
 
-    center = [param(index) for index in range(3)]
-    shape, shape_back = jax.vjp(
-        shape_matrix, [param(3 + index) for index in range(3)], [param(6 + index) for index in range(4)]
-    )
-    center_grad, shape_grad, opacity_grad = None, None, None
-    for view in range(views):
-        def cotangent(feature):
-            return grads_ref[view, pl.ds(pl.multiple_of(feature * GROUPS + chunk * 8, 8), 8), :]
-
-        rotate, offset = rotation(camera_ref[view])
-        eye = camera_center(rotate, offset)
-        basis, basis_back = jax.vjp(lambda place: direction_basis(place, eye), center)
-        colors = [cotangent(6 + channel) for channel in range(3)]
-        basis_grad = []
-        for term in range(16):
-            total = None
-            for channel in range(3):
-                index = 11 + 3 * term + channel
-                piece = basis[term] * colors[channel]
-                keep(index, piece if view == 0 else kept(index) + piece)
-                piece = param(index) * colors[channel]
-                total = piece if total is None else total + piece
-            basis_grad.append(total)
-        (along,) = basis_back(basis_grad)
-        unused, screen_back = jax.vjp(
-            lambda place, matrix: screen_features(place, matrix, rotate, offset), center, shape
+    def step(chunk, carry):
+        spread_columns(params_ref, held_ref, chunk)
+        center = [param(index) for index in range(3)]
+        shape, shape_back = jax.vjp(
+            shape_matrix, [param(3 + index) for index in range(3)], [param(6 + index) for index in range(4)]
         )
-        moved, bent = screen_back([cotangent(index) for index in range(5)])
-        pieces = [along[axis] + moved[axis] for axis in range(3)]
-        faded = cotangent(5)
-        if view == 0:
-            center_grad, shape_grad, opacity_grad = pieces, bent, faded
-        else:
-            center_grad = [one + other for one, other in zip(center_grad, pieces)]
-            shape_grad = [[one + other for one, other in zip(*rows)] for rows in zip(shape_grad, bent)]
-            opacity_grad = opacity_grad + faded
-    scale_grad, quaternion_grad = shape_back(shape_grad)
-    opacity = 1.0 / (1.0 + jnp.exp(-param(10)))
-    firsts = center_grad + list(scale_grad) + list(quaternion_grad) + [opacity * (1.0 - opacity) * opacity_grad]
-    for index, value in enumerate(firsts):
-        keep(index, value)
-    for group in range(CHUNK // LANES):
-        columns = slice(group * LANES, (group + 1) * LANES)
-        out_ref[0:56, columns] = sums_ref[group * PITCH : group * PITCH + 56, :]
-        out_ref[56:PARAMS, columns] = sums_ref[group * PITCH + 56 : group * PITCH + PARAMS, :]
+        center_grad, shape_grad, opacity_grad = None, None, None
+        for view in range(views):
+            def cotangent(feature):
+                return grads_ref[view, pl.ds(pl.multiple_of(feature * GROUPS + chunk * 8, 8), 8), :]
+
+            rotate, offset = camera_of(camera_ref[view])
+            eye = camera_center(rotate, offset)
+            basis, basis_back = jax.vjp(lambda place: direction_basis(place, eye), center)
+            colors = [cotangent(6 + channel) for channel in range(3)]
+            basis_grad = []
+            for term in range(16):
+                total = None
+                for channel in range(3):
+                    index = 11 + 3 * term + channel
+                    piece = basis[term] * colors[channel]
+                    keep(index, piece if view == 0 else kept(index) + piece)
+                    piece = param(index) * colors[channel]
+                    total = piece if total is None else total + piece
+                basis_grad.append(total)
+            (along,) = basis_back(basis_grad)
+            unused, screen_back = jax.vjp(
+                lambda place, matrix: screen_features(place, matrix, rotate, offset), center, shape
+            )
+            moved, bent = screen_back([cotangent(index) for index in range(5)])
+            pieces = [along[axis] + moved[axis] for axis in range(3)]
+            faded = cotangent(5)
+            if view == 0:
+                center_grad, shape_grad, opacity_grad = pieces, bent, faded
+            else:
+                center_grad = [one + other for one, other in zip(center_grad, pieces)]
+                shape_grad = [[one + other for one, other in zip(*rows)] for rows in zip(shape_grad, bent)]
+                opacity_grad = opacity_grad + faded
+        scale_grad, quaternion_grad = shape_back(shape_grad)
+        opacity = 1.0 / (1.0 + jnp.exp(-param(10)))
+        firsts = center_grad + list(scale_grad) + list(quaternion_grad) + [opacity * (1.0 - opacity) * opacity_grad]
+        for index, value in enumerate(firsts):
+            keep(index, value)
+        for group in range(CHUNK // LANES):
+            columns = pl.ds(pl.multiple_of(chunk * CHUNK + group * LANES, LANES), LANES)
+            staged_ref[:, columns] = sums_ref[group * PITCH : group * PITCH + PARAMS, :]
+        send(chunk).start()
+        return carry
+
+    lax.fori_loop(0, CHUNKS, step, 0)
+
+    def finish(chunk, carry):
+        send(chunk).wait()
+        return carry
+
+    lax.fori_loop(0, CHUNKS, finish, 0)
 
 
 def call(kernel, out_shape, operands, smalls=(), scratch=(), **kwargs):
@@ -507,28 +561,32 @@
     )(*operands)
 
 
-def route(tile_lists):
+def route(height, camera, first_tile, tile_lists):
     return call(
-        route_kernel,
-        [jax.ShapeDtypeStruct((OWNERS, LANES), jnp.int32), jax.ShapeDtypeStruct((16 + 2 * CAP, LANES), jnp.int32)],
-        [tile_lists],
-        smalls=0,
+        functools.partial(route_kernel, height),
+        [
+            jax.ShapeDtypeStruct((OWNERS, LANES), jnp.int32),
+            jax.ShapeDtypeStruct((16 + 2 * CAP, LANES), jnp.int32),
+            jax.ShapeDtypeStruct((GEO, LANES), F32),
+        ],
+        [camera, first_tile, tile_lists],
+        smalls=2,
     )
 
 
-def project(camera, gauss_params):
+def project(gauss_params, geometry):
     return pl.pallas_call(
         project_kernel,
-        grid=(CHUNKS,),
         out_shape=jax.ShapeDtypeStruct((FEATS, GROUPS, LANES), F32),
-        in_specs=[
-            pl.BlockSpec(memory_space=pltpu.SMEM),
-            pl.BlockSpec((PARAMS, CHUNK), lambda chunk: (0, chunk)),
+        in_specs=[pl.BlockSpec(memory_space=pltpu.HBM), pl.BlockSpec(memory_space=pltpu.VMEM)],
+        out_specs=pl.BlockSpec(memory_space=pltpu.VMEM),
+        scratch_shapes=[
+            pltpu.VMEM((PARAMS, G_DEV), F32),
+            pltpu.VMEM((8 * PITCH, LANES), F32),
+            pltpu.SemaphoreType.DMA((CHUNKS,)),
         ],
-        out_specs=pl.BlockSpec((FEATS, 8, LANES), lambda chunk: (0, chunk, 0)),
-        scratch_shapes=[pltpu.VMEM((8 * PITCH, LANES), F32)],
         compiler_params=pltpu.CompilerParams(vmem_limit_bytes=VMEM_LIMIT),
-    )(camera, gauss_params)
+    )(gauss_params, geometry)
 
 
 def gather(requested, features):
@@ -537,12 +595,12 @@
     )
 
 
-def render(height, tile_lengths, background, camera, first_tile, arrived, aux, cotangent):
+def render(height, tile_lengths, background, geometry, arrived, aux, cotangent):
     return call(
         functools.partial(render_kernel, height),
         jax.ShapeDtypeStruct((2 * OWNERS, LANES), F32),
-        [tile_lengths, background, camera, first_tile, arrived, aux, cotangent],
-        smalls=4,
+        [tile_lengths, background, geometry, arrived, aux, cotangent],
+        smalls=2,
         scratch=[
             pltpu.VMEM((FEATS * 8, LANES), F32),
             pltpu.VMEM((2 * OWNERS, LANES), F32),
@@ -557,18 +615,16 @@
     views = arrived.shape[0]
     return pl.pallas_call(
         pullback_kernel,
-        grid=(CHUNKS,),
         out_shape=jax.ShapeDtypeStruct((PARAMS, G_DEV), F32),
-        in_specs=[
-            pl.BlockSpec((views, 2 * OWNERS, LANES), lambda chunk: (0, 0, 0)),
-            pl.BlockSpec((PARAMS, CHUNK), lambda chunk: (0, chunk)),
-        ],
-        out_specs=pl.BlockSpec((PARAMS, CHUNK), lambda chunk: (0, chunk)),
+        in_specs=[pl.BlockSpec(memory_space=pltpu.VMEM)] * 2,
+        out_specs=pl.BlockSpec(memory_space=pltpu.HBM),
         scratch_shapes=[
             pltpu.VMEM((8 * PITCH, LANES), F32),
             pltpu.VMEM((8 * PITCH, LANES), F32),
             pltpu.VMEM((views, FEATS * GROUPS, LANES), F32),
-            pltpu.VMEM((views, 8, LANES), F32),
+            pltpu.VMEM((views, 16, LANES), F32),
+            pltpu.VMEM((PARAMS, G_DEV), F32),
+            pltpu.SemaphoreType.DMA((CHUNKS,)),
         ],
         compiler_params=pltpu.CompilerParams(vmem_limit_bytes=VMEM_LIMIT),
     )(arrived, gauss_params)
@@ -580,14 +636,12 @@
     tiles_here = tile_lists.shape[1]
     height = tiles_here * owners_total // TX
     first_tile = (lax.axis_index("img") * tiles_here).astype(jnp.int32).reshape(1)
-    requests, aux = route(tile_lists)
-    features = project(camera, gauss_params)
+    requests, aux, geometry = route(height, camera, first_tile, tile_lists)
+    features = project(gauss_params, geometry)
     requested = lax.all_to_all(requests, "img", split_axis=0, concat_axis=0, tiled=True)
     outgoing = gather(requested, features)
     arrived = lax.all_to_all(outgoing, "img", split_axis=0, concat_axis=0, tiled=True)
-    slot_grads = render(
-        height, tile_lengths, background, camera, first_tile, arrived, aux, pixel_cotangent
-    )
+    slot_grads = render(height, tile_lengths, background, geometry, arrived, aux, pixel_cotangent)
     returned = lax.all_to_all(slot_grads, "img", split_axis=0, concat_axis=0, tiled=True)
     copies = jnp.broadcast_to(returned[None], (views,) + returned.shape)
     everyone = lax.all_to_all(copies, "view", split_axis=0, concat_axis=0, tiled=True)

time: 106 us -> 95.6 us (0.902)
  blocking collectives: 30.4 us -> 47.8 us
  Pallas kernels: 27.5 us -> 17.2 us
  waiting for transfers between devices: 19 us -> 8.83 us
  starting transfers between devices: 25.3 us -> 18.4 us
    all_to_all x0 -> x1, blocking collectives: none -> 17.7 us  [per_device(): lax.all_to_all(outgoing, 'img', split_axis=0, concat_axis=0, tiled=True)]
    all_to_all x1 -> x0, waiting for transfers between devices: 12.2 us -> none  [per_device(): lax.all_to_all(outgoing, 'img', split_axis=0, concat_axis=0, tiled=True)]
    pallas_call x2, Pallas kernels: 19.3 us -> 9.11 us  [the longest x1 8.11 us: pullback(): pl.pallas_call(pullback_kernel, out_shape=jax.ShapeDtypeStruct((PARAMS, G...]
    all_to_all x1 -> x0, starting transfers between devices: 6.9 us -> none  [per_device(): lax.all_to_all(outgoing, 'img', split_axis=0, concat_axis=0, tiled=True)]
    all_to_all x1, waiting for transfers between devices: 6.84 us -> 8.83 us  [per_device(): lax.all_to_all(requests, 'img', split_axis=0, concat_axis=0, tiled=True)]
    unnamed x16 -> x14, local copies, waits for them, and re-layouts: 2.96 us -> 2.96 us
  transfers between devices with their start and end apart: 2 -> 1, of which waited for: 2 -> 1; matrix products, arithmetic and copies ran while one was open for 0% -> 0% of each run, Pallas kernels for 2% -> 1%
where the time goes in v2:
time: 95.6 us; the launch traced here: 95.3 us
  blocking collectives  47.8 us (50%)
  starting transfers between devices  18.4 us (19%)
  Pallas kernels  17.2 us (18%)
  waiting for transfers between devices  8.83 us (9%)
  local copies, waits for them, and re-layouts  2.99 us (3%)
    all_to_all x1, starting transfers between devices, per_device(): lax.all_to_all(requests, 'img', split_axis=0, concat_axis=0, tiled=True)  18.4 us
    all_to_all x1, blocking collectives, per_device(): lax.all_to_all(slot_grads, 'img', split_axis=0, concat_axis=0, tiled=True)  17.8 us
    all_to_all x1, blocking collectives, per_device(): lax.all_to_all(outgoing, 'img', split_axis=0, concat_axis=0, tiled=True)  17.7 us
    all_to_all x1, blocking collectives, per_device(): lax.all_to_all(copies, 'view', split_axis=0, concat_axis=0, tiled=True)  12.3 us
    all_to_all x1, waiting for transfers between devices, per_device(): lax.all_to_all(requests, 'img', split_axis=0, concat_axis=0, tiled=True)  8.83 us
    pallas_call x1, Pallas kernels, pullback(): pl.pallas_call(pullback_kernel, out_shape=jax.ShapeDtypeStruct((PARAMS, G...  8.11 us
    pallas_call x3, Pallas kernels, call(): pl.pallas_call(kernel, out_shape=out_shape, in_specs=[pl.BlockSpec(memory...  8.05 us
    unnamed x14, local copies, waits for them, and re-layouts  2.96 us
  transfers between devices with their start and end apart: 1, of which 1 were waited for; matrix products, arithmetic and copies ran while one was open for 0% of the time, Pallas kernels for 1%

profile of v2, /device:TPU:1, one launch (start us, length us, event | category | flops | bytes accessed | tf_op | source)
XLA Modules:
  0.0 95.3 jit_solution(17635099003099448626)
XLA Ops:
  0.0 0.0 copy-start.2
  0.0 0.0 copy-start.3
  0.0 0.7 copy-done.3
  0.7 0.0 copy-start.6
  0.7 0.7 copy-done.6
  1.4 0.0 copy-start.4
  1.4 0.0 copy-start.5
  1.4 1.8 %shard_map.64 = (s32[128,128]{1,0:T(8,128)}, s32[48,128]{1,0:T(8,128)S(1)}, f32[24,128]{1,0:T(8,128)S(1)}) custom-call(f32[1,6]{1,0:T(1,128)S(1)} %copy-done.6, s32[1]{0:T(128)} %bitcast.first_ref, s32[1,4,256]{2,1,0:T(4,128)S(1)} %copy-done.3), custom_call_target="tpu_custom_call" | custom-call | tf_op jit(solution)/shard_map/pallas_call | solution.py:553
  3.2 18.4 %all-to-all-start = ((s32[128,1,128]{2,1,0:T(1,128)}), s32[128,1,128]{2,1,0:T(1,128)S(1)}, u32[]{:S(2)}, u32[]{:S(2)}) async-start(s32[128,1,128]{2,1,0:T(1,128)} %bitcast.2), calls=%async_computation | async-start | bytes 131072 | tf_op jit(solution)/shard_map/all_to_all | solution.py:641
  21.6 0.0 copy-start
  21.6 1.6 %copy-done = f32[59,8192]{1,0:T(8,128)S(1)} copy-done((f32[59,8192]{1,0:T(8,128)S(1)}, f32[59,8192]{1,0:T(8,128)}, u32[]{:S(2)}) %copy-start) | copy-done | bytes 1933336
  23.2 1.0 %shard_map.65.feats_ref = f32[9,64,128]{2,1,0:T(8,128)S(1)} custom-call(f32[59,8192]{1,0:T(8,128)S(1)} %copy-done, f32[24,128]{1,0:T(8,128)S(1)} %get-tuple-element.8.geo_ref), custom_call_target="tpu_custom_call" | custom-call | tf_op jit(solution)/shard_map/pallas_call | solution.py:578
  24.2 0.0 copy-start.1
  24.2 8.8 %all-to-all-done = s32[128,1,128]{2,1,0:T(1,128)S(1)} async-done(((s32[128,1,128]{2,1,0:T(1,128)}), s32[128,1,128]{2,1,0:T(1,128)S(1)}, u32[]{:S(2)}, u32[]{:S(2)}) %all-to-all-start) | async-done | bytes 65568 | tf_op jit(solution)/shard_map/all_to_all | solution.py:641
  33.0 2.0 %shard_map.66 = f32[256,128]{1,0:T(8,128)S(1)} custom-call(s32[128,128]{1,0:T(8,128)S(1)} %bitcast.12, f32[9,64,128]{2,1,0:T(8,128)S(1)} %shard_map.65.feats_ref), custom_call_target="tpu_custom_call" | custom-call | tf_op jit(solution)/shard_map/pallas_call | solution.py:553
  35.0 17.7 %all_to_all.36 = f32[128,2,128]{2,1,0:T(2,128)S(1)} all-to-all(f32[128,2,128]{2,1,0:T(2,128)S(1)} %bitcast.11), channel_id=1, replica_groups=mesh['img'=128,'view'=4] {'img'}, dimensions={0} | all-to-all | bytes 262144 | tf_op jit(solution)/shard_map/all_to_all | solution.py:643
  52.7 0.0 copy-done.2
  52.7 0.0 copy-done.4
  52.7 0.0 copy-done.5
  52.7 4.3 %shard_map.67 = f32[256,128]{1,0:T(8,128)S(1)} custom-call(s32[1,4]{1,0:T(1,128)S(1)} %copy-done.4, f32[3]{0:T(128)S(1)} %copy-done.5, f32[24,128]{1,0:T(8,128)S(1)} %get-tuple-element.8.geo_ref, f32[256,128]{1,0:T(8,128)S(1)} %bitcast.9, s32[48,128]{1,0:T(8,128)S(1)} %get-tuple-element.10.aux_ref, f32[1,3,4,256]{3,2,1,0:T(4,128)S(1)} %copy-done.2), custom_call_target="tpu_custom_call" | custom-call | tf_op jit(solution)/shard_map/pallas_call | solution.py:553
  57.0 17.8 %all_to_all.37 = f32[128,2,128]{2,1,0:T(2,128)S(1)} all-to-all(f32[128,2,128]{2,1,0:T(2,128)S(1)} %bitcast.10), channel_id=1, replica_groups=mesh['img'=128,'view'=4] {'img'}, dimensions={0} | all-to-all | bytes 262144 | tf_op jit(solution)/shard_map/all_to_all | solution.py:645
  74.9 12.3 %all_to_all.38.arrived_ref = f32[4,256,128]{2,1,0:T(8,128)S(1)} all-to-all(f32[4,256,128]{2,1,0:T(8,128)S(1)} %broadcast_in_dim.9), channel_id=1, replica_groups=mesh['img'=128,'view'=4] {'view'}, dimensions={0} | all-to-all | bytes 1048576 | tf_op jit(solution)/shard_map/all_to_all | solution.py:647
  87.2 0.0 copy-done.1
  87.2 8.1 %shard_map.68 = f32[59,8192]{1,0:T(8,128)} custom-call(f32[4,256,128]{2,1,0:T(8,128)S(1)} %all_to_all.38.arrived_ref, f32[59,8192]{1,0:T(8,128)S(1)} %copy-done.1), custom_call_target="tpu_custom_call" | custom-call | tf_op jit(solution)/shard_map/pallas_call | solution.py:616
  (1 shorter events, 0.0 us)
Async XLA Ops:
  0.0 52.7 %copy-start.2 = (f32[1,3,4,256]{3,2,1,0:T(4,128)S(1)}, f32[1,3,4,256]{3,2,1,0:T(4,128)}, u32[]{:S(2)}) copy-start(f32[1,3,4,256]{3,2,1,0:T(4,128)} %cotangent_ref.1) | copy-start | bytes 36868
  0.0 0.7 copy-start.3
  0.7 0.7 copy-start.6
  1.4 51.4 %copy-start.4 = (s32[1,4]{1,0:T(1,128)S(1)}, s32[1,4]{1,0:T(1,128)}, u32[]{:S(2)}) copy-start(s32[1,4]{1,0:T(1,128)} %lengths_ref.1) | copy-start | bytes 52
  1.4 51.4 %copy-start.5 = (f32[3]{0:T(128)S(1)}, f32[3]{0:T(128)}, u32[]{:S(2)}) copy-start(f32[3]{0:T(128)} %background_ref.1) | copy-start | bytes 40
  3.2 29.9 %all-to-all-start = ((s32[128,1,128]{2,1,0:T(1,128)}), s32[128,1,128]{2,1,0:T(1,128)S(1)}, u32[]{:S(2)}, u32[]{:S(2)}) async-start(s32[128,1,128]{2,1,0:T(1,128)} %bitcast.2), calls=%async_computation | async-start | bytes 131072 | tf_op jit(solution)/shard_map/all_to_all | solution.py:641
  21.6 1.6 %copy-start = (f32[59,8192]{1,0:T(8,128)S(1)}, f32[59,8192]{1,0:T(8,128)}, u32[]{:S(2)}) copy-start(f32[59,8192]{1,0:T(8,128)} %params_ref.3) | copy-start | bytes 5799940
  24.2 63.0 %copy-start.1 = (f32[59,8192]{1,0:T(8,128)S(1)}, f32[59,8192]{1,0:T(8,128)}, u32[]{:S(2)}) copy-start(f32[59,8192]{1,0:T(8,128)} %params_ref.3) | copy-start | bytes 5799940

commit v3 on v2

--- a/solution.py
+++ b/solution.py
@@ -45,6 +45,7 @@
     -0.5900435899266435,
 )
 
+LOG2_E = 1.4426950408889634
 F32 = jnp.float32
 BF16 = jnp.bfloat16
 VMEM_LIMIT = 32 * 1024 * 1024
@@ -75,7 +76,7 @@
 GEO = 24
 
 
-def write_geometry(geo_ref, camera_ref, first_ref, height):
+def write_geometry(height, camera_ref, first_ref, geo_ref):
     row = iota((8, LANES), 0)
     block = jnp.zeros((8, LANES), F32)
     for index in range(6):
@@ -199,10 +200,10 @@
 def spread_columns(params_ref, held_ref, chunk):
     for group in range(CHUNK // LANES):
         columns = pl.ds(pl.multiple_of(chunk * CHUNK + group * LANES, LANES), LANES)
-        held_ref[group * PITCH : group * PITCH + PARAMS, :] = params_ref[:, columns]
-
-
-def project_kernel(params_ref, geo_ref, feats_ref, staged_ref, held_ref, semaphores):
+        held_ref[chunk, group * PITCH : group * PITCH + PARAMS, :] = params_ref[:, columns]
+
+
+def project_kernel(height, camera_ref, first_ref, view_ref, params_ref, feats_ref, held_ref, geo_ref, staged_ref, semaphores):
     def fetch(chunk):
         columns = chunk_columns(chunk)
         return pltpu.make_async_copy(params_ref.at[:, columns], staged_ref.at[:, columns], semaphores.at[chunk])
@@ -212,6 +213,8 @@
         return carry
 
     lax.fori_loop(0, CHUNKS, start, 0)
+    write_geometry(height, camera_ref, first_ref, geo_ref)
+    geo_ref[20:21, :] = jnp.full((1, LANES), view_ref[0].astype(F32), F32)
     rotate, offset = camera_of(geo_ref[...])
     eye = camera_center(rotate, offset)
 
@@ -220,7 +223,7 @@
         spread_columns(staged_ref, held_ref, chunk)
 
         def param(index):
-            return held_ref[pl.ds(index, 8, stride=PITCH), :]
+            return held_ref[chunk, pl.ds(index, 8, stride=PITCH), :]
 
         center = [param(index) for index in range(3)]
         shape = shape_matrix([param(3 + index) for index in range(3)], [param(6 + index) for index in range(4)])
@@ -241,8 +244,7 @@
     lax.fori_loop(0, CHUNKS, step, 0)
 
 
-def route_kernel(height, camera_ref, first_ref, lists_ref, request_ref, aux_ref, geo_ref):
-    write_geometry(geo_ref, camera_ref, first_ref, height)
+def route_kernel(lists_ref, request_ref, aux_ref):
     owner_iota = iota((OWNERS, LANES), 0)
     before = (iota((LANES, 2 * LANES), 0) < iota((LANES, 2 * LANES), 1)).astype(F32)
     before = before.astype(BF16)
@@ -318,12 +320,12 @@
         return tuple(found)
 
     start = tuple(jnp.zeros((8, LANES), F32) for _ in range(2 * FEATS))
-    found = lax.fori_loop(0, GROUPS, step, start, unroll=8)
+    found = lax.fori_loop(0, GROUPS, step, start, unroll=16)
     table = jnp.concatenate(list(found) + [jnp.zeros((PACK - FEATS * CAP, LANES), F32)], axis=0)
     store_rows(out_ref, table)
 
 
-PIX_CHUNK = 64
+PIX_CHUNK = 128
 
 
 def render_kernel(
@@ -349,7 +351,6 @@
     weight_ref[0] = (slot_row < slot_col).astype(F32).astype(BF16)
     weight_ref[1] = (slot_row > slot_col).astype(F32).astype(BF16)
     slot_place = iota((1, SLOTS), 1)
-
     def tile(index, carry):
         def slots(feature):
             return jnp.concatenate(
@@ -363,46 +364,44 @@
         opacity = slots(5)
         live_opacity = jnp.where(slot_place < lengths_ref[0, index], opacity, 0.0)
         colors = [slots(6 + channel) for channel in range(3)]
-        half_a, full_b, half_c = -0.5 * conic_a, -conic_b, -0.5 * conic_c
+        scaled_a, scaled_b, scaled_c = (-0.5 * LOG2_E) * conic_a, -LOG2_E * conic_b, (-0.5 * LOG2_E) * conic_c
         shades = [cotangent_ref[0, channel, pl.ds(index, 1), :] for channel in range(3)]
         behind = (
             shades[0] * background_ref[0] + shades[1] * background_ref[1] + shades[2] * background_ref[2]
         )
         columns = jnp.concatenate(shades + [behind, jnp.zeros((4, PIX), F32)], axis=0).T
 
-        sums = [jnp.zeros((8, SLOTS), F32) for _ in range(9)]
-
         def fold(values):
             return jnp.sum(values.reshape(PIX_CHUNK // 8, 8, SLOTS), axis=0)
 
+        sums = [jnp.zeros((8, SLOTS), F32) for _ in range(9)]
         for chunk in range(PIX // PIX_CHUNK):
             rows = slice(chunk * PIX_CHUNK, (chunk + 1) * PIX_CHUNK)
             shape = (PIX_CHUNK, SLOTS)
             delta_x = pixel_ref[0, rows, :] - at_x
             delta_y = pixel_ref[1, rows, :] - at_y
-            exponent = (half_a * delta_x + full_b * delta_y) * delta_x + half_c * delta_y * delta_y
-            coverage = live_opacity * jnp.exp(exponent)
-            log_pass = jnp.log(1.0 - coverage)
+            exponent = (scaled_a * delta_x + scaled_b * delta_y) * delta_x + scaled_c * delta_y * delta_y
+            coverage = live_opacity * jnp.exp2(exponent)
+            log_pass = jnp.log2(1.0 - coverage)
             high, low = halves(log_pass)
             prefix = dot(high, weight_ref[0]) + dot(low, weight_ref[0])
-            passed = jnp.exp(prefix)
-            weight = coverage * passed
+            weight = coverage * jnp.exp2(prefix)
             shade = [spread(columns[rows, channel : channel + 1], shape) for channel in range(3)]
             gain = shade[0] * colors[0] + shade[1] * colors[1] + shade[2] * colors[2]
             product = weight * gain
             high, low = halves(product)
             later = dot(high, weight_ref[1]) + dot(low, weight_ref[1])
-            remain = jnp.exp(prefix[:, SLOTS - 1 :] + log_pass[:, SLOTS - 1 :])
+            remain = jnp.exp2(prefix[:, SLOTS - 1 :] + log_pass[:, SLOTS - 1 :])
             later = later + spread(columns[rows, 3:4] * remain, shape)
-            slope = -0.5 * (product - coverage / (1.0 - coverage) * later)
+            slope = product - coverage * jnp.exp2(-log_pass) * later
             slope_x = slope * delta_x
             slope_y = slope * delta_y
             parts = [slope, slope_x, slope_y, slope_x * delta_x, slope_x * delta_y, slope_y * delta_y]
-            parts += [shade[channel] * weight for channel in range(3)]
+            parts += [part * weight for part in shade]
             sums = [total + fold(part) for total, part in zip(sums, parts)]
 
-        sums = [jnp.sum(total, axis=0, keepdims=True) for total in sums]
-        total, sum_x, sum_y, sum_xx, sum_xy, sum_yy = sums[:6]
+        sums = [jnp.sum(part, axis=0, keepdims=True) for part in sums]
+        total, sum_x, sum_y, sum_xx, sum_xy, sum_yy = (part * -0.5 for part in sums[:6])
         grads = [
             -2.0 * (conic_a * sum_x + conic_b * sum_y),
             -2.0 * (conic_b * sum_x + conic_c * sum_y),
@@ -416,7 +415,7 @@
                 grad_ref[pl.ds(feature * 8 + 2 * index + half, 1), :] = value[:, half * LANES : (half + 1) * LANES]
         return carry
 
-    lax.fori_loop(0, TILES_DEV, tile, 0)
+    lax.fori_loop(0, TILES_DEV, tile, 0, unroll=TILES_DEV)
 
     slot = aux_ref[16 : 16 + CAP, :]
     wanted = aux_ref[16 + CAP : 16 + 2 * CAP, :].astype(F32)
@@ -437,7 +436,7 @@
 TALL = G_DEV // WIDE
 
 
-def scatter_view(view, arrived_ref, grads_ref, camera_ref):
+def scatter_view(view, arrived_ref, place, grads_ref, camera_ref):
     tall_iota = iota((TALL, LANES), 0)
     wide_iota = iota((WIDE, LANES), 0)
     first = arrived_ref[view, pl.ds(0, LANES, stride=2), :].T
@@ -445,92 +444,124 @@
     rest = FEATS * CAP - LANES
     values = jnp.concatenate([first, second[:rest]], axis=0)
     wanted = second[rest : rest + CAP].astype(jnp.int32)
-    camera_ref[view] = second[rest + CAP : rest + CAP + 16]
+    camera_ref[place] = second[rest + CAP : rest + CAP + 16]
     high_place, low_place = wanted >> 8, wanted & (WIDE - 1)
     high, low = halves(values)
     high, low = high.astype(F32), low.astype(F32)
     lefts, rights = [], []
-    for place in range(CAP):
-        at_high = tall_iota == spread(high_place[place : place + 1], (TALL, LANES))
-        at_low = wide_iota == spread(low_place[place : place + 1], (WIDE, LANES))
+    for rank in range(CAP):
+        at_high = tall_iota == spread(high_place[rank : rank + 1], (TALL, LANES))
+        at_low = wide_iota == spread(low_place[rank : rank + 1], (WIDE, LANES))
         at_low = at_low.astype(F32).astype(BF16)
         for source in (high, low):
-            rows = [source[index * CAP + place : index * CAP + place + 1] for index in range(FEATS)]
+            rows = [source[index * CAP + rank : index * CAP + rank + 1] for index in range(FEATS)]
             left = [jnp.where(at_high, spread(row, (TALL, LANES)), 0.0) for row in rows]
             lefts.append(jnp.concatenate(left, axis=0).astype(BF16))
             rights.append(at_low)
     total = dot_lanes(jnp.concatenate(lefts, axis=1), jnp.concatenate(rights, axis=1))
     for half in range(2):
-        grads_ref[view, pl.ds(half, FEATS * TALL, stride=2), :] = total[:, half * LANES : (half + 1) * LANES]
+        grads_ref[place, pl.ds(half, FEATS * TALL, stride=2), :] = total[:, half * LANES : (half + 1) * LANES]
+
+
+SHAPE_ROWS = (3, 4, 5, 6, 7, 8, 9, 59, 60)
+
+
+def pull_view(chunk, place, center, shape, param, grads_ref, camera_ref, kept, keep):
+    def cotangent(feature):
+        return grads_ref[place, pl.ds(pl.multiple_of(feature * GROUPS + chunk * 8, 8), 8), :]
+
+    def add(index, value):
+        before = kept(index)
+        keep(index, value if before is None else before + value)
+
+    rotate, offset = camera_of(camera_ref[place])
+    eye = camera_center(rotate, offset)
+    basis, basis_back = jax.vjp(lambda spot: direction_basis(spot, eye), center)
+    colors = [cotangent(6 + channel) for channel in range(3)]
+    basis_grad = []
+    for term in range(16):
+        total = None
+        for channel in range(3):
+            index = 11 + 3 * term + channel
+            add(index, basis[term] * colors[channel])
+            piece = param(index) * colors[channel]
+            total = piece if total is None else total + piece
+        basis_grad.append(total)
+    (along,) = basis_back(basis_grad)
+    unused, screen_back = jax.vjp(
+        lambda spot, matrix: screen_features(spot, matrix, rotate, offset), center, shape
+    )
+    moved, bent = screen_back([cotangent(index) for index in range(5)])
+    for axis in range(3):
+        add(axis, along[axis] + moved[axis])
+    for row in range(3):
+        for col in range(3):
+            add(SHAPE_ROWS[3 * row + col], bent[row][col])
+    add(10, cotangent(5))
+
+
+def own_pullback_kernel(returned_ref, held_ref, partial_ref, grads_ref, camera_ref):
+    scatter_view(0, returned_ref, 0, grads_ref, camera_ref)
+
+    def step(chunk, carry):
+        def param(index):
+            return held_ref[chunk, pl.ds(index, 8, stride=PITCH), :]
+
+        def keep(index, value):
+            partial_ref[chunk, pl.ds(index, 8, stride=PITCH), :] = value
+
+        center = [param(index) for index in range(3)]
+        shape = shape_matrix([param(3 + index) for index in range(3)], [param(6 + index) for index in range(4)])
+        pull_view(chunk, 0, center, shape, param, grads_ref, camera_ref, lambda index: None, keep)
+        return carry
+
+    lax.fori_loop(0, CHUNKS, step, 0)
 
 
 def pullback_kernel(
-    arrived_ref, params_ref, out_ref, held_ref, sums_ref, grads_ref, camera_ref, staged_ref, semaphores
+    view_ref, arrived_ref, held_ref, partial_ref, out_ref, sums_ref, grads_ref, camera_ref, staged_ref, semaphores
 ):
     views = arrived_ref.shape[0]
 
-    def one_view(view, carry):
-        scatter_view(view, arrived_ref, grads_ref, camera_ref)
+    def one_view(place, carry):
+        view = lax.rem(view_ref[0] + 1 + place, views)
+        scatter_view(view, arrived_ref, place, grads_ref, camera_ref)
         return carry
 
-    lax.fori_loop(0, views, one_view, 0)
+    lax.fori_loop(0, views - 1, one_view, 0)
 
     def send(chunk):
         columns = chunk_columns(chunk)
         return pltpu.make_async_copy(staged_ref.at[:, columns], out_ref.at[:, columns], semaphores.at[chunk])
 
-    def param(index):
-        return held_ref[pl.ds(index, 8, stride=PITCH), :]
-
-    def keep(index, value):
-        sums_ref[pl.ds(index, 8, stride=PITCH), :] = value
-
-    def kept(index):
-        return sums_ref[pl.ds(index, 8, stride=PITCH), :]
-
     def step(chunk, carry):
-        spread_columns(params_ref, held_ref, chunk)
+        def param(index):
+            return held_ref[chunk, pl.ds(index, 8, stride=PITCH), :]
+
+        def first(index):
+            return partial_ref[chunk, pl.ds(index, 8, stride=PITCH), :]
+
+        def keep(index, value):
+            sums_ref[pl.ds(index, 8, stride=PITCH), :] = value
+
+        def kept(index):
+            return sums_ref[pl.ds(index, 8, stride=PITCH), :]
+
         center = [param(index) for index in range(3)]
         shape, shape_back = jax.vjp(
             shape_matrix, [param(3 + index) for index in range(3)], [param(6 + index) for index in range(4)]
         )
-        center_grad, shape_grad, opacity_grad = None, None, None
-        for view in range(views):
-            def cotangent(feature):
-                return grads_ref[view, pl.ds(pl.multiple_of(feature * GROUPS + chunk * 8, 8), 8), :]
-
-            rotate, offset = camera_of(camera_ref[view])
-            eye = camera_center(rotate, offset)
-            basis, basis_back = jax.vjp(lambda place: direction_basis(place, eye), center)
-            colors = [cotangent(6 + channel) for channel in range(3)]
-            basis_grad = []
-            for term in range(16):
-                total = None
-                for channel in range(3):
-                    index = 11 + 3 * term + channel
-                    piece = basis[term] * colors[channel]
-                    keep(index, piece if view == 0 else kept(index) + piece)
-                    piece = param(index) * colors[channel]
-                    total = piece if total is None else total + piece
-                basis_grad.append(total)
-            (along,) = basis_back(basis_grad)
-            unused, screen_back = jax.vjp(
-                lambda place, matrix: screen_features(place, matrix, rotate, offset), center, shape
+        for place in range(views - 1):
+            pull_view(
+                chunk, place, center, shape, param, grads_ref, camera_ref, kept if place else first, keep
             )
-            moved, bent = screen_back([cotangent(index) for index in range(5)])
-            pieces = [along[axis] + moved[axis] for axis in range(3)]
-            faded = cotangent(5)
-            if view == 0:
-                center_grad, shape_grad, opacity_grad = pieces, bent, faded
-            else:
-                center_grad = [one + other for one, other in zip(center_grad, pieces)]
-                shape_grad = [[one + other for one, other in zip(*rows)] for rows in zip(shape_grad, bent)]
-                opacity_grad = opacity_grad + faded
-        scale_grad, quaternion_grad = shape_back(shape_grad)
+        scale_grad, quaternion_grad = shape_back(
+            [[kept(SHAPE_ROWS[3 * row + col]) for col in range(3)] for row in range(3)]
+        )
         opacity = 1.0 / (1.0 + jnp.exp(-param(10)))
-        firsts = center_grad + list(scale_grad) + list(quaternion_grad) + [opacity * (1.0 - opacity) * opacity_grad]
-        for index, value in enumerate(firsts):
-            keep(index, value)
+        finals = list(scale_grad) + list(quaternion_grad) + [opacity * (1.0 - opacity) * kept(10)]
+        for index, value in enumerate(finals):
+            keep(3 + index, value)
         for group in range(CHUNK // LANES):
             columns = pl.ds(pl.multiple_of(chunk * CHUNK + group * LANES, LANES), LANES)
             staged_ref[:, columns] = sums_ref[group * PITCH : group * PITCH + PARAMS, :]
@@ -561,32 +592,37 @@
     )(*operands)
 
 
-def route(height, camera, first_tile, tile_lists):
+HELD = jax.ShapeDtypeStruct((CHUNKS, 8 * PITCH, LANES), F32)
+
+
+def route(tile_lists):
     return call(
-        functools.partial(route_kernel, height),
+        route_kernel,
         [
             jax.ShapeDtypeStruct((OWNERS, LANES), jnp.int32),
             jax.ShapeDtypeStruct((16 + 2 * CAP, LANES), jnp.int32),
+        ],
+        [tile_lists],
+        smalls=0,
+    )
+
+
+def project(height, camera, first_tile, view, gauss_params):
+    return pl.pallas_call(
+        functools.partial(project_kernel, height),
+        out_shape=[
+            jax.ShapeDtypeStruct((FEATS, GROUPS, LANES), F32),
+            HELD,
             jax.ShapeDtypeStruct((GEO, LANES), F32),
         ],
-        [camera, first_tile, tile_lists],
-        smalls=2,
-    )
-
-
-def project(gauss_params, geometry):
-    return pl.pallas_call(
-        project_kernel,
-        out_shape=jax.ShapeDtypeStruct((FEATS, GROUPS, LANES), F32),
-        in_specs=[pl.BlockSpec(memory_space=pltpu.HBM), pl.BlockSpec(memory_space=pltpu.VMEM)],
-        out_specs=pl.BlockSpec(memory_space=pltpu.VMEM),
+        in_specs=[pl.BlockSpec(memory_space=pltpu.SMEM)] * 3 + [pl.BlockSpec(memory_space=pltpu.HBM)],
+        out_specs=[pl.BlockSpec(memory_space=pltpu.VMEM)] * 3,
         scratch_shapes=[
             pltpu.VMEM((PARAMS, G_DEV), F32),
-            pltpu.VMEM((8 * PITCH, LANES), F32),
             pltpu.SemaphoreType.DMA((CHUNKS,)),
         ],
         compiler_params=pltpu.CompilerParams(vmem_limit_bytes=VMEM_LIMIT),
-    )(gauss_params, geometry)
+    )(camera, first_tile, view, gauss_params)
 
 
 def gather(requested, features):
@@ -611,23 +647,33 @@
     )
 
 
-def pullback(arrived, gauss_params):
-    views = arrived.shape[0]
+def own_pullback(returned, held):
+    return call(
+        own_pullback_kernel,
+        HELD,
+        [returned.reshape((1,) + returned.shape), held],
+        smalls=0,
+        scratch=[pltpu.VMEM((1, FEATS * GROUPS, LANES), F32), pltpu.VMEM((1, 16, LANES), F32)],
+        cost_estimate=pl.CostEstimate(flops=20_000_000, bytes_accessed=4_000_000, transcendentals=0),
+    )
+
+
+def pullback(view, arrived, held, partial):
+    others = arrived.shape[0] - 1
     return pl.pallas_call(
         pullback_kernel,
         out_shape=jax.ShapeDtypeStruct((PARAMS, G_DEV), F32),
-        in_specs=[pl.BlockSpec(memory_space=pltpu.VMEM)] * 2,
+        in_specs=[pl.BlockSpec(memory_space=pltpu.SMEM)] + [pl.BlockSpec(memory_space=pltpu.VMEM)] * 3,
         out_specs=pl.BlockSpec(memory_space=pltpu.HBM),
         scratch_shapes=[
             pltpu.VMEM((8 * PITCH, LANES), F32),
-            pltpu.VMEM((8 * PITCH, LANES), F32),
-            pltpu.VMEM((views, FEATS * GROUPS, LANES), F32),
-            pltpu.VMEM((views, 16, LANES), F32),
+            pltpu.VMEM((others, FEATS * GROUPS, LANES), F32),
+            pltpu.VMEM((others, 16, LANES), F32),
             pltpu.VMEM((PARAMS, G_DEV), F32),
             pltpu.SemaphoreType.DMA((CHUNKS,)),
         ],
         compiler_params=pltpu.CompilerParams(vmem_limit_bytes=VMEM_LIMIT),
-    )(arrived, gauss_params)
+    )(view, arrived, held, partial)
 
 
 def per_device(gauss_params, camera, background, tile_lists, tile_lengths, pixel_cotangent):
@@ -636,8 +682,9 @@
     tiles_here = tile_lists.shape[1]
     height = tiles_here * owners_total // TX
     first_tile = (lax.axis_index("img") * tiles_here).astype(jnp.int32).reshape(1)
-    requests, aux, geometry = route(height, camera, first_tile, tile_lists)
-    features = project(gauss_params, geometry)
+    view = lax.axis_index("view").astype(jnp.int32).reshape(1)
+    requests, aux = route(tile_lists)
+    features, held, geometry = project(height, camera, first_tile, view, gauss_params)
     requested = lax.all_to_all(requests, "img", split_axis=0, concat_axis=0, tiled=True)
     outgoing = gather(requested, features)
     arrived = lax.all_to_all(outgoing, "img", split_axis=0, concat_axis=0, tiled=True)
@@ -645,7 +692,8 @@
     returned = lax.all_to_all(slot_grads, "img", split_axis=0, concat_axis=0, tiled=True)
     copies = jnp.broadcast_to(returned[None], (views,) + returned.shape)
     everyone = lax.all_to_all(copies, "view", split_axis=0, concat_axis=0, tiled=True)
-    return pullback(everyone, gauss_params)
+    partial = own_pullback(returned, held)
+    return pullback(view, everyone, held, partial)
 
 
 def solution(mesh):

time: 95.6 us -> 94.6 us (0.990)
  blocking collectives: 47.8 us -> 36.3 us
  starting transfers between devices: 18.4 us -> 22.4 us
  waiting for transfers between devices: 8.83 us -> 12.6 us
  local copies, waits for them, and re-layouts: 2.99 us -> 6.72 us
  Pallas kernels: 17.2 us -> 16.1 us
    all_to_all x1 -> x0, blocking collectives: 12.3 us -> none  [per_device(): lax.all_to_all(copies, 'view', split_axis=0, concat_axis=0, tiled=True)]
    all_to_all x0 -> x1, waiting for transfers between devices: none -> 5.03 us  [per_device(): lax.all_to_all(copies, 'view', split_axis=0, concat_axis=0, tiled=True)]
    all_to_all x0 -> x1, starting transfers between devices: none -> 4.01 us  [per_device(): lax.all_to_all(copies, 'view', split_axis=0, concat_axis=0, tiled=True)]
    unnamed x14 -> x16, local copies, waits for them, and re-layouts: 2.96 us -> 5.89 us
    pallas_call x1, Pallas kernels: 8.11 us -> 6.37 us  [pullback(): pl.pallas_call(pullback_kernel, out_shape=jax.ShapeDtypeStruct((PARAMS, G...]
    all_to_all x1, waiting for transfers between devices: 8.83 us -> 7.57 us  [per_device(): lax.all_to_all(requests, 'img', split_axis=0, concat_axis=0, tiled=True)]
    pallas_call x3 -> x4, Pallas kernels: 8.05 us -> 8.11 us  [call(): pl.pallas_call(kernel, out_shape=out_shape, in_specs=[pl.BlockSpec(memory...]
  transfers between devices with their start and end apart: 1 -> 2, of which waited for: 1 -> 2; matrix products, arithmetic and copies ran while one was open for 0% -> 0% of each run, Pallas kernels for 1% -> 4%
where the time goes in v3:
time: 94.6 us; the launch traced here: 94.2 us
  blocking collectives  36.3 us (38%)
  starting transfers between devices  22.4 us (24%)
  Pallas kernels  16.1 us (17%)
  waiting for transfers between devices  12.6 us (13%)
  local copies, waits for them, and re-layouts  6.72 us (7%)
    all_to_all x1, blocking collectives, per_device(): lax.all_to_all(outgoing, 'img', split_axis=0, concat_axis=0, tiled=True)  18.5 us
    all_to_all x1, starting transfers between devices, per_device(): lax.all_to_all(requests, 'img', split_axis=0, concat_axis=0, tiled=True)  18.4 us
    all_to_all x1, blocking collectives, per_device(): lax.all_to_all(slot_grads, 'img', split_axis=0, concat_axis=0, tiled=True)  17.9 us
    pallas_call x4, Pallas kernels, call(): pl.pallas_call(kernel, out_shape=out_shape, in_specs=[pl.BlockSpec(memory...  8.11 us
    all_to_all x1, waiting for transfers between devices, per_device(): lax.all_to_all(requests, 'img', split_axis=0, concat_axis=0, tiled=True)  7.57 us
    pallas_call x1, Pallas kernels, pullback(): pl.pallas_call(pullback_kernel, out_shape=jax.ShapeDtypeStruct((PARAMS, G...  6.37 us
    unnamed x16, local copies, waits for them, and re-layouts  5.89 us
    all_to_all x1, waiting for transfers between devices, per_device(): lax.all_to_all(copies, 'view', split_axis=0, concat_axis=0, tiled=True)  5.03 us
  transfers between devices with their start and end apart: 2, of which 2 were waited for; matrix products, arithmetic and copies ran while one was open for 0% of the time, Pallas kernels for 4%

profile of v3, /device:TPU:1, one launch (start us, length us, event | category | flops | bytes accessed | tf_op | source)
XLA Modules:
  0.0 94.2 jit_solution(18439346421136806806)
XLA Ops:
  0.0 0.0 copy-start.3
  0.0 0.0 copy-start.4
  0.0 0.7 copy-done.4
  0.7 0.0 copy-start.6
  0.7 0.0 copy-start.7
  0.7 1.3 %shard_map.65 = (s32[128,128]{1,0:T(8,128)}, s32[48,128]{1,0:T(8,128)S(1)}) custom-call(s32[1,4,256]{2,1,0:T(4,128)S(1)} %copy-done.4), custom_call_target="tpu_custom_call" | custom-call | tf_op jit(solution)/shard_map/pallas_call | solution.py:584
  2.0 18.4 %all-to-all-start = ((s32[128,1,128]{2,1,0:T(1,128)}), s32[128,1,128]{2,1,0:T(1,128)S(1)}, u32[]{:S(2)}, u32[]{:S(2)}) async-start(s32[128,1,128]{2,1,0:T(1,128)} %bitcast.3), calls=%async_computation | async-start | bytes 131072 | tf_op jit(solution)/shard_map/all_to_all | solution.py:688
  20.4 0.0 copy-start.2
  20.4 1.6 %copy-done.2 = f32[59,8192]{1,0:T(8,128)S(1)} copy-done((f32[59,8192]{1,0:T(8,128)S(1)}, f32[59,8192]{1,0:T(8,128)}, u32[]{:S(2)}) %copy-start.2) | copy-done | bytes 1933336
  22.0 0.0 copy-start.5
  22.0 0.7 copy-done.5
  22.6 1.6 %shard_map.64 = (f32[9,64,128]{2,1,0:T(8,128)S(1)}, f32[8,520,128]{2,1,0:T(8,128)S(1)}, f32[24,128]{1,0:T(8,128)S(1)}) custom-call(f32[1,6]{1,0:T(1,128)S(1)} %copy-done.5, s32[1]{0:T(128)} %bitcast.1.first_ref, s32[1]{0:T(128)} %bitcast.view_ref, f32[59,8192]{1,0:T(8,128)S(1)} %copy-done.2), custom_call_target="tpu_custom_call" | custom-call | tf_op jit(solution)/shard_map/pallas_call | solution.py:611
  24.3 7.6 %all-to-all-done = s32[128,1,128]{2,1,0:T(1,128)S(1)} async-done(((s32[128,1,128]{2,1,0:T(1,128)}), s32[128,1,128]{2,1,0:T(1,128)S(1)}, u32[]{:S(2)}, u32[]{:S(2)}) %all-to-all-start) | async-done | bytes 65568 | tf_op jit(solution)/shard_map/all_to_all | solution.py:688
  31.8 1.7 %shard_map.66 = f32[256,128]{1,0:T(8,128)S(1)} custom-call(s32[128,128]{1,0:T(8,128)S(1)} %bitcast.16, f32[9,64,128]{2,1,0:T(8,128)S(1)} %get-tuple-element.12.feats_ref), custom_call_target="tpu_custom_call" | custom-call | tf_op jit(solution)/shard_map/pallas_call | solution.py:584
  33.5 18.5 %all_to_all.36 = f32[128,2,128]{2,1,0:T(2,128)S(1)} all-to-all(f32[128,2,128]{2,1,0:T(2,128)S(1)} %bitcast.15), channel_id=1, replica_groups=mesh['img'=128,'view'=4] {'img'}, dimensions={0} | all-to-all | bytes 262144 | tf_op jit(solution)/shard_map/all_to_all | solution.py:690
  52.0 0.0 copy-done.3
  52.0 0.0 copy-done.6
  52.0 0.0 copy-done.7
  52.0 3.3 %shard_map.67 = f32[256,128]{1,0:T(8,128)S(1)} custom-call(s32[1,4]{1,0:T(1,128)S(1)} %copy-done.6, f32[3]{0:T(128)S(1)} %copy-done.7, f32[24,128]{1,0:T(8,128)S(1)} %get-tuple-element.10.geo_ref, f32[256,128]{1,0:T(8,128)S(1)} %bitcast.13, s32[48,128]{1,0:T(8,128)S(1)} %get-tuple-element.13.aux_ref, f32[1,3,4,256]{3,2,1,0:T(4,128)S(1)} %copy-done.3), custom_call_target="tpu_custom_call" | custom-call | tf_op jit(solution)/shard_map/pallas_call | solution.py:584
  55.3 17.9 %all_to_all.37 = f32[128,2,128]{2,1,0:T(2,128)S(1)} all-to-all(f32[128,2,128]{2,1,0:T(2,128)S(1)} %bitcast.14), channel_id=1, replica_groups=mesh['img'=128,'view'=4] {'img'}, dimensions={0} | all-to-all | bytes 262144 | tf_op jit(solution)/shard_map/all_to_all | solution.py:692
  73.2 0.8 broadcast_in_dim.11
  74.0 4.0 %all-to-all-start.3 = ((f32[4,256,128]{2,1,0:T(8,128)}), f32[4,256,128]{2,1,0:T(8,128)S(1)}, u32[]{:S(2)}, u32[]{:S(2)}) async-start(f32[4,256,128]{2,1,0:T(8,128)} %broadcast_in_dim.11), calls=%async_computation.3 | async-start | bytes 1048576 | tf_op jit(solution)/shard_map/all_to_all | solution.py:694
  78.1 1.8 %shard_map.68.partial_ref = f32[8,520,128]{2,1,0:T(8,128)S(1)} custom-call(f32[1,256,128]{2,1,0:T(8,128)S(1)} %bitcast.12, f32[8,520,128]{2,1,0:T(8,128)S(1)} %get-tuple-element.14.held_ref), custom_call_target="tpu_custom_call" | custom-call | flops 20000000 | bytes 4000000 | tf_op jit(solution)/shard_map/pallas_call | solution.py:584
  79.9 0.0 copy-start
  79.9 1.3 %copy-done = f32[8,520,128]{2,1,0:T(8,128)} copy-done((f32[8,520,128]{2,1,0:T(8,128)}, f32[8,520,128]{2,1,0:T(8,128)S(1)}, u32[]{:S(2)}) %copy-start) | copy-done | bytes 2129944
  81.2 5.0 %all-to-all-done.3.arrived_ref = f32[4,256,128]{2,1,0:T(8,128)S(1)} async-done(((f32[4,256,128]{2,1,0:T(8,128)}), f32[4,256,128]{2,1,0:T(8,128)S(1)}, u32[]{:S(2)}, u32[]{:S(2)}) %all-to-all-start.3) | async-done | bytes 524320 | tf_op jit(solution)/shard_map/all_to_all | solution.py:694
  86.2 0.0 copy-start.1
  86.3 1.6 %copy-done.1 = f32[8,520,128]{2,1,0:T(8,128)S(1)} copy-done((f32[8,520,128]{2,1,0:T(8,128)S(1)}, f32[8,520,128]{2,1,0:T(8,128)}, u32[]{:S(2)}) %copy-start.1) | copy-done | bytes 2129944
  87.9 6.4 %shard_map.69 = f32[59,8192]{1,0:T(8,128)} custom-call(s32[1]{0:T(128)} %bitcast.view_ref, f32[4,256,128]{2,1,0:T(8,128)S(1)} %all-to-all-done.3.arrived_ref, f32[8,520,128]{2,1,0:T(8,128)S(1)} %get-tuple-element.14.held_ref, f32[8,520,128]{2,1,0:T(8,128)S(1)} %copy-done.1), custom_call_target="tpu_custom_call" | custom-call | tf_op jit(solution)/shard_map/pallas_call | solution.py:663
Async XLA Ops:
  0.0 52.0 %copy-start.3 = (f32[1,3,4,256]{3,2,1,0:T(4,128)S(1)}, f32[1,3,4,256]{3,2,1,0:T(4,128)}, u32[]{:S(2)}) copy-start(f32[1,3,4,256]{3,2,1,0:T(4,128)} %cotangent_ref.1) | copy-start | bytes 36868
  0.0 0.7 copy-start.4
  0.7 51.3 %copy-start.6 = (s32[1,4]{1,0:T(1,128)S(1)}, s32[1,4]{1,0:T(1,128)}, u32[]{:S(2)}) copy-start(s32[1,4]{1,0:T(1,128)} %lengths_ref.1) | copy-start | bytes 52
  0.7 51.3 %copy-start.7 = (f32[3]{0:T(128)S(1)}, f32[3]{0:T(128)}, u32[]{:S(2)}) copy-start(f32[3]{0:T(128)} %background_ref.1) | copy-start | bytes 40
  2.0 29.9 %all-to-all-start = ((s32[128,1,128]{2,1,0:T(1,128)}), s32[128,1,128]{2,1,0:T(1,128)S(1)}, u32[]{:S(2)}, u32[]{:S(2)}) async-start(s32[128,1,128]{2,1,0:T(1,128)} %bitcast.3), calls=%async_computation | async-start | bytes 131072 | tf_op jit(solution)/shard_map/all_to_all | solution.py:688
  20.4 1.6 %copy-start.2 = (f32[59,8192]{1,0:T(8,128)S(1)}, f32[59,8192]{1,0:T(8,128)}, u32[]{:S(2)}) copy-start(f32[59,8192]{1,0:T(8,128)} %params_ref.1) | copy-start | bytes 5799940
  22.0 0.7 copy-start.5
  74.0 12.2 %all-to-all-start.3 = ((f32[4,256,128]{2,1,0:T(8,128)}), f32[4,256,128]{2,1,0:T(8,128)S(1)}, u32[]{:S(2)}, u32[]{:S(2)}) async-start(f32[4,256,128]{2,1,0:T(8,128)} %broadcast_in_dim.11), calls=%async_computation.3 | async-start | bytes 1048576 | tf_op jit(solution)/shard_map/all_to_all | solution.py:694
  79.9 1.3 %copy-start = (f32[8,520,128]{2,1,0:T(8,128)}, f32[8,520,128]{2,1,0:T(8,128)S(1)}, u32[]{:S(2)}) copy-start(f32[8,520,128]{2,1,0:T(8,128)S(1)} %shard_map.68.partial_ref) | copy-start | bytes 6389764
  86.2 1.6 %copy-start.1 = (f32[8,520,128]{2,1,0:T(8,128)S(1)}, f32[8,520,128]{2,1,0:T(8,128)}, u32[]{:S(2)}) copy-start(f32[8,520,128]{2,1,0:T(8,128)} %copy-done) | copy-start | bytes 6389764

commit v4 on v3

--- a/solution.py
+++ b/solution.py
@@ -23,6 +23,7 @@
 CHUNK = G_DEV // CHUNKS
 FEATS = 9
 PACK = 256
+SENT = FEATS * CAP + CAP + 16
 
 FOCAL = 2.0
 DILATION = 0.0001
@@ -48,7 +49,8 @@
 LOG2_E = 1.4426950408889634
 F32 = jnp.float32
 BF16 = jnp.bfloat16
-VMEM_LIMIT = 32 * 1024 * 1024
+VMEM_LIMIT = 16 * 1024 * 1024
+LAST_VMEM_LIMIT = 52 * 1024 * 1024
 
 
 def iota(shape, axis, dtype=jnp.int32):
@@ -436,15 +438,25 @@
 TALL = G_DEV // WIDE
 
 
+def duplicate_kernel(returned_ref, own_ref, copies_ref, semaphores):
+    own_ref[:LANES, :] = returned_ref[pl.ds(0, LANES, stride=2), :].T
+    own_ref[LANES:, :] = returned_ref[pl.ds(1, LANES, stride=2), :].T[: SENT - LANES]
+    copies = [
+        pltpu.make_async_copy(own_ref, copies_ref.at[view], semaphores.at[view])
+        for view in range(copies_ref.shape[0])
+    ]
+    for copy in copies:
+        copy.start()
+    for copy in copies:
+        copy.wait()
+
+
 def scatter_view(view, arrived_ref, place, grads_ref, camera_ref):
     tall_iota = iota((TALL, LANES), 0)
     wide_iota = iota((WIDE, LANES), 0)
-    first = arrived_ref[view, pl.ds(0, LANES, stride=2), :].T
-    second = arrived_ref[view, pl.ds(1, LANES, stride=2), :].T
-    rest = FEATS * CAP - LANES
-    values = jnp.concatenate([first, second[:rest]], axis=0)
-    wanted = second[rest : rest + CAP].astype(jnp.int32)
-    camera_ref[place] = second[rest + CAP : rest + CAP + 16]
+    values = arrived_ref[view, : FEATS * CAP, :]
+    wanted = arrived_ref[view, FEATS * CAP : FEATS * CAP + CAP, :].astype(jnp.int32)
+    camera_ref[place] = arrived_ref[view, FEATS * CAP + CAP : SENT, :]
     high_place, low_place = wanted >> 8, wanted & (WIDE - 1)
     high, low = halves(values)
     high, low = high.astype(F32), low.astype(F32)
@@ -500,7 +512,18 @@
     add(10, cotangent(5))
 
 
-def own_pullback_kernel(returned_ref, held_ref, partial_ref, grads_ref, camera_ref):
+def each_chunk(action):
+    def body(chunk, carry):
+        action(chunk)
+        return carry
+
+    lax.fori_loop(0, CHUNKS, body, 0)
+
+
+def own_pullback_kernel(returned_ref, held_ref, out_ref, grads_ref, camera_ref, partial_ref, semaphores):
+    def send(chunk):
+        return pltpu.make_async_copy(partial_ref.at[chunk], out_ref.at[chunk], semaphores.at[chunk])
+
     scatter_view(0, returned_ref, 0, grads_ref, camera_ref)
 
     def step(chunk, carry):
@@ -513,15 +536,30 @@
         center = [param(index) for index in range(3)]
         shape = shape_matrix([param(3 + index) for index in range(3)], [param(6 + index) for index in range(4)])
         pull_view(chunk, 0, center, shape, param, grads_ref, camera_ref, lambda index: None, keep)
+        send(chunk).start()
         return carry
 
     lax.fori_loop(0, CHUNKS, step, 0)
+    each_chunk(lambda chunk: send(chunk).wait())
 
 
 def pullback_kernel(
-    view_ref, arrived_ref, held_ref, partial_ref, out_ref, sums_ref, grads_ref, camera_ref, staged_ref, semaphores
+    view_ref, arrived_ref, held_hbm, partial_hbm, out_ref,
+    held_ref, partial_ref, sums_ref, grads_ref, camera_ref, staged_ref, held_sems, partial_sems, semaphores,
 ):
     views = arrived_ref.shape[0]
+
+    def fetch_held(chunk):
+        return pltpu.make_async_copy(held_hbm.at[chunk], held_ref.at[chunk], held_sems.at[chunk])
+
+    def fetch_partial(chunk):
+        return pltpu.make_async_copy(partial_hbm.at[chunk], partial_ref.at[chunk], partial_sems.at[chunk])
+
+    def start(chunk):
+        fetch_held(chunk).start()
+        fetch_partial(chunk).start()
+
+    each_chunk(start)
 
     def one_view(place, carry):
         view = lax.rem(view_ref[0] + 1 + place, views)
@@ -535,6 +573,9 @@
         return pltpu.make_async_copy(staged_ref.at[:, columns], out_ref.at[:, columns], semaphores.at[chunk])
 
     def step(chunk, carry):
+        fetch_held(chunk).wait()
+        fetch_partial(chunk).wait()
+
         def param(index):
             return held_ref[chunk, pl.ds(index, 8, stride=PITCH), :]
 
@@ -569,12 +610,7 @@
         return carry
 
     lax.fori_loop(0, CHUNKS, step, 0)
-
-    def finish(chunk, carry):
-        send(chunk).wait()
-        return carry
-
-    lax.fori_loop(0, CHUNKS, finish, 0)
+    each_chunk(lambda chunk: send(chunk).wait())
 
 
 def call(kernel, out_shape, operands, smalls=(), scratch=(), **kwargs):
@@ -647,15 +683,35 @@
     )
 
 
-def own_pullback(returned, held):
-    return call(
+def duplicate(returned, views):
+    return pl.pallas_call(
+        duplicate_kernel,
+        out_shape=[
+            jax.ShapeDtypeStruct((SENT, LANES), F32),
+            jax.ShapeDtypeStruct((views, SENT, LANES), F32),
+        ],
+        in_specs=[pl.BlockSpec(memory_space=pltpu.VMEM)],
+        out_specs=[pl.BlockSpec(memory_space=pltpu.VMEM), pl.BlockSpec(memory_space=pltpu.HBM)],
+        scratch_shapes=[pltpu.SemaphoreType.DMA((views,))],
+        compiler_params=pltpu.CompilerParams(vmem_limit_bytes=VMEM_LIMIT),
+    )(returned)
+
+
+def own_pullback(own, held):
+    return pl.pallas_call(
         own_pullback_kernel,
-        HELD,
-        [returned.reshape((1,) + returned.shape), held],
-        smalls=0,
-        scratch=[pltpu.VMEM((1, FEATS * GROUPS, LANES), F32), pltpu.VMEM((1, 16, LANES), F32)],
+        out_shape=HELD,
+        in_specs=[pl.BlockSpec(memory_space=pltpu.VMEM)] * 2,
+        out_specs=pl.BlockSpec(memory_space=pltpu.HBM),
+        scratch_shapes=[
+            pltpu.VMEM((1, FEATS * GROUPS, LANES), F32),
+            pltpu.VMEM((1, 16, LANES), F32),
+            pltpu.VMEM(HELD.shape, F32),
+            pltpu.SemaphoreType.DMA((CHUNKS,)),
+        ],
+        compiler_params=pltpu.CompilerParams(vmem_limit_bytes=VMEM_LIMIT),
         cost_estimate=pl.CostEstimate(flops=20_000_000, bytes_accessed=4_000_000, transcendentals=0),
-    )
+    )(own.reshape((1,) + own.shape), held)
 
 
 def pullback(view, arrived, held, partial):
@@ -663,16 +719,22 @@
     return pl.pallas_call(
         pullback_kernel,
         out_shape=jax.ShapeDtypeStruct((PARAMS, G_DEV), F32),
-        in_specs=[pl.BlockSpec(memory_space=pltpu.SMEM)] + [pl.BlockSpec(memory_space=pltpu.VMEM)] * 3,
+        in_specs=[
+            pl.BlockSpec(memory_space=space) for space in (pltpu.SMEM, pltpu.VMEM, pltpu.HBM, pltpu.HBM)
+        ],
         out_specs=pl.BlockSpec(memory_space=pltpu.HBM),
         scratch_shapes=[
+            pltpu.VMEM(HELD.shape, F32),
+            pltpu.VMEM(HELD.shape, F32),
             pltpu.VMEM((8 * PITCH, LANES), F32),
             pltpu.VMEM((others, FEATS * GROUPS, LANES), F32),
             pltpu.VMEM((others, 16, LANES), F32),
             pltpu.VMEM((PARAMS, G_DEV), F32),
             pltpu.SemaphoreType.DMA((CHUNKS,)),
+            pltpu.SemaphoreType.DMA((CHUNKS,)),
+            pltpu.SemaphoreType.DMA((CHUNKS,)),
         ],
-        compiler_params=pltpu.CompilerParams(vmem_limit_bytes=VMEM_LIMIT),
+        compiler_params=pltpu.CompilerParams(vmem_limit_bytes=LAST_VMEM_LIMIT),
     )(view, arrived, held, partial)
 
 
@@ -690,9 +752,9 @@
     arrived = lax.all_to_all(outgoing, "img", split_axis=0, concat_axis=0, tiled=True)
     slot_grads = render(height, tile_lengths, background, geometry, arrived, aux, pixel_cotangent)
     returned = lax.all_to_all(slot_grads, "img", split_axis=0, concat_axis=0, tiled=True)
-    copies = jnp.broadcast_to(returned[None], (views,) + returned.shape)
+    own, copies = duplicate(returned, views)
     everyone = lax.all_to_all(copies, "view", split_axis=0, concat_axis=0, tiled=True)
-    partial = own_pullback(returned, held)
+    partial = own_pullback(own, held)
     return pullback(view, everyone, held, partial)
 
 

time: 94.6 us -> 91.2 us (0.964)
  local copies, waits for them, and re-layouts: 6.72 us -> 4.28 us
  waiting for transfers between devices: 12.6 us -> 10.6 us
  Pallas kernels: 16.1 us -> 17.2 us
    pallas_call x0 -> x2, Pallas kernels: none -> 2.95 us  [the longest x1 2.09 us: own_pullback(): pl.pallas_call(own_pullback_kernel, out_shape=HELD, in_specs=[pl.BlockSpe...]
    all_to_all x1, waiting for transfers between devices: 5.03 us -> 3.01 us  [per_device(): lax.all_to_all(copies, 'view', split_axis=0, concat_axis=0, tiled=True)]
    pallas_call x4 -> x3, Pallas kernels: 8.11 us -> 6.29 us  [call(): pl.pallas_call(kernel, out_shape=out_shape, in_specs=[pl.BlockSpec(memory...]
    unnamed x16, local copies, waits for them, and re-layouts: 5.89 us -> 4.28 us
where the time goes in v4:
time: 91.2 us; the launch traced here: 90.9 us
  blocking collectives  36.3 us (40%)
  starting transfers between devices  22.4 us (25%)
  Pallas kernels  17.2 us (19%)
  waiting for transfers between devices  10.6 us (12%)
  local copies, waits for them, and re-layouts  4.28 us (5%)
    all_to_all x1, blocking collectives, per_device(): lax.all_to_all(outgoing, 'img', split_axis=0, concat_axis=0, tiled=True)  18.5 us
    all_to_all x1, starting transfers between devices, per_device(): lax.all_to_all(requests, 'img', split_axis=0, concat_axis=0, tiled=True)  18.4 us
    all_to_all x1, blocking collectives, per_device(): lax.all_to_all(slot_grads, 'img', split_axis=0, concat_axis=0, tiled=True)  17.9 us
    all_to_all x1, waiting for transfers between devices, per_device(): lax.all_to_all(requests, 'img', split_axis=0, concat_axis=0, tiled=True)  7.56 us
    pallas_call x1, Pallas kernels, pullback(): pl.pallas_call(pullback_kernel, out_shape=jax.ShapeDtypeStruct((PARAMS, G...  6.3 us
    pallas_call x3, Pallas kernels, call(): pl.pallas_call(kernel, out_shape=out_shape, in_specs=[pl.BlockSpec(memory...  6.29 us
    unnamed x16, local copies, waits for them, and re-layouts  4.28 us
    all_to_all x1, starting transfers between devices, per_device(): lax.all_to_all(copies, 'view', split_axis=0, concat_axis=0, tiled=True)  4.02 us
  transfers between devices with their start and end apart: 2, of which 2 were waited for; matrix products, arithmetic and copies ran while one was open for 0% of the time, Pallas kernels for 4%

profile of v4, /device:TPU:1, one launch (start us, length us, event | category | flops | bytes accessed | tf_op | source)
XLA Modules:
  0.0 90.9 jit_solution(9625040592144625244)
XLA Ops:
  0.0 0.0 copy-start.3
  0.0 0.0 copy-start.4
  0.0 0.7 copy-done.4
  0.7 0.0 copy-start.6
  0.7 0.0 copy-start.7
  0.7 1.3 %shard_map.65 = (s32[128,128]{1,0:T(8,128)}, s32[48,128]{1,0:T(8,128)S(1)}) custom-call(s32[1,4,256]{2,1,0:T(4,128)S(1)} %copy-done.4), custom_call_target="tpu_custom_call" | custom-call | tf_op jit(solution)/shard_map/pallas_call | solution.py:620
  2.0 18.4 %all-to-all-start = ((s32[128,1,128]{2,1,0:T(1,128)}), s32[128,1,128]{2,1,0:T(1,128)S(1)}, u32[]{:S(2)}, u32[]{:S(2)}) async-start(s32[128,1,128]{2,1,0:T(1,128)} %bitcast.3), calls=%async_computation | async-start | bytes 131072 | tf_op jit(solution)/shard_map/all_to_all | solution.py:750
  20.4 0.0 copy-start.2
  20.4 1.6 %copy-done.2 = f32[59,8192]{1,0:T(8,128)S(1)} copy-done((f32[59,8192]{1,0:T(8,128)S(1)}, f32[59,8192]{1,0:T(8,128)}, u32[]{:S(2)}) %copy-start.2) | copy-done | bytes 1933336
  22.0 0.0 copy-start.5
  22.0 0.7 copy-done.5
  22.6 1.6 %shard_map.64 = (f32[9,64,128]{2,1,0:T(8,128)S(1)}, f32[8,520,128]{2,1,0:T(8,128)S(1)}, f32[24,128]{1,0:T(8,128)S(1)}) custom-call(f32[1,6]{1,0:T(1,128)S(1)} %copy-done.5, s32[1]{0:T(128)} %bitcast.1.first_ref, s32[1]{0:T(128)} %bitcast.view_ref, f32[59,8192]{1,0:T(8,128)S(1)} %copy-done.2), custom_call_target="tpu_custom_call" | custom-call | tf_op jit(solution)/shard_map/pallas_call | solution.py:647
  24.3 0.0 copy-start
  24.3 7.6 %all-to-all-done = s32[128,1,128]{2,1,0:T(1,128)S(1)} async-done(((s32[128,1,128]{2,1,0:T(1,128)}), s32[128,1,128]{2,1,0:T(1,128)S(1)}, u32[]{:S(2)}, u32[]{:S(2)}) %all-to-all-start) | async-done | bytes 65568 | tf_op jit(solution)/shard_map/all_to_all | solution.py:750
  31.8 1.7 %shard_map.66 = f32[256,128]{1,0:T(8,128)S(1)} custom-call(s32[128,128]{1,0:T(8,128)S(1)} %bitcast.15, f32[9,64,128]{2,1,0:T(8,128)S(1)} %get-tuple-element.14.feats_ref), custom_call_target="tpu_custom_call" | custom-call | tf_op jit(solution)/shard_map/pallas_call | solution.py:620
  33.5 18.5 %all_to_all.38 = f32[128,2,128]{2,1,0:T(2,128)S(1)} all-to-all(f32[128,2,128]{2,1,0:T(2,128)S(1)} %bitcast.14), channel_id=1, replica_groups=mesh['img'=128,'view'=4] {'img'}, dimensions={0} | all-to-all | bytes 262144 | tf_op jit(solution)/shard_map/all_to_all | solution.py:752
  52.0 0.0 copy-done.3
  52.0 0.0 copy-done.6
  52.0 0.0 copy-done.7
  52.0 3.3 %shard_map.67 = f32[256,128]{1,0:T(8,128)S(1)} custom-call(s32[1,4]{1,0:T(1,128)S(1)} %copy-done.6, f32[3]{0:T(128)S(1)} %copy-done.7, f32[24,128]{1,0:T(8,128)S(1)} %get-tuple-element.12.geo_ref, f32[256,128]{1,0:T(8,128)S(1)} %bitcast.11, s32[48,128]{1,0:T(8,128)S(1)} %get-tuple-element.15.aux_ref, f32[1,3,4,256]{3,2,1,0:T(4,128)S(1)} %copy-done.3), custom_call_target="tpu_custom_call" | custom-call | tf_op jit(solution)/shard_map/pallas_call | solution.py:620
  55.4 17.9 %all_to_all.39 = f32[128,2,128]{2,1,0:T(2,128)S(1)} all-to-all(f32[128,2,128]{2,1,0:T(2,128)S(1)} %bitcast.12), channel_id=1, replica_groups=mesh['img'=128,'view'=4] {'img'}, dimensions={0} | all-to-all | bytes 262144 | tf_op jit(solution)/shard_map/all_to_all | solution.py:754
  73.2 0.9 shard_map.68
  74.1 4.0 %all-to-all-start.3 = ((f32[4,176,128]{2,1,0:T(8,128)}), f32[4,176,128]{2,1,0:T(8,128)S(1)}, u32[]{:S(2)}, u32[]{:S(2)}) async-start(f32[4,176,128]{2,1,0:T(8,128)} %get-tuple-element.16), calls=%async_computation.3 | async-start | bytes 720896 | tf_op jit(solution)/shard_map/all_to_all | solution.py:756
  78.1 2.1 %shard_map.69.partial_hbm = f32[8,520,128]{2,1,0:T(8,128)S(1)} custom-call(f32[1,176,128]{2,1,0:T(8,128)S(1)} %bitcast.16, f32[8,520,128]{2,1,0:T(8,128)S(1)} %get-tuple-element.17.held_ref.held_hbm), custom_call_target="tpu_custom_call" | custom-call | flops 20000000 | bytes 4000000 | tf_op jit(solution)/shard_map/pallas_call | solution.py:701
  80.2 0.0 copy-done
  80.2 0.0 copy-start.1
  80.2 1.3 %copy-done.1 = f32[8,520,128]{2,1,0:T(8,128)} copy-done((f32[8,520,128]{2,1,0:T(8,128)}, f32[8,520,128]{2,1,0:T(8,128)S(1)}, u32[]{:S(2)}) %copy-start.1) | copy-done | bytes 2129944
  81.6 3.0 %all-to-all-done.3.arrived_ref = f32[4,176,128]{2,1,0:T(8,128)S(1)} async-done(((f32[4,176,128]{2,1,0:T(8,128)}), f32[4,176,128]{2,1,0:T(8,128)S(1)}, u32[]{:S(2)}, u32[]{:S(2)}) %all-to-all-start.3) | async-done | bytes 360480 | tf_op jit(solution)/shard_map/all_to_all | solution.py:756
  84.6 6.3 %shard_map.70 = f32[59,8192]{1,0:T(8,128)} custom-call(s32[1]{0:T(128)} %bitcast.view_ref, f32[4,176,128]{2,1,0:T(8,128)S(1)} %all-to-all-done.3.arrived_ref, f32[8,520,128]{2,1,0:T(8,128)} %copy-done, f32[8,520,128]{2,1,0:T(8,128)} %copy-done.1), custom_call_target="tpu_custom_call" | custom-call | tf_op jit(solution)/shard_map/pallas_call | solution.py:719
Async XLA Ops:
  0.0 52.0 %copy-start.3 = (f32[1,3,4,256]{3,2,1,0:T(4,128)S(1)}, f32[1,3,4,256]{3,2,1,0:T(4,128)}, u32[]{:S(2)}) copy-start(f32[1,3,4,256]{3,2,1,0:T(4,128)} %cotangent_ref.1) | copy-start | bytes 36868
  0.0 0.7 copy-start.4
  0.7 51.3 %copy-start.6 = (s32[1,4]{1,0:T(1,128)S(1)}, s32[1,4]{1,0:T(1,128)}, u32[]{:S(2)}) copy-start(s32[1,4]{1,0:T(1,128)} %lengths_ref.1) | copy-start | bytes 52
  0.7 51.3 %copy-start.7 = (f32[3]{0:T(128)S(1)}, f32[3]{0:T(128)}, u32[]{:S(2)}) copy-start(f32[3]{0:T(128)} %background_ref.1) | copy-start | bytes 40
  2.0 29.9 %all-to-all-start = ((s32[128,1,128]{2,1,0:T(1,128)}), s32[128,1,128]{2,1,0:T(1,128)S(1)}, u32[]{:S(2)}, u32[]{:S(2)}) async-start(s32[128,1,128]{2,1,0:T(1,128)} %bitcast.3), calls=%async_computation | async-start | bytes 131072 | tf_op jit(solution)/shard_map/all_to_all | solution.py:750
  20.4 1.6 %copy-start.2 = (f32[59,8192]{1,0:T(8,128)S(1)}, f32[59,8192]{1,0:T(8,128)}, u32[]{:S(2)}) copy-start(f32[59,8192]{1,0:T(8,128)} %params_ref.1) | copy-start | bytes 5799940
  22.0 0.7 copy-start.5
  24.3 55.9 %copy-start = (f32[8,520,128]{2,1,0:T(8,128)}, f32[8,520,128]{2,1,0:T(8,128)S(1)}, u32[]{:S(2)}) copy-start(f32[8,520,128]{2,1,0:T(8,128)S(1)} %get-tuple-element.17.held_ref.held_hbm) | copy-start | bytes 6389764
  74.1 10.5 %all-to-all-start.3 = ((f32[4,176,128]{2,1,0:T(8,128)}), f32[4,176,128]{2,1,0:T(8,128)S(1)}, u32[]{:S(2)}, u32[]{:S(2)}) async-start(f32[4,176,128]{2,1,0:T(8,128)} %get-tuple-element.16), calls=%async_computation.3 | async-start | bytes 720896 | tf_op jit(solution)/shard_map/all_to_all | solution.py:756
  80.2 1.3 %copy-start.1 = (f32[8,520,128]{2,1,0:T(8,128)}, f32[8,520,128]{2,1,0:T(8,128)S(1)}, u32[]{:S(2)}) copy-start(f32[8,520,128]{2,1,0:T(8,128)S(1)} %shard_map.69.partial_hbm) | copy-start | bytes 6389764

commit v5 on v4

--- a/solution.py
+++ b/solution.py
@@ -50,7 +50,8 @@
 F32 = jnp.float32
 BF16 = jnp.bfloat16
 VMEM_LIMIT = 16 * 1024 * 1024
-LAST_VMEM_LIMIT = 52 * 1024 * 1024
+ROUTE_VMEM_LIMIT = 60 * 1024 * 1024
+WIDE_VMEM_LIMIT = 52 * 1024 * 1024
 
 
 def iota(shape, axis, dtype=jnp.int32):
@@ -78,7 +79,7 @@
 GEO = 24
 
 
-def write_geometry(height, camera_ref, first_ref, geo_ref):
+def write_geometry(height, camera_ref, geo_ref):
     row = iota((8, LANES), 0)
     block = jnp.zeros((8, LANES), F32)
     for index in range(6):
@@ -100,7 +101,7 @@
         geo_ref[index : index + 1, :] = value
     geo_ref[9:12, :] = block[3:6, :]
     for index in range(TILES_DEV):
-        tile_id = first_ref[0] + index
+        tile_id = lax.axis_index("img") * TILES_DEV + index
         tile_x = ((tile_id % TX * SIDE).astype(F32) + 0.5) * (2.0 / (TX * SIDE)) - 1.0
         tile_y = ((tile_id // TX * SIDE).astype(F32) + 0.5) * (2.0 / (height * SIDE)) - 1.0
         geo_ref[12 + index : 13 + index, :] = jnp.full((1, LANES), tile_x, F32)
@@ -205,24 +206,37 @@
         held_ref[chunk, group * PITCH : group * PITCH + PARAMS, :] = params_ref[:, columns]
 
 
-def project_kernel(height, camera_ref, first_ref, view_ref, params_ref, feats_ref, held_ref, geo_ref, staged_ref, semaphores):
+def each_chunk(action):
+    def body(chunk, carry):
+        action(chunk)
+        return carry
+
+    lax.fori_loop(0, CHUNKS, body, 0)
+
+
+def project_kernel(
+    height, camera_hbm, params_ref, feats_ref, geo_ref, out_ref,
+    staged_ref, held_ref, camera_ref, semaphores, out_semaphores, camera_semaphore,
+):
     def fetch(chunk):
         columns = chunk_columns(chunk)
         return pltpu.make_async_copy(params_ref.at[:, columns], staged_ref.at[:, columns], semaphores.at[chunk])
 
-    def start(chunk, carry):
-        fetch(chunk).start()
-        return carry
-
-    lax.fori_loop(0, CHUNKS, start, 0)
-    write_geometry(height, camera_ref, first_ref, geo_ref)
-    geo_ref[20:21, :] = jnp.full((1, LANES), view_ref[0].astype(F32), F32)
+    def keep(chunk):
+        return pltpu.make_async_copy(held_ref.at[chunk], out_ref.at[chunk], out_semaphores.at[chunk])
+
+    camera_copy = pltpu.make_async_copy(camera_hbm, camera_ref, camera_semaphore)
+    camera_copy.start()
+    each_chunk(lambda chunk: fetch(chunk).start())
+    camera_copy.wait()
+    write_geometry(height, camera_ref, geo_ref)
     rotate, offset = camera_of(geo_ref[...])
     eye = camera_center(rotate, offset)
 
     def step(chunk, carry):
         fetch(chunk).wait()
         spread_columns(staged_ref, held_ref, chunk)
+        keep(chunk).start()
 
         def param(index):
             return held_ref[chunk, pl.ds(index, 8, stride=PITCH), :]
@@ -244,9 +258,12 @@
         return carry
 
     lax.fori_loop(0, CHUNKS, step, 0)
-
-
-def route_kernel(lists_ref, request_ref, aux_ref):
+    each_chunk(lambda chunk: keep(chunk).wait())
+
+
+def route_kernel(lists_hbm, request_ref, aux_ref, lists_ref, semaphore):
+    lists_copy = pltpu.make_async_copy(lists_hbm, lists_ref, semaphore)
+    lists_copy.start()
     owner_iota = iota((OWNERS, LANES), 0)
     before = (iota((LANES, 2 * LANES), 0) < iota((LANES, 2 * LANES), 1)).astype(F32)
     before = before.astype(BF16)
@@ -254,6 +271,7 @@
     lane = iota((1, LANES), 1)
     carried = jnp.zeros((OWNERS, LANES), F32)
     table = jnp.zeros((4 * CAP, OWNERS), F32)
+    lists_copy.wait()
     for row in range(8):
         ids = lists_ref[0, row // 2 : row // 2 + 1, (row % 2) * LANES : (row % 2 + 1) * LANES]
         owner = ids // G_DEV
@@ -512,21 +530,21 @@
     add(10, cotangent(5))
 
 
-def each_chunk(action):
-    def body(chunk, carry):
-        action(chunk)
-        return carry
-
-    lax.fori_loop(0, CHUNKS, body, 0)
-
-
-def own_pullback_kernel(returned_ref, held_ref, out_ref, grads_ref, camera_ref, partial_ref, semaphores):
+def own_pullback_kernel(
+    returned_ref, held_hbm, out_ref, held_ref, grads_ref, camera_ref, partial_ref, held_sems, semaphores
+):
+    def fetch(chunk):
+        return pltpu.make_async_copy(held_hbm.at[chunk], held_ref.at[chunk], held_sems.at[chunk])
+
     def send(chunk):
         return pltpu.make_async_copy(partial_ref.at[chunk], out_ref.at[chunk], semaphores.at[chunk])
 
+    each_chunk(lambda chunk: fetch(chunk).start())
     scatter_view(0, returned_ref, 0, grads_ref, camera_ref)
 
     def step(chunk, carry):
+        fetch(chunk).wait()
+
         def param(index):
             return held_ref[chunk, pl.ds(index, 8, stride=PITCH), :]
 
@@ -544,7 +562,7 @@
 
 
 def pullback_kernel(
-    view_ref, arrived_ref, held_hbm, partial_hbm, out_ref,
+    arrived_ref, held_hbm, partial_hbm, out_ref,
     held_ref, partial_ref, sums_ref, grads_ref, camera_ref, staged_ref, held_sems, partial_sems, semaphores,
 ):
     views = arrived_ref.shape[0]
@@ -562,7 +580,7 @@
     each_chunk(start)
 
     def one_view(place, carry):
-        view = lax.rem(view_ref[0] + 1 + place, views)
+        view = lax.rem(lax.axis_index("view") + 1 + place, views)
         scatter_view(view, arrived_ref, place, grads_ref, camera_ref)
         return carry
 
@@ -632,33 +650,42 @@
 
 
 def route(tile_lists):
-    return call(
+    return pl.pallas_call(
         route_kernel,
-        [
+        out_shape=[
             jax.ShapeDtypeStruct((OWNERS, LANES), jnp.int32),
             jax.ShapeDtypeStruct((16 + 2 * CAP, LANES), jnp.int32),
         ],
-        [tile_lists],
-        smalls=0,
-    )
-
-
-def project(height, camera, first_tile, view, gauss_params):
+        in_specs=[pl.BlockSpec(memory_space=pl.ANY)],
+        out_specs=[pl.BlockSpec(memory_space=pltpu.VMEM)] * 2,
+        scratch_shapes=[
+            pltpu.VMEM(tile_lists.shape, jnp.int32),
+            pltpu.SemaphoreType.DMA,
+        ],
+        compiler_params=pltpu.CompilerParams(vmem_limit_bytes=ROUTE_VMEM_LIMIT),
+    )(tile_lists)
+
+
+def project(height, camera, gauss_params):
     return pl.pallas_call(
         functools.partial(project_kernel, height),
         out_shape=[
             jax.ShapeDtypeStruct((FEATS, GROUPS, LANES), F32),
+            jax.ShapeDtypeStruct((GEO, LANES), F32),
             HELD,
-            jax.ShapeDtypeStruct((GEO, LANES), F32),
-        ],
-        in_specs=[pl.BlockSpec(memory_space=pltpu.SMEM)] * 3 + [pl.BlockSpec(memory_space=pltpu.HBM)],
-        out_specs=[pl.BlockSpec(memory_space=pltpu.VMEM)] * 3,
+        ],
+        in_specs=[pl.BlockSpec(memory_space=pl.ANY)] * 2,
+        out_specs=[pl.BlockSpec(memory_space=space) for space in (pltpu.VMEM, pltpu.VMEM, pl.ANY)],
         scratch_shapes=[
             pltpu.VMEM((PARAMS, G_DEV), F32),
+            pltpu.VMEM(HELD.shape, F32),
+            pltpu.SMEM(camera.shape, F32),
             pltpu.SemaphoreType.DMA((CHUNKS,)),
-        ],
-        compiler_params=pltpu.CompilerParams(vmem_limit_bytes=VMEM_LIMIT),
-    )(camera, first_tile, view, gauss_params)
+            pltpu.SemaphoreType.DMA((CHUNKS,)),
+            pltpu.SemaphoreType.DMA,
+        ],
+        compiler_params=pltpu.CompilerParams(vmem_limit_bytes=WIDE_VMEM_LIMIT),
+    )(camera, gauss_params)
 
 
 def gather(requested, features):
@@ -691,7 +718,7 @@
             jax.ShapeDtypeStruct((views, SENT, LANES), F32),
         ],
         in_specs=[pl.BlockSpec(memory_space=pltpu.VMEM)],
-        out_specs=[pl.BlockSpec(memory_space=pltpu.VMEM), pl.BlockSpec(memory_space=pltpu.HBM)],
+        out_specs=[pl.BlockSpec(memory_space=pltpu.VMEM), pl.BlockSpec(memory_space=pl.ANY)],
         scratch_shapes=[pltpu.SemaphoreType.DMA((views,))],
         compiler_params=pltpu.CompilerParams(vmem_limit_bytes=VMEM_LIMIT),
     )(returned)
@@ -701,28 +728,30 @@
     return pl.pallas_call(
         own_pullback_kernel,
         out_shape=HELD,
-        in_specs=[pl.BlockSpec(memory_space=pltpu.VMEM)] * 2,
-        out_specs=pl.BlockSpec(memory_space=pltpu.HBM),
+        in_specs=[pl.BlockSpec(memory_space=pltpu.VMEM), pl.BlockSpec(memory_space=pl.ANY)],
+        out_specs=pl.BlockSpec(memory_space=pl.ANY),
         scratch_shapes=[
+            pltpu.VMEM(HELD.shape, F32),
             pltpu.VMEM((1, FEATS * GROUPS, LANES), F32),
             pltpu.VMEM((1, 16, LANES), F32),
             pltpu.VMEM(HELD.shape, F32),
             pltpu.SemaphoreType.DMA((CHUNKS,)),
-        ],
-        compiler_params=pltpu.CompilerParams(vmem_limit_bytes=VMEM_LIMIT),
+            pltpu.SemaphoreType.DMA((CHUNKS,)),
+        ],
+        compiler_params=pltpu.CompilerParams(vmem_limit_bytes=WIDE_VMEM_LIMIT),
         cost_estimate=pl.CostEstimate(flops=20_000_000, bytes_accessed=4_000_000, transcendentals=0),
     )(own.reshape((1,) + own.shape), held)
 
 
-def pullback(view, arrived, held, partial):
+def pullback(arrived, held, partial):
     others = arrived.shape[0] - 1
     return pl.pallas_call(
         pullback_kernel,
         out_shape=jax.ShapeDtypeStruct((PARAMS, G_DEV), F32),
         in_specs=[
-            pl.BlockSpec(memory_space=space) for space in (pltpu.SMEM, pltpu.VMEM, pltpu.HBM, pltpu.HBM)
-        ],
-        out_specs=pl.BlockSpec(memory_space=pltpu.HBM),
+            pl.BlockSpec(memory_space=space) for space in (pltpu.VMEM, pl.ANY, pl.ANY)
+        ],
+        out_specs=pl.BlockSpec(memory_space=pl.ANY),
         scratch_shapes=[
             pltpu.VMEM(HELD.shape, F32),
             pltpu.VMEM(HELD.shape, F32),
@@ -734,8 +763,8 @@
             pltpu.SemaphoreType.DMA((CHUNKS,)),
             pltpu.SemaphoreType.DMA((CHUNKS,)),
         ],
-        compiler_params=pltpu.CompilerParams(vmem_limit_bytes=LAST_VMEM_LIMIT),
-    )(view, arrived, held, partial)
+        compiler_params=pltpu.CompilerParams(vmem_limit_bytes=WIDE_VMEM_LIMIT),
+    )(arrived, held, partial)
 
 
 def per_device(gauss_params, camera, background, tile_lists, tile_lengths, pixel_cotangent):
@@ -743,10 +772,8 @@
     views = lax.axis_size("view")
     tiles_here = tile_lists.shape[1]
     height = tiles_here * owners_total // TX
-    first_tile = (lax.axis_index("img") * tiles_here).astype(jnp.int32).reshape(1)
-    view = lax.axis_index("view").astype(jnp.int32).reshape(1)
     requests, aux = route(tile_lists)
-    features, held, geometry = project(height, camera, first_tile, view, gauss_params)
+    features, geometry, held = project(height, camera, gauss_params)
     requested = lax.all_to_all(requests, "img", split_axis=0, concat_axis=0, tiled=True)
     outgoing = gather(requested, features)
     arrived = lax.all_to_all(outgoing, "img", split_axis=0, concat_axis=0, tiled=True)
@@ -755,7 +782,7 @@
     own, copies = duplicate(returned, views)
     everyone = lax.all_to_all(copies, "view", split_axis=0, concat_axis=0, tiled=True)
     partial = own_pullback(own, held)
-    return pullback(view, everyone, held, partial)
+    return pullback(everyone, held, partial)
 
 
 def solution(mesh):

time: 91.2 us -> 90.7 us (level)
  local copies, waits for them, and re-layouts: 4.28 us -> 0.67 us
  Pallas kernels: 17.2 us -> 19.4 us
  waiting for transfers between devices: 10.6 us -> 12 us
    unnamed x16 -> x10, local copies, waits for them, and re-layouts: 4.28 us -> 0.67 us
    pallas_call x0 -> x1, Pallas kernels: none -> 1.99 us  [route(): pl.pallas_call(route_kernel, out_shape=[jax.ShapeDtypeStruct((OWNERS, LAN...]
    pallas_call x3 -> x2, Pallas kernels: 6.29 us -> 5.03 us  [call(): pl.pallas_call(kernel, out_shape=out_shape, in_specs=[pl.BlockSpec(memory...]
  transfers between devices with their start and end apart: 2 -> 2, of which waited for: 2 -> 2; matrix products, arithmetic and copies ran while one was open for 0% -> 0% of each run, Pallas kernels for 4% -> 6%
where the time goes in v5:
time: 90.7 us; the launch traced here: 90.2 us
  blocking collectives  35.6 us (39%)
  starting transfers between devices  22.5 us (25%)
  Pallas kernels  19.4 us (21%)
  waiting for transfers between devices  12 us (13%)
    all_to_all x1, starting transfers between devices, per_device(): lax.all_to_all(requests, 'img', split_axis=0, concat_axis=0, tiled=True)  18.4 us
    all_to_all x1, blocking collectives, per_device(): lax.all_to_all(slot_grads, 'img', split_axis=0, concat_axis=0, tiled=True)  17.9 us
    all_to_all x1, blocking collectives, per_device(): lax.all_to_all(outgoing, 'img', split_axis=0, concat_axis=0, tiled=True)  17.7 us
    all_to_all x1, waiting for transfers between devices, per_device(): lax.all_to_all(requests, 'img', split_axis=0, concat_axis=0, tiled=True)  8.28 us
    pallas_call x1, Pallas kernels, pullback(): pl.pallas_call(pullback_kernel, out_shape=jax.ShapeDtypeStruct((PARAMS, G...  6.32 us
    pallas_call x2, Pallas kernels, call(): pl.pallas_call(kernel, out_shape=out_shape, in_specs=[pl.BlockSpec(memory...  5.03 us
    all_to_all x1, starting transfers between devices, per_device(): lax.all_to_all(copies, 'view', split_axis=0, concat_axis=0, tiled=True)  4.02 us
    all_to_all x1, waiting for transfers between devices, per_device(): lax.all_to_all(copies, 'view', split_axis=0, concat_axis=0, tiled=True)  3.7 us
  transfers between devices with their start and end apart: 2, of which 2 were waited for; matrix products, arithmetic and copies ran while one was open for 0% of the time, Pallas kernels for 6%

profile of v5, /device:TPU:1, one launch (start us, length us, event | category | flops | bytes accessed | tf_op | source)
XLA Modules:
  0.0 90.2 jit_solution(16407108871236527441)
XLA Ops:
  0.0 0.0 copy-start.1
  0.0 0.0 copy-start.3
  0.0 0.0 copy-start.4
  0.0 2.0 %shard_map.65 = (s32[128,128]{1,0:T(8,128)}, s32[48,128]{1,0:T(8,128)}) custom-call(s32[1,4,256]{2,1,0:T(4,128)} %lists_hbm.1), custom_call_target="tpu_custom_call" | custom-call | tf_op jit(solution)/shard_map/pallas_call | solution.py:653
  2.0 0.0 copy-start
  2.0 18.4 %all-to-all-start = ((s32[128,1,128]{2,1,0:T(1,128)}), s32[128,1,128]{2,1,0:T(1,128)S(1)}, u32[]{:S(2)}, u32[]{:S(2)}) async-start(s32[128,1,128]{2,1,0:T(1,128)} %bitcast.15), calls=%async_computation | async-start | bytes 131072 | tf_op jit(solution)/shard_map/all_to_all | solution.py:777
  20.5 0.0 copy-start.2
  20.5 0.6 copy-done.2
  21.1 2.5 %shard_map.64 = (f32[9,64,128]{2,1,0:T(8,128)S(1)}, f32[24,128]{1,0:T(8,128)S(1)}, f32[8,520,128]{2,1,0:T(8,128)}) custom-call(f32[1,6]{1,0:T(1,128)S(1)} %copy-done.2, f32[59,8192]{1,0:T(8,128)} %params_ref.1), custom_call_target="tpu_custom_call" | custom-call | tf_op jit(solution)/shard_map/pallas_call | solution.py:670
  23.6 8.3 %all-to-all-done = s32[128,1,128]{2,1,0:T(1,128)S(1)} async-done(((s32[128,1,128]{2,1,0:T(1,128)}), s32[128,1,128]{2,1,0:T(1,128)S(1)}, u32[]{:S(2)}, u32[]{:S(2)}) %all-to-all-start) | async-done | bytes 65568 | tf_op jit(solution)/shard_map/all_to_all | solution.py:777
  31.9 1.7 %shard_map.66 = f32[256,128]{1,0:T(8,128)S(1)} custom-call(s32[128,128]{1,0:T(8,128)S(1)} %bitcast.13, f32[9,64,128]{2,1,0:T(8,128)S(1)} %get-tuple-element.14.feats_ref), custom_call_target="tpu_custom_call" | custom-call | tf_op jit(solution)/shard_map/pallas_call | solution.py:638
  33.6 17.7 %all_to_all.38 = f32[128,2,128]{2,1,0:T(2,128)S(1)} all-to-all(f32[128,2,128]{2,1,0:T(2,128)S(1)} %bitcast.12), channel_id=1, replica_groups=mesh['img'=128,'view'=4] {'img'}, dimensions={0} | all-to-all | bytes 262144 | tf_op jit(solution)/shard_map/all_to_all | solution.py:779
  51.3 0.0 copy-done.1
  51.3 0.0 copy-done.3
  51.4 0.0 copy-done.4
  51.4 0.0 copy-done
  51.4 3.3 %shard_map.67 = f32[256,128]{1,0:T(8,128)S(1)} custom-call(s32[1,4]{1,0:T(1,128)S(1)} %copy-done.3, f32[3]{0:T(128)S(1)} %copy-done.4, f32[24,128]{1,0:T(8,128)S(1)} %get-tuple-element.12.geo_ref, f32[256,128]{1,0:T(8,128)S(1)} %bitcast.9, s32[48,128]{1,0:T(8,128)S(1)} %copy-done, f32[1,3,4,256]{3,2,1,0:T(4,128)S(1)} %copy-done.1), custom_call_target="tpu_custom_call" | custom-call | tf_op jit(solution)/shard_map/pallas_call | solution.py:638
  54.7 17.9 %all_to_all.39 = f32[128,2,128]{2,1,0:T(2,128)S(1)} all-to-all(f32[128,2,128]{2,1,0:T(2,128)S(1)} %bitcast.10), channel_id=1, replica_groups=mesh['img'=128,'view'=4] {'img'}, dimensions={0} | all-to-all | bytes 262144 | tf_op jit(solution)/shard_map/all_to_all | solution.py:781
  72.6 0.9 shard_map.68
  73.4 4.0 %all-to-all-start.3 = ((f32[4,176,128]{2,1,0:T(8,128)}), f32[4,176,128]{2,1,0:T(8,128)S(1)}, u32[]{:S(2)}, u32[]{:S(2)}) async-start(f32[4,176,128]{2,1,0:T(8,128)} %get-tuple-element.16), calls=%async_computation.3 | async-start | bytes 720896 | tf_op jit(solution)/shard_map/all_to_all | solution.py:783
  77.5 2.7 %shard_map.69.partial_hbm = f32[8,520,128]{2,1,0:T(8,128)} custom-call(f32[1,176,128]{2,1,0:T(8,128)S(1)} %bitcast.14, f32[8,520,128]{2,1,0:T(8,128)} %get-tuple-element.17.held_hbm), custom_call_target="tpu_custom_call" | custom-call | flops 20000000 | bytes 4000000 | tf_op jit(solution)/shard_map/pallas_call | solution.py:728
  80.2 3.7 %all-to-all-done.3.arrived_ref = f32[4,176,128]{2,1,0:T(8,128)S(1)} async-done(((f32[4,176,128]{2,1,0:T(8,128)}), f32[4,176,128]{2,1,0:T(8,128)S(1)}, u32[]{:S(2)}, u32[]{:S(2)}) %all-to-all-start.3) | async-done | bytes 360480 | tf_op jit(solution)/shard_map/all_to_all | solution.py:783
  83.9 6.3 %shard_map.70 = f32[59,8192]{1,0:T(8,128)} custom-call(f32[4,176,128]{2,1,0:T(8,128)S(1)} %all-to-all-done.3.arrived_ref, f32[8,520,128]{2,1,0:T(8,128)} %get-tuple-element.17.held_hbm, f32[8,520,128]{2,1,0:T(8,128)} %shard_map.69.partial_hbm), custom_call_target="tpu_custom_call" | custom-call | tf_op jit(solution)/shard_map/pallas_call | solution.py:748
Async XLA Ops:
  0.0 51.3 %copy-start.1 = (f32[1,3,4,256]{3,2,1,0:T(4,128)S(1)}, f32[1,3,4,256]{3,2,1,0:T(4,128)}, u32[]{:S(2)}) copy-start(f32[1,3,4,256]{3,2,1,0:T(4,128)} %cotangent_ref.1) | copy-start | bytes 36868
  0.0 51.3 %copy-start.3 = (s32[1,4]{1,0:T(1,128)S(1)}, s32[1,4]{1,0:T(1,128)}, u32[]{:S(2)}) copy-start(s32[1,4]{1,0:T(1,128)} %lengths_ref.1) | copy-start | bytes 52
  0.0 51.3 %copy-start.4 = (f32[3]{0:T(128)S(1)}, f32[3]{0:T(128)}, u32[]{:S(2)}) copy-start(f32[3]{0:T(128)} %background_ref.1) | copy-start | bytes 40
  2.0 49.4 %copy-start = (s32[48,128]{1,0:T(8,128)S(1)}, s32[48,128]{1,0:T(8,128)}, u32[]{:S(2)}) copy-start(s32[48,128]{1,0:T(8,128)} %get-tuple-element.15.aux_ref) | copy-start | bytes 73732
  2.0 29.9 %all-to-all-start = ((s32[128,1,128]{2,1,0:T(1,128)}), s32[128,1,128]{2,1,0:T(1,128)S(1)}, u32[]{:S(2)}, u32[]{:S(2)}) async-start(s32[128,1,128]{2,1,0:T(1,128)} %bitcast.15), calls=%async_computation | async-start | bytes 131072 | tf_op jit(solution)/shard_map/all_to_all | solution.py:777
  20.5 0.7 copy-start.2
  73.4 10.5 %all-to-all-start.3 = ((f32[4,176,128]{2,1,0:T(8,128)}), f32[4,176,128]{2,1,0:T(8,128)S(1)}, u32[]{:S(2)}, u32[]{:S(2)}) async-start(f32[4,176,128]{2,1,0:T(8,128)} %get-tuple-element.16), calls=%async_computation.3 | async-start | bytes 720896 | tf_op jit(solution)/shard_map/all_to_all | solution.py:783

commit v6 on v5

--- a/solution.py
+++ b/solution.py
@@ -325,24 +325,64 @@
     out_ref[pl.ds(1, LANES, stride=2), :] = table[LANES:].T
 
 
-def gather_kernel(request_ref, feats_ref, out_ref):
+WIDE = 256
+TALL = G_DEV // WIDE
+EXACT = 2
+
+
+def split(values, parts):
+    pieces = []
+    for _ in range(parts):
+        piece = values.astype(BF16)
+        pieces.append(piece)
+        values = values - piece.astype(F32)
+    return pieces
+
+
+def gather_kernel(request_ref, feats_ref, out_ref, table_ref):
     wanted = request_ref[...].astype(F32).T[:CAP].astype(jnp.int32)
     high, low = wanted >> 7, wanted & (LANES - 1)
     parts = [(high[:8], low[:8]), (high[8:], low[8:])]
-
-    def step(group, found):
-        found = list(found)
-        for index in range(FEATS):
-            row = feats_ref[index, pl.ds(group, 1), :]
-            for part, (at_group, at_lane) in enumerate(parts):
-                place = 2 * index + part
-                found[place] = jnp.where(at_group == group, pick(row, at_lane), found[place])
-        return tuple(found)
-
-    start = tuple(jnp.zeros((8, LANES), F32) for _ in range(2 * FEATS))
-    found = lax.fori_loop(0, GROUPS, step, start, unroll=16)
-    table = jnp.concatenate(list(found) + [jnp.zeros((PACK - FEATS * CAP, LANES), F32)], axis=0)
-    store_rows(out_ref, table)
+    high_place, low_place = wanted >> 8, wanted & (WIDE - 1)
+    tall_iota, wide_iota = iota((TALL, LANES), 0), iota((WIDE, LANES), 0)
+
+    pieces, counts = [], []
+    for index in range(EXACT, FEATS):
+        wide = jnp.concatenate(
+            [feats_ref[index, pl.ds(half, TALL, stride=2), :] for half in range(2)], axis=1
+        )
+        counts.append(3 if index < 5 else 2)
+        pieces += split(wide, counts[-1])
+    left = jnp.concatenate(pieces, axis=0)
+
+    found = [jnp.zeros((8, LANES), F32) for _ in range(2 * EXACT)]
+    for pair in range(CAP // 2):
+        rights = []
+        for rank in (2 * pair, 2 * pair + 1):
+            at_low = wide_iota == spread(low_place[rank : rank + 1], (WIDE, LANES))
+            rights.append(at_low.astype(F32).astype(BF16))
+        product = dot(left, jnp.concatenate(rights, axis=1))
+        for group in range(pair * (GROUPS // 8), (pair + 1) * (GROUPS // 8)):
+            for index in range(EXACT):
+                row = feats_ref[index, group : group + 1, :]
+                for part, (at_group, at_lane) in enumerate(parts):
+                    place = 2 * index + part
+                    found[place] = jnp.where(at_group == group, pick(row, at_lane), found[place])
+        for half, rank in enumerate((2 * pair, 2 * pair + 1)):
+            at_high = tall_iota == spread(high_place[rank : rank + 1], (TALL, LANES))
+            lanes = slice(half * LANES, (half + 1) * LANES)
+            first = 0
+            for index, count in enumerate(counts):
+                total = product[first : first + TALL, lanes]
+                for piece in range(1, count):
+                    total = total + product[first + piece * TALL : first + (piece + 1) * TALL, lanes]
+                first += count * TALL
+                value = jnp.sum(jnp.where(at_high, total, 0.0), axis=0, keepdims=True)
+                place = (EXACT + index) * CAP + rank
+                table_ref[place : place + 1, :] = value
+    table_ref[: EXACT * CAP, :] = jnp.concatenate(found, axis=0)
+    table_ref[FEATS * CAP :, :] = jnp.zeros((PACK - FEATS * CAP, LANES), F32)
+    store_rows(out_ref, table_ref[...])
 
 
 PIX_CHUNK = 128
@@ -452,10 +492,6 @@
     store_rows(out_ref, jnp.concatenate(blocks, axis=0))
 
 
-WIDE = 256
-TALL = G_DEV // WIDE
-
-
 def duplicate_kernel(returned_ref, own_ref, copies_ref, semaphores):
     own_ref[:LANES, :] = returned_ref[pl.ds(0, LANES, stride=2), :].T
     own_ref[LANES:, :] = returned_ref[pl.ds(1, LANES, stride=2), :].T[: SENT - LANES]
@@ -584,7 +620,7 @@
         scatter_view(view, arrived_ref, place, grads_ref, camera_ref)
         return carry
 
-    lax.fori_loop(0, views - 1, one_view, 0)
+    lax.fori_loop(0, views - 1, one_view, 0, unroll=True)
 
     def send(chunk):
         columns = chunk_columns(chunk)
@@ -690,7 +726,11 @@
 
 def gather(requested, features):
     return call(
-        gather_kernel, jax.ShapeDtypeStruct((2 * OWNERS, LANES), F32), [requested, features], smalls=0
+        gather_kernel,
+        jax.ShapeDtypeStruct((2 * OWNERS, LANES), F32),
+        [requested, features],
+        smalls=0,
+        scratch=[pltpu.VMEM((PACK, LANES), F32)],
     )
 
 

time: 90.7 us -> 89.7 us (0.989)
  Pallas kernels: 19.4 us -> 18.4 us
where the time goes in v6:
time: 89.7 us; the launch traced here: 89.3 us
  blocking collectives  35.6 us (40%)
  starting transfers between devices  22.5 us (25%)
  Pallas kernels  18.4 us (21%)
  waiting for transfers between devices  12 us (13%)
    all_to_all x1, starting transfers between devices, per_device(): lax.all_to_all(requests, 'img', split_axis=0, concat_axis=0, tiled=True)  18.4 us
    all_to_all x1, blocking collectives, per_device(): lax.all_to_all(slot_grads, 'img', split_axis=0, concat_axis=0, tiled=True)  17.9 us
    all_to_all x1, blocking collectives, per_device(): lax.all_to_all(outgoing, 'img', split_axis=0, concat_axis=0, tiled=True)  17.7 us
    all_to_all x1, waiting for transfers between devices, per_device(): lax.all_to_all(requests, 'img', split_axis=0, concat_axis=0, tiled=True)  8.28 us
    pallas_call x1, Pallas kernels, pullback(): pl.pallas_call(pullback_kernel, out_shape=jax.ShapeDtypeStruct((PARAMS, G...  5.88 us
    pallas_call x2, Pallas kernels, call(): pl.pallas_call(kernel, out_shape=out_shape, in_specs=[pl.BlockSpec(memory...  4.39 us
    all_to_all x1, starting transfers between devices, per_device(): lax.all_to_all(copies, 'view', split_axis=0, concat_axis=0, tiled=True)  4.03 us
    all_to_all x1, waiting for transfers between devices, per_device(): lax.all_to_all(copies, 'view', split_axis=0, concat_axis=0, tiled=True)  3.7 us
  transfers between devices with their start and end apart: 2, of which 2 were waited for; matrix products, arithmetic and copies ran while one was open for 0% of the time, Pallas kernels for 6%

profile of v6, /device:TPU:1, one launch (start us, length us, event | category | flops | bytes accessed | tf_op | source)
XLA Modules:
  0.0 89.3 jit_solution(9362472828240365499)
XLA Ops:
  0.0 0.0 copy-start.1
  0.0 0.0 copy-start.3
  0.0 0.0 copy-start.4
  0.0 2.0 %shard_map.65 = (s32[128,128]{1,0:T(8,128)}, s32[48,128]{1,0:T(8,128)}) custom-call(s32[1,4,256]{2,1,0:T(4,128)} %lists_hbm.1), custom_call_target="tpu_custom_call" | custom-call | tf_op jit(solution)/shard_map/pallas_call | solution.py:689
  2.0 0.0 copy-start
  2.0 18.4 %all-to-all-start = ((s32[128,1,128]{2,1,0:T(1,128)}), s32[128,1,128]{2,1,0:T(1,128)S(1)}, u32[]{:S(2)}, u32[]{:S(2)}) async-start(s32[128,1,128]{2,1,0:T(1,128)} %bitcast.15), calls=%async_computation | async-start | bytes 131072 | tf_op jit(solution)/shard_map/all_to_all | solution.py:817
  20.5 0.0 copy-start.2
  20.5 0.6 copy-done.2
  21.1 2.5 %shard_map.64 = (f32[9,64,128]{2,1,0:T(8,128)S(1)}, f32[24,128]{1,0:T(8,128)S(1)}, f32[8,520,128]{2,1,0:T(8,128)}) custom-call(f32[1,6]{1,0:T(1,128)S(1)} %copy-done.2, f32[59,8192]{1,0:T(8,128)} %params_ref.1), custom_call_target="tpu_custom_call" | custom-call | tf_op jit(solution)/shard_map/pallas_call | solution.py:706
  23.6 8.3 %all-to-all-done = s32[128,1,128]{2,1,0:T(1,128)S(1)} async-done(((s32[128,1,128]{2,1,0:T(1,128)}), s32[128,1,128]{2,1,0:T(1,128)S(1)}, u32[]{:S(2)}, u32[]{:S(2)}) %all-to-all-start) | async-done | bytes 65568 | tf_op jit(solution)/shard_map/all_to_all | solution.py:817
  31.9 1.1 %shard_map.66 = f32[256,128]{1,0:T(8,128)S(1)} custom-call(s32[128,128]{1,0:T(8,128)S(1)} %bitcast.13, f32[9,64,128]{2,1,0:T(8,128)S(1)} %get-tuple-element.14.feats_ref), custom_call_target="tpu_custom_call" | custom-call | tf_op jit(solution)/shard_map/pallas_call | solution.py:674
  33.0 17.7 %all_to_all.38 = f32[128,2,128]{2,1,0:T(2,128)S(1)} all-to-all(f32[128,2,128]{2,1,0:T(2,128)S(1)} %bitcast.12), channel_id=1, replica_groups=mesh['img'=128,'view'=4] {'img'}, dimensions={0} | all-to-all | bytes 262144 | tf_op jit(solution)/shard_map/all_to_all | solution.py:819
  50.7 0.0 copy-done.1
  50.7 0.0 copy-done.3
  50.7 0.0 copy-done.4
  50.7 0.0 copy-done
  50.7 3.3 %shard_map.67 = f32[256,128]{1,0:T(8,128)S(1)} custom-call(s32[1,4]{1,0:T(1,128)S(1)} %copy-done.3, f32[3]{0:T(128)S(1)} %copy-done.4, f32[24,128]{1,0:T(8,128)S(1)} %get-tuple-element.12.geo_ref, f32[256,128]{1,0:T(8,128)S(1)} %bitcast.9, s32[48,128]{1,0:T(8,128)S(1)} %copy-done, f32[1,3,4,256]{3,2,1,0:T(4,128)S(1)} %copy-done.1), custom_call_target="tpu_custom_call" | custom-call | tf_op jit(solution)/shard_map/pallas_call | solution.py:674
  54.1 17.9 %all_to_all.39 = f32[128,2,128]{2,1,0:T(2,128)S(1)} all-to-all(f32[128,2,128]{2,1,0:T(2,128)S(1)} %bitcast.10), channel_id=1, replica_groups=mesh['img'=128,'view'=4] {'img'}, dimensions={0} | all-to-all | bytes 262144 | tf_op jit(solution)/shard_map/all_to_all | solution.py:821
  71.9 0.9 shard_map.68
  72.8 4.0 %all-to-all-start.3 = ((f32[4,176,128]{2,1,0:T(8,128)}), f32[4,176,128]{2,1,0:T(8,128)S(1)}, u32[]{:S(2)}, u32[]{:S(2)}) async-start(f32[4,176,128]{2,1,0:T(8,128)} %get-tuple-element.16), calls=%async_computation.3 | async-start | bytes 720896 | tf_op jit(solution)/shard_map/all_to_all | solution.py:823
  76.8 2.7 %shard_map.69.partial_hbm = f32[8,520,128]{2,1,0:T(8,128)} custom-call(f32[1,176,128]{2,1,0:T(8,128)S(1)} %bitcast.14, f32[8,520,128]{2,1,0:T(8,128)} %get-tuple-element.17.held_hbm), custom_call_target="tpu_custom_call" | custom-call | flops 20000000 | bytes 4000000 | tf_op jit(solution)/shard_map/pallas_call | solution.py:768
  79.6 3.7 %all-to-all-done.3.arrived_ref = f32[4,176,128]{2,1,0:T(8,128)S(1)} async-done(((f32[4,176,128]{2,1,0:T(8,128)}), f32[4,176,128]{2,1,0:T(8,128)S(1)}, u32[]{:S(2)}, u32[]{:S(2)}) %all-to-all-start.3) | async-done | bytes 360480 | tf_op jit(solution)/shard_map/all_to_all | solution.py:823
  83.3 5.9 %shard_map.70 = f32[59,8192]{1,0:T(8,128)} custom-call(f32[4,176,128]{2,1,0:T(8,128)S(1)} %all-to-all-done.3.arrived_ref, f32[8,520,128]{2,1,0:T(8,128)} %get-tuple-element.17.held_hbm, f32[8,520,128]{2,1,0:T(8,128)} %shard_map.69.partial_hbm), custom_call_target="tpu_custom_call" | custom-call | tf_op jit(solution)/shard_map/pallas_call | solution.py:788
Async XLA Ops:
  0.0 50.7 %copy-start.1 = (f32[1,3,4,256]{3,2,1,0:T(4,128)S(1)}, f32[1,3,4,256]{3,2,1,0:T(4,128)}, u32[]{:S(2)}) copy-start(f32[1,3,4,256]{3,2,1,0:T(4,128)} %cotangent_ref.1) | copy-start | bytes 36868
  0.0 50.7 %copy-start.3 = (s32[1,4]{1,0:T(1,128)S(1)}, s32[1,4]{1,0:T(1,128)}, u32[]{:S(2)}) copy-start(s32[1,4]{1,0:T(1,128)} %lengths_ref.1) | copy-start | bytes 52
  0.0 50.7 %copy-start.4 = (f32[3]{0:T(128)S(1)}, f32[3]{0:T(128)}, u32[]{:S(2)}) copy-start(f32[3]{0:T(128)} %background_ref.1) | copy-start | bytes 40
  2.0 48.7 %copy-start = (s32[48,128]{1,0:T(8,128)S(1)}, s32[48,128]{1,0:T(8,128)}, u32[]{:S(2)}) copy-start(s32[48,128]{1,0:T(8,128)} %get-tuple-element.15.aux_ref) | copy-start | bytes 73732
  2.0 29.9 %all-to-all-start = ((s32[128,1,128]{2,1,0:T(1,128)}), s32[128,1,128]{2,1,0:T(1,128)S(1)}, u32[]{:S(2)}, u32[]{:S(2)}) async-start(s32[128,1,128]{2,1,0:T(1,128)} %bitcast.15), calls=%async_computation | async-start | bytes 131072 | tf_op jit(solution)/shard_map/all_to_all | solution.py:817
  20.5 0.7 copy-start.2
  72.8 10.5 %all-to-all-start.3 = ((f32[4,176,128]{2,1,0:T(8,128)}), f32[4,176,128]{2,1,0:T(8,128)S(1)}, u32[]{:S(2)}, u32[]{:S(2)}) async-start(f32[4,176,128]{2,1,0:T(8,128)} %get-tuple-element.16), calls=%async_computation.3 | async-start | bytes 720896 | tf_op jit(solution)/shard_map/all_to_all | solution.py:823

commit v7 on v6

--- a/solution.py
+++ b/solution.py
@@ -109,8 +109,8 @@
     geo_ref[20:GEO, :] = jnp.zeros((GEO - 20, LANES), F32)
 
 
-def camera_of(geo):
-    entries = [spread(geo[index : index + 1, :], (8, LANES)) for index in range(12)]
+def camera_of(geo, rows=8):
+    entries = [spread(geo[index : index + 1, :], (rows, LANES)) for index in range(12)]
     return [entries[0:3], entries[3:6], entries[6:9]], entries[9:12]
 
 
@@ -215,15 +215,11 @@
 
 
 def project_kernel(
-    height, camera_hbm, params_ref, feats_ref, geo_ref, out_ref,
-    staged_ref, held_ref, camera_ref, semaphores, out_semaphores, camera_semaphore,
+    height, camera_hbm, params_ref, feats_ref, geo_ref, staged_ref, held_ref, camera_ref, semaphores, camera_semaphore
 ):
     def fetch(chunk):
         columns = chunk_columns(chunk)
         return pltpu.make_async_copy(params_ref.at[:, columns], staged_ref.at[:, columns], semaphores.at[chunk])
-
-    def keep(chunk):
-        return pltpu.make_async_copy(held_ref.at[chunk], out_ref.at[chunk], out_semaphores.at[chunk])
 
     camera_copy = pltpu.make_async_copy(camera_hbm, camera_ref, camera_semaphore)
     camera_copy.start()
@@ -236,7 +232,6 @@
     def step(chunk, carry):
         fetch(chunk).wait()
         spread_columns(staged_ref, held_ref, chunk)
-        keep(chunk).start()
 
         def param(index):
             return held_ref[chunk, pl.ds(index, 8, stride=PITCH), :]
@@ -258,7 +253,6 @@
         return carry
 
     lax.fori_loop(0, CHUNKS, step, 0)
-    each_chunk(lambda chunk: keep(chunk).wait())
 
 
 def route_kernel(lists_hbm, request_ref, aux_ref, lists_ref, semaphore):
@@ -532,15 +526,27 @@
 SHAPE_ROWS = (3, 4, 5, 6, 7, 8, 9, 59, 60)
 
 
+def read_chunks(ref, block, index):
+    return jnp.concatenate(
+        [ref[block * WIDTH + part, pl.ds(index, 8, stride=PITCH), :] for part in range(WIDTH)], axis=0
+    )
+
+
+def write_chunks(ref, block, index, value):
+    for part in range(WIDTH):
+        ref[block * WIDTH + part, pl.ds(index, 8, stride=PITCH), :] = value[8 * part : 8 * part + 8]
+
+
 def pull_view(chunk, place, center, shape, param, grads_ref, camera_ref, kept, keep):
     def cotangent(feature):
-        return grads_ref[place, pl.ds(pl.multiple_of(feature * GROUPS + chunk * 8, 8), 8), :]
+        rows = 8 * WIDTH
+        return grads_ref[place, pl.ds(pl.multiple_of(feature * GROUPS + chunk * rows, rows), rows), :]
 
     def add(index, value):
         before = kept(index)
         keep(index, value if before is None else before + value)
 
-    rotate, offset = camera_of(camera_ref[place])
+    rotate, offset = camera_of(camera_ref[place], 8 * WIDTH)
     eye = camera_center(rotate, offset)
     basis, basis_back = jax.vjp(lambda spot: direction_basis(spot, eye), center)
     colors = [cotangent(6 + channel) for channel in range(3)]
@@ -567,10 +573,15 @@
 
 
 def own_pullback_kernel(
-    returned_ref, held_hbm, out_ref, held_ref, grads_ref, camera_ref, partial_ref, held_sems, semaphores
+    returned_ref, params_ref, out_ref, held_hbm,
+    staged_ref, held_ref, grads_ref, camera_ref, partial_ref, fetch_sems, held_sems, semaphores,
 ):
     def fetch(chunk):
-        return pltpu.make_async_copy(held_hbm.at[chunk], held_ref.at[chunk], held_sems.at[chunk])
+        columns = chunk_columns(chunk)
+        return pltpu.make_async_copy(params_ref.at[:, columns], staged_ref.at[:, columns], fetch_sems.at[chunk])
+
+    def hold(chunk):
+        return pltpu.make_async_copy(held_ref.at[chunk], held_hbm.at[chunk], held_sems.at[chunk])
 
     def send(chunk):
         return pltpu.make_async_copy(partial_ref.at[chunk], out_ref.at[chunk], semaphores.at[chunk])
@@ -578,28 +589,34 @@
     each_chunk(lambda chunk: fetch(chunk).start())
     scatter_view(0, returned_ref, 0, grads_ref, camera_ref)
 
-    def step(chunk, carry):
-        fetch(chunk).wait()
+    def step(block, carry):
+        for part in range(WIDTH):
+            chunk = block * WIDTH + part
+            fetch(chunk).wait()
+            spread_columns(staged_ref, held_ref, chunk)
+            hold(chunk).start()
 
         def param(index):
-            return held_ref[chunk, pl.ds(index, 8, stride=PITCH), :]
+            return read_chunks(held_ref, block, index)
 
         def keep(index, value):
-            partial_ref[chunk, pl.ds(index, 8, stride=PITCH), :] = value
+            write_chunks(partial_ref, block, index, value)
 
         center = [param(index) for index in range(3)]
         shape = shape_matrix([param(3 + index) for index in range(3)], [param(6 + index) for index in range(4)])
-        pull_view(chunk, 0, center, shape, param, grads_ref, camera_ref, lambda index: None, keep)
-        send(chunk).start()
+        pull_view(block, 0, center, shape, param, grads_ref, camera_ref, lambda index: None, keep)
+        for part in range(WIDTH):
+            send(block * WIDTH + part).start()
         return carry
 
-    lax.fori_loop(0, CHUNKS, step, 0)
+    lax.fori_loop(0, CHUNKS // WIDTH, step, 0)
     each_chunk(lambda chunk: send(chunk).wait())
+    each_chunk(lambda chunk: hold(chunk).wait())
 
 
 def pullback_kernel(
     arrived_ref, held_hbm, partial_hbm, out_ref,
-    held_ref, partial_ref, sums_ref, grads_ref, camera_ref, staged_ref, held_sems, partial_sems, semaphores,
+    held_ref, partial_ref, grads_ref, camera_ref, staged_ref, held_sems, partial_sems, semaphores,
 ):
     views = arrived_ref.shape[0]
 
@@ -626,30 +643,26 @@
         columns = chunk_columns(chunk)
         return pltpu.make_async_copy(staged_ref.at[:, columns], out_ref.at[:, columns], semaphores.at[chunk])
 
-    def step(chunk, carry):
-        fetch_held(chunk).wait()
-        fetch_partial(chunk).wait()
+    def step(block, carry):
+        for part in range(WIDTH):
+            fetch_held(block * WIDTH + part).wait()
+            fetch_partial(block * WIDTH + part).wait()
 
         def param(index):
-            return held_ref[chunk, pl.ds(index, 8, stride=PITCH), :]
-
-        def first(index):
-            return partial_ref[chunk, pl.ds(index, 8, stride=PITCH), :]
+            return read_chunks(held_ref, block, index)
 
         def keep(index, value):
-            sums_ref[pl.ds(index, 8, stride=PITCH), :] = value
+            write_chunks(partial_ref, block, index, value)
 
         def kept(index):
-            return sums_ref[pl.ds(index, 8, stride=PITCH), :]
+            return read_chunks(partial_ref, block, index)
 
         center = [param(index) for index in range(3)]
         shape, shape_back = jax.vjp(
             shape_matrix, [param(3 + index) for index in range(3)], [param(6 + index) for index in range(4)]
         )
         for place in range(views - 1):
-            pull_view(
-                chunk, place, center, shape, param, grads_ref, camera_ref, kept if place else first, keep
-            )
+            pull_view(block, place, center, shape, param, grads_ref, camera_ref, kept, keep)
         scale_grad, quaternion_grad = shape_back(
             [[kept(SHAPE_ROWS[3 * row + col]) for col in range(3)] for row in range(3)]
         )
@@ -657,13 +670,15 @@
         finals = list(scale_grad) + list(quaternion_grad) + [opacity * (1.0 - opacity) * kept(10)]
         for index, value in enumerate(finals):
             keep(3 + index, value)
-        for group in range(CHUNK // LANES):
-            columns = pl.ds(pl.multiple_of(chunk * CHUNK + group * LANES, LANES), LANES)
-            staged_ref[:, columns] = sums_ref[group * PITCH : group * PITCH + PARAMS, :]
-        send(chunk).start()
+        for part in range(WIDTH):
+            chunk = block * WIDTH + part
+            for group in range(CHUNK // LANES):
+                columns = pl.ds(pl.multiple_of(chunk * CHUNK + group * LANES, LANES), LANES)
+                staged_ref[:, columns] = partial_ref[chunk, group * PITCH : group * PITCH + PARAMS, :]
+            send(chunk).start()
         return carry
 
-    lax.fori_loop(0, CHUNKS, step, 0)
+    lax.fori_loop(0, CHUNKS // WIDTH, step, 0)
     each_chunk(lambda chunk: send(chunk).wait())
 
 
@@ -682,6 +697,7 @@
     )(*operands)
 
 
+WIDTH = 2
 HELD = jax.ShapeDtypeStruct((CHUNKS, 8 * PITCH, LANES), F32)
 
 
@@ -708,15 +724,13 @@
         out_shape=[
             jax.ShapeDtypeStruct((FEATS, GROUPS, LANES), F32),
             jax.ShapeDtypeStruct((GEO, LANES), F32),
-            HELD,
         ],
         in_specs=[pl.BlockSpec(memory_space=pl.ANY)] * 2,
-        out_specs=[pl.BlockSpec(memory_space=space) for space in (pltpu.VMEM, pltpu.VMEM, pl.ANY)],
+        out_specs=[pl.BlockSpec(memory_space=pltpu.VMEM)] * 2,
         scratch_shapes=[
             pltpu.VMEM((PARAMS, G_DEV), F32),
             pltpu.VMEM(HELD.shape, F32),
             pltpu.SMEM(camera.shape, F32),
-            pltpu.SemaphoreType.DMA((CHUNKS,)),
             pltpu.SemaphoreType.DMA((CHUNKS,)),
             pltpu.SemaphoreType.DMA,
         ],
@@ -764,23 +778,25 @@
     )(returned)
 
 
-def own_pullback(own, held):
+def own_pullback(own, gauss_params):
     return pl.pallas_call(
         own_pullback_kernel,
-        out_shape=HELD,
+        out_shape=[HELD, HELD],
         in_specs=[pl.BlockSpec(memory_space=pltpu.VMEM), pl.BlockSpec(memory_space=pl.ANY)],
-        out_specs=pl.BlockSpec(memory_space=pl.ANY),
+        out_specs=[pl.BlockSpec(memory_space=pl.ANY)] * 2,
         scratch_shapes=[
+            pltpu.VMEM((PARAMS, G_DEV), F32),
             pltpu.VMEM(HELD.shape, F32),
             pltpu.VMEM((1, FEATS * GROUPS, LANES), F32),
             pltpu.VMEM((1, 16, LANES), F32),
             pltpu.VMEM(HELD.shape, F32),
             pltpu.SemaphoreType.DMA((CHUNKS,)),
             pltpu.SemaphoreType.DMA((CHUNKS,)),
+            pltpu.SemaphoreType.DMA((CHUNKS,)),
         ],
         compiler_params=pltpu.CompilerParams(vmem_limit_bytes=WIDE_VMEM_LIMIT),
         cost_estimate=pl.CostEstimate(flops=20_000_000, bytes_accessed=4_000_000, transcendentals=0),
-    )(own.reshape((1,) + own.shape), held)
+    )(own.reshape((1,) + own.shape), gauss_params)
 
 
 def pullback(arrived, held, partial):
@@ -795,7 +811,6 @@
         scratch_shapes=[
             pltpu.VMEM(HELD.shape, F32),
             pltpu.VMEM(HELD.shape, F32),
-            pltpu.VMEM((8 * PITCH, LANES), F32),
             pltpu.VMEM((others, FEATS * GROUPS, LANES), F32),
             pltpu.VMEM((others, 16, LANES), F32),
             pltpu.VMEM((PARAMS, G_DEV), F32),
@@ -813,7 +828,7 @@
     tiles_here = tile_lists.shape[1]
     height = tiles_here * owners_total // TX
     requests, aux = route(tile_lists)
-    features, geometry, held = project(height, camera, gauss_params)
+    features, geometry = project(height, camera, gauss_params)
     requested = lax.all_to_all(requests, "img", split_axis=0, concat_axis=0, tiled=True)
     outgoing = gather(requested, features)
     arrived = lax.all_to_all(outgoing, "img", split_axis=0, concat_axis=0, tiled=True)
@@ -821,7 +836,7 @@
     returned = lax.all_to_all(slot_grads, "img", split_axis=0, concat_axis=0, tiled=True)
     own, copies = duplicate(returned, views)
     everyone = lax.all_to_all(copies, "view", split_axis=0, concat_axis=0, tiled=True)
-    partial = own_pullback(own, held)
+    partial, held = own_pullback(own, gauss_params)
     return pullback(everyone, held, partial)
 
 

time: 89.7 us -> 89.5 us (level)
  no operation moved by 1% of the time
where the time goes in v7:
time: 89.5 us; the launch traced here: 89 us
  blocking collectives  35.5 us (40%)
  starting transfers between devices  22.5 us (25%)
  Pallas kernels  18 us (20%)
  waiting for transfers between devices  12.1 us (14%)
    all_to_all x1, starting transfers between devices, per_device(): lax.all_to_all(requests, 'img', split_axis=0, concat_axis=0, tiled=True)  18.4 us
    all_to_all x1, blocking collectives, per_device(): lax.all_to_all(slot_grads, 'img', split_axis=0, concat_axis=0, tiled=True)  17.9 us
    all_to_all x1, blocking collectives, per_device(): lax.all_to_all(outgoing, 'img', split_axis=0, concat_axis=0, tiled=True)  17.7 us
    all_to_all x1, waiting for transfers between devices, per_device(): lax.all_to_all(requests, 'img', split_axis=0, concat_axis=0, tiled=True)  9.02 us
    pallas_call x1, Pallas kernels, pullback(): pl.pallas_call(pullback_kernel, out_shape=jax.ShapeDtypeStruct((PARAMS, G...  5.69 us
    pallas_call x2, Pallas kernels, call(): pl.pallas_call(kernel, out_shape=out_shape, in_specs=[pl.BlockSpec(memory...  4.39 us
    all_to_all x1, starting transfers between devices, per_device(): lax.all_to_all(copies, 'view', split_axis=0, concat_axis=0, tiled=True)  4.02 us
    pallas_call x1, Pallas kernels, own_pullback(): pl.pallas_call(own_pullback_kernel, out_shape=[HELD, HELD], in_specs=[pl....  3.34 us
  transfers between devices with their start and end apart: 2, of which 2 were waited for; matrix products, arithmetic and copies ran while one was open for 0% of the time, Pallas kernels for 6%

profile of v7, /device:TPU:1, one launch (start us, length us, event | category | flops | bytes accessed | tf_op | source)
XLA Modules:
  0.0 89.0 jit_solution(9658803548406358047)
XLA Ops:
  0.0 0.0 copy-start.1
  0.0 0.0 copy-start.3
  0.0 0.0 copy-start.4
  0.0 2.0 %shard_map.65 = (s32[128,128]{1,0:T(8,128)}, s32[48,128]{1,0:T(8,128)}) custom-call(s32[1,4,256]{2,1,0:T(4,128)} %lists_hbm.1), custom_call_target="tpu_custom_call" | custom-call | tf_op jit(solution)/shard_map/pallas_call | solution.py:705
  2.0 0.0 copy-start
  2.0 18.4 %all-to-all-start = ((s32[128,1,128]{2,1,0:T(1,128)}), s32[128,1,128]{2,1,0:T(1,128)S(1)}, u32[]{:S(2)}, u32[]{:S(2)}) async-start(s32[128,1,128]{2,1,0:T(1,128)} %bitcast.15), calls=%async_computation | async-start | bytes 131072 | tf_op jit(solution)/shard_map/all_to_all | solution.py:832
  20.5 0.0 copy-start.2
  20.5 0.6 copy-done.2
  21.1 1.8 %shard_map.64 = (f32[9,64,128]{2,1,0:T(8,128)S(1)}, f32[24,128]{1,0:T(8,128)S(1)}) custom-call(f32[1,6]{1,0:T(1,128)S(1)} %copy-done.2, f32[59,8192]{1,0:T(8,128)} %params_ref.3), custom_call_target="tpu_custom_call" | custom-call | tf_op jit(solution)/shard_map/pallas_call | solution.py:722
  22.9 9.0 %all-to-all-done = s32[128,1,128]{2,1,0:T(1,128)S(1)} async-done(((s32[128,1,128]{2,1,0:T(1,128)}), s32[128,1,128]{2,1,0:T(1,128)S(1)}, u32[]{:S(2)}, u32[]{:S(2)}) %all-to-all-start) | async-done | bytes 65568 | tf_op jit(solution)/shard_map/all_to_all | solution.py:832
  31.9 1.1 %shard_map.66 = f32[256,128]{1,0:T(8,128)S(1)} custom-call(s32[128,128]{1,0:T(8,128)S(1)} %bitcast.13, f32[9,64,128]{2,1,0:T(8,128)S(1)} %get-tuple-element.15.feats_ref), custom_call_target="tpu_custom_call" | custom-call | tf_op jit(solution)/shard_map/pallas_call | solution.py:689
  33.0 17.7 %all_to_all.38 = f32[128,2,128]{2,1,0:T(2,128)S(1)} all-to-all(f32[128,2,128]{2,1,0:T(2,128)S(1)} %bitcast.12), channel_id=1, replica_groups=mesh['img'=128,'view'=4] {'img'}, dimensions={0} | all-to-all | bytes 262144 | tf_op jit(solution)/shard_map/all_to_all | solution.py:834
  50.6 0.0 copy-done.1
  50.6 0.0 copy-done.3
  50.6 0.0 copy-done.4
  50.6 0.0 copy-done
  50.7 3.3 %shard_map.67 = f32[256,128]{1,0:T(8,128)S(1)} custom-call(s32[1,4]{1,0:T(1,128)S(1)} %copy-done.3, f32[3]{0:T(128)S(1)} %copy-done.4, f32[24,128]{1,0:T(8,128)S(1)} %get-tuple-element.13.geo_ref, f32[256,128]{1,0:T(8,128)S(1)} %bitcast.9, s32[48,128]{1,0:T(8,128)S(1)} %copy-done, f32[1,3,4,256]{3,2,1,0:T(4,128)S(1)} %copy-done.1), custom_call_target="tpu_custom_call" | custom-call | tf_op jit(solution)/shard_map/pallas_call | solution.py:689
  54.0 17.9 %all_to_all.39 = f32[128,2,128]{2,1,0:T(2,128)S(1)} all-to-all(f32[128,2,128]{2,1,0:T(2,128)S(1)} %bitcast.10), channel_id=1, replica_groups=mesh['img'=128,'view'=4] {'img'}, dimensions={0} | all-to-all | bytes 262144 | tf_op jit(solution)/shard_map/all_to_all | solution.py:836
  71.9 0.9 shard_map.68
  72.7 4.0 %all-to-all-start.3 = ((f32[4,176,128]{2,1,0:T(8,128)}), f32[4,176,128]{2,1,0:T(8,128)S(1)}, u32[]{:S(2)}, u32[]{:S(2)}) async-start(f32[4,176,128]{2,1,0:T(8,128)} %get-tuple-element.17), calls=%async_computation.3 | async-start | bytes 720896 | tf_op jit(solution)/shard_map/all_to_all | solution.py:838
  76.7 3.3 %shard_map.69 = (f32[8,520,128]{2,1,0:T(8,128)}, f32[8,520,128]{2,1,0:T(8,128)}) custom-call(f32[1,176,128]{2,1,0:T(8,128)S(1)} %bitcast.14, f32[59,8192]{1,0:T(8,128)} %params_ref.3), custom_call_target="tpu_custom_call" | custom-call | flops 20000000 | bytes 4000000 | tf_op jit(solution)/shard_map/pallas_call | solution.py:782
  80.1 3.1 %all-to-all-done.3.arrived_ref = f32[4,176,128]{2,1,0:T(8,128)S(1)} async-done(((f32[4,176,128]{2,1,0:T(8,128)}), f32[4,176,128]{2,1,0:T(8,128)S(1)}, u32[]{:S(2)}, u32[]{:S(2)}) %all-to-all-start.3) | async-done | bytes 360480 | tf_op jit(solution)/shard_map/all_to_all | solution.py:838
  83.2 5.7 %shard_map.70 = f32[59,8192]{1,0:T(8,128)} custom-call(f32[4,176,128]{2,1,0:T(8,128)S(1)} %all-to-all-done.3.arrived_ref, f32[8,520,128]{2,1,0:T(8,128)} %get-tuple-element.19.held_hbm, f32[8,520,128]{2,1,0:T(8,128)} %get-tuple-element.20.partial_hbm), custom_call_target="tpu_custom_call" | custom-call | tf_op jit(solution)/shard_map/pallas_call | solution.py:804
Async XLA Ops:
  0.0 50.6 %copy-start.1 = (f32[1,3,4,256]{3,2,1,0:T(4,128)S(1)}, f32[1,3,4,256]{3,2,1,0:T(4,128)}, u32[]{:S(2)}) copy-start(f32[1,3,4,256]{3,2,1,0:T(4,128)} %cotangent_ref.1) | copy-start | bytes 36868
  0.0 50.6 %copy-start.3 = (s32[1,4]{1,0:T(1,128)S(1)}, s32[1,4]{1,0:T(1,128)}, u32[]{:S(2)}) copy-start(s32[1,4]{1,0:T(1,128)} %lengths_ref.1) | copy-start | bytes 52
  0.0 50.6 %copy-start.4 = (f32[3]{0:T(128)S(1)}, f32[3]{0:T(128)}, u32[]{:S(2)}) copy-start(f32[3]{0:T(128)} %background_ref.1) | copy-start | bytes 40
  2.0 48.6 %copy-start = (s32[48,128]{1,0:T(8,128)S(1)}, s32[48,128]{1,0:T(8,128)}, u32[]{:S(2)}) copy-start(s32[48,128]{1,0:T(8,128)} %get-tuple-element.16.aux_ref) | copy-start | bytes 73732
  2.0 29.9 %all-to-all-start = ((s32[128,1,128]{2,1,0:T(1,128)}), s32[128,1,128]{2,1,0:T(1,128)S(1)}, u32[]{:S(2)}, u32[]{:S(2)}) async-start(s32[128,1,128]{2,1,0:T(1,128)} %bitcast.15), calls=%async_computation | async-start | bytes 131072 | tf_op jit(solution)/shard_map/all_to_all | solution.py:832
  20.5 0.7 copy-start.2
  72.7 10.5 %all-to-all-start.3 = ((f32[4,176,128]{2,1,0:T(8,128)}), f32[4,176,128]{2,1,0:T(8,128)S(1)}, u32[]{:S(2)}, u32[]{:S(2)}) async-start(f32[4,176,128]{2,1,0:T(8,128)} %get-tuple-element.17), calls=%async_computation.3 | async-start | bytes 720896 | tf_op jit(solution)/shard_map/all_to_all | solution.py:838

commit v8 on v7

--- a/solution.py
+++ b/solution.py
@@ -379,12 +379,12 @@
     store_rows(out_ref, table_ref[...])
 
 
-PIX_CHUNK = 128
+PIX_CHUNK = 256
 
 
 def render_kernel(
     height, lengths_ref, background_ref, geo_ref, arrived_ref, aux_ref, cotangent_ref, out_ref,
-    slot_ref, table_ref, grad_ref, pixel_ref, weight_ref,
+    slot_ref, table_ref, grad_ref, rows_ref, weight_ref,
 ):
     table_ref[:LANES, :] = arrived_ref[pl.ds(0, LANES, stride=2), :].T
     table_ref[LANES:, :] = arrived_ref[pl.ds(1, LANES, stride=2), :].T
@@ -398,9 +398,7 @@
             value = jnp.where(at_rank[place], pick(row, owner), value)
         slot_ref[index * 8 : index * 8 + 8, :] = value
 
-    within = iota((PIX, SLOTS), 0)
-    pixel_ref[0] = (within % SIDE).astype(F32) * (2.0 / (TX * SIDE))
-    pixel_ref[1] = (within // SIDE).astype(F32) * (2.0 / (height * SIDE))
+    along = iota((SIDE, SLOTS), 0).astype(F32)
     slot_row, slot_col = iota((SLOTS, SLOTS), 0), iota((SLOTS, SLOTS), 1)
     weight_ref[0] = (slot_row < slot_col).astype(F32).astype(BF16)
     weight_ref[1] = (slot_row > slot_col).astype(F32).astype(BF16)
@@ -425,6 +423,22 @@
         )
         columns = jnp.concatenate(shades + [behind, jnp.zeros((4, PIX), F32)], axis=0).T
 
+        shade_high, shade_low = (part.astype(F32) for part in halves(jnp.concatenate(shades, axis=0)))
+        color_high, color_low = (part.astype(F32) for part in halves(jnp.concatenate(colors, axis=0)))
+        filler = jnp.zeros((7, PIX), F32)
+        gains = lax.dot_general(
+            jnp.concatenate([shade_high, shade_high, shade_low, filler], axis=0).astype(BF16),
+            jnp.concatenate([color_high, color_low, color_high, filler], axis=0).astype(BF16),
+            (((0,), (0,)), ((), ())),
+            preferred_element_type=F32,
+        )
+        delta_x = along * (2.0 / (TX * SIDE)) - at_x
+        slope_a = scaled_a * delta_x
+        delta_y = along * (2.0 / (height * SIDE)) - at_y
+        rows_ref[index, 0] = delta_y
+        rows_ref[index, 1] = scaled_b * delta_y
+        rows_ref[index, 2] = scaled_c * delta_y * delta_y
+
         def fold(values):
             return jnp.sum(values.reshape(PIX_CHUNK // 8, 8, SLOTS), axis=0)
 
@@ -432,27 +446,40 @@
         for chunk in range(PIX // PIX_CHUNK):
             rows = slice(chunk * PIX_CHUNK, (chunk + 1) * PIX_CHUNK)
             shape = (PIX_CHUNK, SLOTS)
-            delta_x = pixel_ref[0, rows, :] - at_x
-            delta_y = pixel_ref[1, rows, :] - at_y
-            exponent = (scaled_a * delta_x + scaled_b * delta_y) * delta_x + scaled_c * delta_y * delta_y
+            lines = range(chunk * PIX_CHUNK // SIDE, (chunk + 1) * PIX_CHUNK // SIDE)
+            exponent = jnp.concatenate(
+                [
+                    (slope_a + rows_ref[index, 1, line : line + 1, :]) * delta_x
+                    + rows_ref[index, 2, line : line + 1, :]
+                    for line in lines
+                ],
+                axis=0,
+            )
             coverage = live_opacity * jnp.exp2(exponent)
             log_pass = jnp.log2(1.0 - coverage)
             high, low = halves(log_pass)
             prefix = dot(high, weight_ref[0]) + dot(low, weight_ref[0])
             weight = coverage * jnp.exp2(prefix)
             shade = [spread(columns[rows, channel : channel + 1], shape) for channel in range(3)]
-            gain = shade[0] * colors[0] + shade[1] * colors[1] + shade[2] * colors[2]
-            product = weight * gain
+            product = weight * gains[rows]
             high, low = halves(product)
             later = dot(high, weight_ref[1]) + dot(low, weight_ref[1])
             remain = jnp.exp2(prefix[:, SLOTS - 1 :] + log_pass[:, SLOTS - 1 :])
             later = later + spread(columns[rows, 3:4] * remain, shape)
             slope = product - coverage * jnp.exp2(-log_pass) * later
-            slope_x = slope * delta_x
-            slope_y = slope * delta_y
-            parts = [slope, slope_x, slope_y, slope_x * delta_x, slope_x * delta_y, slope_y * delta_y]
-            parts += [part * weight for part in shade]
-            sums = [total + fold(part) for total, part in zip(sums, parts)]
+            total, sum_x, sum_y, sum_xx, sum_xy, sum_yy = sums[:6]
+            for place, line in enumerate(lines):
+                down = rows_ref[index, 0, line : line + 1, :]
+                part = slope[place * SIDE : (place + 1) * SIDE]
+                part_x = part * delta_x
+                part_xx = part_x * delta_x
+                part, part_x, part_xx = (value[:8] + value[8:] for value in (part, part_x, part_xx))
+                part_y = part * down
+                total, sum_x, sum_xx = total + part, sum_x + part_x, sum_xx + part_xx
+                sum_y, sum_yy, sum_xy = sum_y + part_y, sum_yy + part_y * down, sum_xy + part_x * down
+            sums = [total, sum_x, sum_y, sum_xx, sum_xy, sum_yy] + [
+                past + fold(value * weight) for past, value in zip(sums[6:], shade)
+            ]
 
         sums = [jnp.sum(part, axis=0, keepdims=True) for part in sums]
         total, sum_x, sum_y, sum_xx, sum_xy, sum_yy = (part * -0.5 for part in sums[:6])
@@ -758,7 +785,7 @@
             pltpu.VMEM((FEATS * 8, LANES), F32),
             pltpu.VMEM((2 * OWNERS, LANES), F32),
             pltpu.VMEM((FEATS * 8, LANES), F32),
-            pltpu.VMEM((2, PIX, SLOTS), F32),
+            pltpu.VMEM((TILES_DEV, 3, SIDE, SLOTS), F32),
             pltpu.VMEM((2, SLOTS, SLOTS), BF16),
         ],
     )

time: 89.5 us -> 88.9 us (level)
  no operation moved by 1% of the time
where the time goes in v8:
time: 88.9 us; the launch traced here: 88.5 us
  blocking collectives  35.5 us (40%)
  starting transfers between devices  22.5 us (25%)
  Pallas kernels  17.5 us (20%)
  waiting for transfers between devices  12.1 us (14%)
    all_to_all x1, starting transfers between devices, per_device(): lax.all_to_all(requests, 'img', split_axis=0, concat_axis=0, tiled=True)  18.4 us
    all_to_all x1, blocking collectives, per_device(): lax.all_to_all(slot_grads, 'img', split_axis=0, concat_axis=0, tiled=True)  17.9 us
    all_to_all x1, blocking collectives, per_device(): lax.all_to_all(outgoing, 'img', split_axis=0, concat_axis=0, tiled=True)  17.7 us
    all_to_all x1, waiting for transfers between devices, per_device(): lax.all_to_all(requests, 'img', split_axis=0, concat_axis=0, tiled=True)  9.02 us
    pallas_call x1, Pallas kernels, pullback(): pl.pallas_call(pullback_kernel, out_shape=jax.ShapeDtypeStruct((PARAMS, G...  5.69 us
    all_to_all x1, starting transfers between devices, per_device(): lax.all_to_all(copies, 'view', split_axis=0, concat_axis=0, tiled=True)  4.02 us
    pallas_call x2, Pallas kernels, call(): pl.pallas_call(kernel, out_shape=out_shape, in_specs=[pl.BlockSpec(memory...  3.87 us
    pallas_call x1, Pallas kernels, own_pullback(): pl.pallas_call(own_pullback_kernel, out_shape=[HELD, HELD], in_specs=[pl....  3.34 us
  transfers between devices with their start and end apart: 2, of which 2 were waited for; matrix products, arithmetic and copies ran while one was open for 0% of the time, Pallas kernels for 6%

profile of v8, /device:TPU:1, one launch (start us, length us, event | category | flops | bytes accessed | tf_op | source)
XLA Modules:
  0.0 88.5 jit_solution(1736048888757535394)
XLA Ops:
  0.0 0.0 copy-start.1
  0.0 0.0 copy-start.3
  0.0 0.0 copy-start.4
  0.0 2.0 %shard_map.65 = (s32[128,128]{1,0:T(8,128)}, s32[48,128]{1,0:T(8,128)}) custom-call(s32[1,4,256]{2,1,0:T(4,128)} %lists_hbm.1), custom_call_target="tpu_custom_call" | custom-call | tf_op jit(solution)/shard_map/pallas_call | solution.py:732
  2.0 0.0 copy-start
  2.0 18.4 %all-to-all-start = ((s32[128,1,128]{2,1,0:T(1,128)}), s32[128,1,128]{2,1,0:T(1,128)S(1)}, u32[]{:S(2)}, u32[]{:S(2)}) async-start(s32[128,1,128]{2,1,0:T(1,128)} %bitcast.15), calls=%async_computation | async-start | bytes 131072 | tf_op jit(solution)/shard_map/all_to_all | solution.py:859
  20.5 0.0 copy-start.2
  20.5 0.6 copy-done.2
  21.1 1.8 %shard_map.64 = (f32[9,64,128]{2,1,0:T(8,128)S(1)}, f32[24,128]{1,0:T(8,128)S(1)}) custom-call(f32[1,6]{1,0:T(1,128)S(1)} %copy-done.2, f32[59,8192]{1,0:T(8,128)} %params_ref.3), custom_call_target="tpu_custom_call" | custom-call | tf_op jit(solution)/shard_map/pallas_call | solution.py:749
  22.9 9.0 %all-to-all-done = s32[128,1,128]{2,1,0:T(1,128)S(1)} async-done(((s32[128,1,128]{2,1,0:T(1,128)}), s32[128,1,128]{2,1,0:T(1,128)S(1)}, u32[]{:S(2)}, u32[]{:S(2)}) %all-to-all-start) | async-done | bytes 65568 | tf_op jit(solution)/shard_map/all_to_all | solution.py:859
  31.9 1.1 %shard_map.66 = f32[256,128]{1,0:T(8,128)S(1)} custom-call(s32[128,128]{1,0:T(8,128)S(1)} %bitcast.13, f32[9,64,128]{2,1,0:T(8,128)S(1)} %get-tuple-element.15.feats_ref), custom_call_target="tpu_custom_call" | custom-call | tf_op jit(solution)/shard_map/pallas_call | solution.py:716
  33.0 17.7 %all_to_all.38 = f32[128,2,128]{2,1,0:T(2,128)S(1)} all-to-all(f32[128,2,128]{2,1,0:T(2,128)S(1)} %bitcast.12), channel_id=1, replica_groups=mesh['img'=128,'view'=4] {'img'}, dimensions={0} | all-to-all | bytes 262144 | tf_op jit(solution)/shard_map/all_to_all | solution.py:861
  50.6 0.0 copy-done.1
  50.6 0.0 copy-done.3
  50.6 0.0 copy-done.4
  50.6 0.0 copy-done
  50.7 2.8 %shard_map.67 = f32[256,128]{1,0:T(8,128)S(1)} custom-call(s32[1,4]{1,0:T(1,128)S(1)} %copy-done.3, f32[3]{0:T(128)S(1)} %copy-done.4, f32[24,128]{1,0:T(8,128)S(1)} %get-tuple-element.13.geo_ref, f32[256,128]{1,0:T(8,128)S(1)} %bitcast.9, s32[48,128]{1,0:T(8,128)S(1)} %copy-done, f32[1,3,4,256]{3,2,1,0:T(4,128)S(1)} %copy-done.1), custom_call_target="tpu_custom_call" | custom-call | tf_op jit(solution)/shard_map/pallas_call | solution.py:716
  53.5 17.9 %all_to_all.39 = f32[128,2,128]{2,1,0:T(2,128)S(1)} all-to-all(f32[128,2,128]{2,1,0:T(2,128)S(1)} %bitcast.10), channel_id=1, replica_groups=mesh['img'=128,'view'=4] {'img'}, dimensions={0} | all-to-all | bytes 262144 | tf_op jit(solution)/shard_map/all_to_all | solution.py:863
  71.3 0.9 shard_map.68
  72.2 4.0 %all-to-all-start.3 = ((f32[4,176,128]{2,1,0:T(8,128)}), f32[4,176,128]{2,1,0:T(8,128)S(1)}, u32[]{:S(2)}, u32[]{:S(2)}) async-start(f32[4,176,128]{2,1,0:T(8,128)} %get-tuple-element.17), calls=%async_computation.3 | async-start | bytes 720896 | tf_op jit(solution)/shard_map/all_to_all | solution.py:865
  76.2 3.3 %shard_map.69 = (f32[8,520,128]{2,1,0:T(8,128)}, f32[8,520,128]{2,1,0:T(8,128)}) custom-call(f32[1,176,128]{2,1,0:T(8,128)S(1)} %bitcast.14, f32[59,8192]{1,0:T(8,128)} %params_ref.3), custom_call_target="tpu_custom_call" | custom-call | flops 20000000 | bytes 4000000 | tf_op jit(solution)/shard_map/pallas_call | solution.py:809
  79.6 3.1 %all-to-all-done.3.arrived_ref = f32[4,176,128]{2,1,0:T(8,128)S(1)} async-done(((f32[4,176,128]{2,1,0:T(8,128)}), f32[4,176,128]{2,1,0:T(8,128)S(1)}, u32[]{:S(2)}, u32[]{:S(2)}) %all-to-all-start.3) | async-done | bytes 360480 | tf_op jit(solution)/shard_map/all_to_all | solution.py:865
  82.7 5.7 %shard_map.70 = f32[59,8192]{1,0:T(8,128)} custom-call(f32[4,176,128]{2,1,0:T(8,128)S(1)} %all-to-all-done.3.arrived_ref, f32[8,520,128]{2,1,0:T(8,128)} %get-tuple-element.19.held_hbm, f32[8,520,128]{2,1,0:T(8,128)} %get-tuple-element.20.partial_hbm), custom_call_target="tpu_custom_call" | custom-call | tf_op jit(solution)/shard_map/pallas_call | solution.py:831
Async XLA Ops:
  0.0 50.6 %copy-start.1 = (f32[1,3,4,256]{3,2,1,0:T(4,128)S(1)}, f32[1,3,4,256]{3,2,1,0:T(4,128)}, u32[]{:S(2)}) copy-start(f32[1,3,4,256]{3,2,1,0:T(4,128)} %cotangent_ref.1) | copy-start | bytes 36868
  0.0 50.6 %copy-start.3 = (s32[1,4]{1,0:T(1,128)S(1)}, s32[1,4]{1,0:T(1,128)}, u32[]{:S(2)}) copy-start(s32[1,4]{1,0:T(1,128)} %lengths_ref.1) | copy-start | bytes 52
  0.0 50.6 %copy-start.4 = (f32[3]{0:T(128)S(1)}, f32[3]{0:T(128)}, u32[]{:S(2)}) copy-start(f32[3]{0:T(128)} %background_ref.1) | copy-start | bytes 40
  2.0 48.6 %copy-start = (s32[48,128]{1,0:T(8,128)S(1)}, s32[48,128]{1,0:T(8,128)}, u32[]{:S(2)}) copy-start(s32[48,128]{1,0:T(8,128)} %get-tuple-element.16.aux_ref) | copy-start | bytes 73732
  2.0 29.9 %all-to-all-start = ((s32[128,1,128]{2,1,0:T(1,128)}), s32[128,1,128]{2,1,0:T(1,128)S(1)}, u32[]{:S(2)}, u32[]{:S(2)}) async-start(s32[128,1,128]{2,1,0:T(1,128)} %bitcast.15), calls=%async_computation | async-start | bytes 131072 | tf_op jit(solution)/shard_map/all_to_all | solution.py:859
  20.5 0.7 copy-start.2
  72.2 10.5 %all-to-all-start.3 = ((f32[4,176,128]{2,1,0:T(8,128)}), f32[4,176,128]{2,1,0:T(8,128)S(1)}, u32[]{:S(2)}, u32[]{:S(2)}) async-start(f32[4,176,128]{2,1,0:T(8,128)} %get-tuple-element.17), calls=%async_computation.3 | async-start | bytes 720896 | tf_op jit(solution)/shard_map/all_to_all | solution.py:865

commit v9 on v8

--- a/solution.py
+++ b/solution.py
@@ -514,14 +514,13 @@
 
 
 def duplicate_kernel(returned_ref, own_ref, copies_ref, semaphores):
-    own_ref[:LANES, :] = returned_ref[pl.ds(0, LANES, stride=2), :].T
-    own_ref[LANES:, :] = returned_ref[pl.ds(1, LANES, stride=2), :].T[: SENT - LANES]
-    copies = [
-        pltpu.make_async_copy(own_ref, copies_ref.at[view], semaphores.at[view])
-        for view in range(copies_ref.shape[0])
-    ]
-    for copy in copies:
-        copy.start()
+    copies = []
+    for part, rows in enumerate((slice(0, LANES), slice(LANES, SENT))):
+        own_ref[rows, :] = returned_ref[pl.ds(part, LANES, stride=2), :].T[: rows.stop - rows.start]
+        for view in range(copies_ref.shape[0]):
+            copy = pltpu.make_async_copy(own_ref.at[rows], copies_ref.at[view, rows], semaphores.at[view, part])
+            copy.start()
+            copies.append(copy)
     for copy in copies:
         copy.wait()
 
@@ -800,7 +799,7 @@
         ],
         in_specs=[pl.BlockSpec(memory_space=pltpu.VMEM)],
         out_specs=[pl.BlockSpec(memory_space=pltpu.VMEM), pl.BlockSpec(memory_space=pl.ANY)],
-        scratch_shapes=[pltpu.SemaphoreType.DMA((views,))],
+        scratch_shapes=[pltpu.SemaphoreType.DMA((views, 2))],
         compiler_params=pltpu.CompilerParams(vmem_limit_bytes=VMEM_LIMIT),
     )(returned)
 

time: 88.9 us -> 89 us (level)
  no operation moved by 1% of the time
where the time goes in v9:
time: 89 us; the launch traced here: 88.5 us
  blocking collectives  35.5 us (40%)
  starting transfers between devices  22.5 us (25%)
  Pallas kernels  17.5 us (20%)
  waiting for transfers between devices  12.1 us (14%)
    all_to_all x1, starting transfers between devices, per_device(): lax.all_to_all(requests, 'img', split_axis=0, concat_axis=0, tiled=True)  18.4 us
    all_to_all x1, blocking collectives, per_device(): lax.all_to_all(slot_grads, 'img', split_axis=0, concat_axis=0, tiled=True)  17.9 us
    all_to_all x1, blocking collectives, per_device(): lax.all_to_all(outgoing, 'img', split_axis=0, concat_axis=0, tiled=True)  17.7 us
    all_to_all x1, waiting for transfers between devices, per_device(): lax.all_to_all(requests, 'img', split_axis=0, concat_axis=0, tiled=True)  9.02 us
    pallas_call x1, Pallas kernels, pullback(): pl.pallas_call(pullback_kernel, out_shape=jax.ShapeDtypeStruct((PARAMS, G...  5.69 us
    all_to_all x1, starting transfers between devices, per_device(): lax.all_to_all(copies, 'view', split_axis=0, concat_axis=0, tiled=True)  4.02 us
    pallas_call x2, Pallas kernels, call(): pl.pallas_call(kernel, out_shape=out_shape, in_specs=[pl.BlockSpec(memory...  3.87 us
    pallas_call x1, Pallas kernels, own_pullback(): pl.pallas_call(own_pullback_kernel, out_shape=[HELD, HELD], in_specs=[pl....  3.34 us
  transfers between devices with their start and end apart: 2, of which 2 were waited for; matrix products, arithmetic and copies ran while one was open for 0% of the time, Pallas kernels for 6%

profile of v9, /device:TPU:1, one launch (start us, length us, event | category | flops | bytes accessed | tf_op | source)
XLA Modules:
  0.0 88.5 jit_solution(10402977187661923289)
XLA Ops:
  0.0 0.0 copy-start.1
  0.0 0.0 copy-start.3
  0.0 0.0 copy-start.4
  0.0 2.0 %shard_map.65 = (s32[128,128]{1,0:T(8,128)}, s32[48,128]{1,0:T(8,128)}) custom-call(s32[1,4,256]{2,1,0:T(4,128)} %lists_hbm.1), custom_call_target="tpu_custom_call" | custom-call | tf_op jit(solution)/shard_map/pallas_call | solution.py:731
  2.0 0.0 copy-start
  2.0 18.4 %all-to-all-start = ((s32[128,1,128]{2,1,0:T(1,128)}), s32[128,1,128]{2,1,0:T(1,128)S(1)}, u32[]{:S(2)}, u32[]{:S(2)}) async-start(s32[128,1,128]{2,1,0:T(1,128)} %bitcast.15), calls=%async_computation | async-start | bytes 131072 | tf_op jit(solution)/shard_map/all_to_all | solution.py:858
  20.5 0.0 copy-start.2
  20.5 0.6 copy-done.2
  21.1 1.8 %shard_map.64 = (f32[9,64,128]{2,1,0:T(8,128)S(1)}, f32[24,128]{1,0:T(8,128)S(1)}) custom-call(f32[1,6]{1,0:T(1,128)S(1)} %copy-done.2, f32[59,8192]{1,0:T(8,128)} %params_ref.3), custom_call_target="tpu_custom_call" | custom-call | tf_op jit(solution)/shard_map/pallas_call | solution.py:748
  22.9 9.0 %all-to-all-done = s32[128,1,128]{2,1,0:T(1,128)S(1)} async-done(((s32[128,1,128]{2,1,0:T(1,128)}), s32[128,1,128]{2,1,0:T(1,128)S(1)}, u32[]{:S(2)}, u32[]{:S(2)}) %all-to-all-start) | async-done | bytes 65568 | tf_op jit(solution)/shard_map/all_to_all | solution.py:858
  31.9 1.1 %shard_map.66 = f32[256,128]{1,0:T(8,128)S(1)} custom-call(s32[128,128]{1,0:T(8,128)S(1)} %bitcast.13, f32[9,64,128]{2,1,0:T(8,128)S(1)} %get-tuple-element.15.feats_ref), custom_call_target="tpu_custom_call" | custom-call | tf_op jit(solution)/shard_map/pallas_call | solution.py:715
  33.0 17.7 %all_to_all.38 = f32[128,2,128]{2,1,0:T(2,128)S(1)} all-to-all(f32[128,2,128]{2,1,0:T(2,128)S(1)} %bitcast.12), channel_id=1, replica_groups=mesh['img'=128,'view'=4] {'img'}, dimensions={0} | all-to-all | bytes 262144 | tf_op jit(solution)/shard_map/all_to_all | solution.py:860
  50.6 0.0 copy-done.1
  50.6 0.0 copy-done.3
  50.6 0.0 copy-done.4
  50.6 0.0 copy-done
  50.7 2.8 %shard_map.67 = f32[256,128]{1,0:T(8,128)S(1)} custom-call(s32[1,4]{1,0:T(1,128)S(1)} %copy-done.3, f32[3]{0:T(128)S(1)} %copy-done.4, f32[24,128]{1,0:T(8,128)S(1)} %get-tuple-element.13.geo_ref, f32[256,128]{1,0:T(8,128)S(1)} %bitcast.9, s32[48,128]{1,0:T(8,128)S(1)} %copy-done, f32[1,3,4,256]{3,2,1,0:T(4,128)S(1)} %copy-done.1), custom_call_target="tpu_custom_call" | custom-call | tf_op jit(solution)/shard_map/pallas_call | solution.py:715
  53.5 17.9 %all_to_all.39 = f32[128,2,128]{2,1,0:T(2,128)S(1)} all-to-all(f32[128,2,128]{2,1,0:T(2,128)S(1)} %bitcast.10), channel_id=1, replica_groups=mesh['img'=128,'view'=4] {'img'}, dimensions={0} | all-to-all | bytes 262144 | tf_op jit(solution)/shard_map/all_to_all | solution.py:862
  71.3 0.9 %shard_map.68 = (f32[176,128]{1,0:T(8,128)S(1)}, f32[4,176,128]{2,1,0:T(8,128)}) custom-call(f32[256,128]{1,0:T(8,128)S(1)} %bitcast.11), custom_call_target="tpu_custom_call" | custom-call | tf_op jit(solution)/shard_map/pallas_call | solution.py:794
  72.2 4.0 %all-to-all-start.3 = ((f32[4,176,128]{2,1,0:T(8,128)}), f32[4,176,128]{2,1,0:T(8,128)S(1)}, u32[]{:S(2)}, u32[]{:S(2)}) async-start(f32[4,176,128]{2,1,0:T(8,128)} %get-tuple-element.17), calls=%async_computation.3 | async-start | bytes 720896 | tf_op jit(solution)/shard_map/all_to_all | solution.py:864
  76.3 3.3 %shard_map.69 = (f32[8,520,128]{2,1,0:T(8,128)}, f32[8,520,128]{2,1,0:T(8,128)}) custom-call(f32[1,176,128]{2,1,0:T(8,128)S(1)} %bitcast.14, f32[59,8192]{1,0:T(8,128)} %params_ref.3), custom_call_target="tpu_custom_call" | custom-call | flops 20000000 | bytes 4000000 | tf_op jit(solution)/shard_map/pallas_call | solution.py:808
  79.6 3.1 %all-to-all-done.3.arrived_ref = f32[4,176,128]{2,1,0:T(8,128)S(1)} async-done(((f32[4,176,128]{2,1,0:T(8,128)}), f32[4,176,128]{2,1,0:T(8,128)S(1)}, u32[]{:S(2)}, u32[]{:S(2)}) %all-to-all-start.3) | async-done | bytes 360480 | tf_op jit(solution)/shard_map/all_to_all | solution.py:864
  82.7 5.7 %shard_map.70 = f32[59,8192]{1,0:T(8,128)} custom-call(f32[4,176,128]{2,1,0:T(8,128)S(1)} %all-to-all-done.3.arrived_ref, f32[8,520,128]{2,1,0:T(8,128)} %get-tuple-element.19.held_hbm, f32[8,520,128]{2,1,0:T(8,128)} %get-tuple-element.20.partial_hbm), custom_call_target="tpu_custom_call" | custom-call | tf_op jit(solution)/shard_map/pallas_call | solution.py:830
Async XLA Ops:
  0.0 50.6 %copy-start.1 = (f32[1,3,4,256]{3,2,1,0:T(4,128)S(1)}, f32[1,3,4,256]{3,2,1,0:T(4,128)}, u32[]{:S(2)}) copy-start(f32[1,3,4,256]{3,2,1,0:T(4,128)} %cotangent_ref.1) | copy-start | bytes 36868
  0.0 50.6 %copy-start.3 = (s32[1,4]{1,0:T(1,128)S(1)}, s32[1,4]{1,0:T(1,128)}, u32[]{:S(2)}) copy-start(s32[1,4]{1,0:T(1,128)} %lengths_ref.1) | copy-start | bytes 52
  0.0 50.6 %copy-start.4 = (f32[3]{0:T(128)S(1)}, f32[3]{0:T(128)}, u32[]{:S(2)}) copy-start(f32[3]{0:T(128)} %background_ref.1) | copy-start | bytes 40
  2.0 48.6 %copy-start = (s32[48,128]{1,0:T(8,128)S(1)}, s32[48,128]{1,0:T(8,128)}, u32[]{:S(2)}) copy-start(s32[48,128]{1,0:T(8,128)} %get-tuple-element.16.aux_ref) | copy-start | bytes 73732
  2.0 29.9 %all-to-all-start = ((s32[128,1,128]{2,1,0:T(1,128)}), s32[128,1,128]{2,1,0:T(1,128)S(1)}, u32[]{:S(2)}, u32[]{:S(2)}) async-start(s32[128,1,128]{2,1,0:T(1,128)} %bitcast.15), calls=%async_computation | async-start | bytes 131072 | tf_op jit(solution)/shard_map/all_to_all | solution.py:858
  20.5 0.7 copy-start.2
  72.2 10.5 %all-to-all-start.3 = ((f32[4,176,128]{2,1,0:T(8,128)}), f32[4,176,128]{2,1,0:T(8,128)S(1)}, u32[]{:S(2)}, u32[]{:S(2)}) async-start(f32[4,176,128]{2,1,0:T(8,128)} %get-tuple-element.17), calls=%async_computation.3 | async-start | bytes 720896 | tf_op jit(solution)/shard_map/all_to_all | solution.py:864
